TPU v7x, 512 devices: a whole 4x8x8 slice. The times are simulated.
512 devices in a mesh: docs: 32 (over y, x), heads: 16 (over z, core).
Axes of the slice: x: 4, y: 8, z: 8, core: 2. Of those that a mesh axis runs over, the one named last changes fastest.
Arguments:
- queries: bfloat16 [65536, 2048], P(('docs', 'heads')), may hold values from -5 to 5
- keys: bfloat16 [65536, 512], P(('docs', 'heads')), may hold values from -5 to 5
- values: bfloat16 [65536, 512], P(('docs', 'heads')), may hold values from -6 to 6
- lengths: int32 [32], replicated, may hold values from 1 to 3072, as said below
Outputs:
- attended: bfloat16 [65536, 2048], P(('docs', 'heads'))
Inputs may be any that keep to these rules, and one draw needn't show every extreme that they name: The lengths sum to 65536; the largest is exactly 3072.
All inputs are finite; a program needn't handle non-finite values.
Results may differ from a plain program's by a relative error of at most 0.009.
Values may be sent and summed in bfloat16 or wider, within the bound.
No kernel may reach another device: no remote copies, remote signals or barrier semaphores. Data moves between devices by JAX's collectives and lax.ppermute only.
A program may use at most 64 MiB of HBM per device.

v0:
```python
import math

import jax
import jax.numpy as jnp
from jax import lax
from jax.sharding import PartitionSpec as P

QUERY_HEADS = 16
KEY_VALUE_HEADS = 4
HEAD_SIZE = 128


def from_behind(x, axis, by):
    size = lax.axis_size(axis)
    pairs = [(i, i + by) for i in range(size) if 0 <= i + by < size]
    return lax.ppermute(x, axis, pairs)


def documents_of(places, bounds):
    labels = jnp.sum((bounds[None, :] <= places[:, None]).astype(jnp.int32), axis=1)
    return jnp.where(places >= 0, labels, -1)


def earlier(key_rows, value_rows):
    block_length = key_rows.shape[0]
    near_keys, near_values = from_behind((key_rows, value_rows), "docs", 1)
    far_keys, far_values = from_behind((key_rows, value_rows), "docs", 2)
    key_all = jnp.concatenate([far_keys, near_keys, key_rows], axis=0)
    value_all = jnp.concatenate([far_values, near_values, value_rows], axis=0)
    return (key_all, value_all, block_length + block_length)


def attend(query_rows, key_rows, value_rows, query_places, key_places, bounds):
    row_count, groups, per_group = (query_rows.shape[0], query_rows.shape[1], query_rows.shape[2])
    query_docs = documents_of(query_places, bounds)
    key_docs = documents_of(key_places, bounds)
    query_stride = math.gcd(row_count, 512)
    key_step = math.gcd(key_rows.shape[0], 512)
    tile_count = key_rows.shape[0] // key_step
    key_tiles = key_rows.reshape(tile_count, key_step, groups, HEAD_SIZE)
    value_tiles = value_rows.reshape(tile_count, key_step, groups, HEAD_SIZE)
    place_tiles = key_places.reshape(tile_count, key_step)
    doc_tiles = key_docs.reshape(tile_count, key_step)
    pieces = []
    for offset in range(0, row_count, query_stride):
        query_tile_rows = query_rows[offset : offset + query_stride]
        query_place = query_places[offset : offset + query_stride]
        query_doc = query_docs[offset : offset + query_stride]

        def update(carry, key_tile_rows, value_tile_rows, key_place, key_doc):
            running_max, running_sum, weighted = carry
            scores = jnp.einsum(
                "qgsd,kgd->gsqk", query_tile_rows, key_tile_rows, preferred_element_type=jnp.float32
            ) * HEAD_SIZE ** (-0.5)
            visible = (key_doc[None, :] == query_doc[:, None]) & (
                key_place[None, :] <= query_place[:, None]
            )
            scores = jnp.where(visible, scores, -1e30)
            new_max = jnp.maximum(running_max, jnp.max(scores, axis=-1))
            weights = jnp.where(visible, jnp.exp(scores - new_max[..., None]), 0.0)
            factor = jnp.exp(running_max - new_max)
            running_sum = running_sum * factor + jnp.sum(weights, axis=-1)
            weighted = weighted * factor[..., None] + jnp.einsum(
                "gsqk,kgd->gsqd",
                weights.astype(jnp.bfloat16),
                value_tile_rows,
                preferred_element_type=jnp.float32,
            )
            return (new_max, running_sum, weighted)

        def visit_block(carry, tiles):
            key_tile_rows, value_tile_rows, key_place, key_doc = tiles
            carry = update(carry, key_tile_rows, value_tile_rows, key_place, key_doc)
            return (carry, None)

        initial = (
            jnp.full((groups, per_group, query_stride), -1e30, jnp.float32),
            jnp.zeros((groups, per_group, query_stride), jnp.float32),
            jnp.zeros((groups, per_group, query_stride, HEAD_SIZE), jnp.float32),
        )
        (running_max, running_sum, weighted), unused = lax.scan(
            visit_block, initial, (key_tiles, value_tiles, place_tiles, doc_tiles)
        )
        final_output = weighted / running_sum[..., None]
        pieces.append(final_output.transpose(2, 0, 1, 3).astype(jnp.bfloat16))
    return jnp.concatenate(pieces, axis=0)


def per_device(queries, keys, values, lengths):
    local_len = queries.shape[0]
    head_ways = lax.axis_size("heads")
    head_index = lax.axis_index("heads")
    doc_index = lax.axis_index("docs")
    block_length = local_len * head_ways
    block_start = doc_index * block_length
    group_width = QUERY_HEADS // KEY_VALUE_HEADS
    bounds = jnp.cumsum(lengths)
    local_heads = QUERY_HEADS // head_ways
    key_value_count = max(1, local_heads // group_width)
    per_kv = local_heads // key_value_count
    key_value_first = head_index * local_heads // group_width
    key_block_rows, value_block_rows = (
        lax.all_gather(keys, "heads", axis=0, tiled=True),
        lax.all_gather(values, "heads", axis=0, tiled=True),
    )
    own_keys = lax.dynamic_slice_in_dim(
        key_block_rows.reshape(block_length, KEY_VALUE_HEADS, HEAD_SIZE),
        key_value_first,
        key_value_count,
        1,
    )
    value_own = lax.dynamic_slice_in_dim(
        value_block_rows.reshape(block_length, KEY_VALUE_HEADS, HEAD_SIZE),
        key_value_first,
        key_value_count,
        1,
    )
    query_block = lax.all_to_all(queries, "heads", split_axis=1, concat_axis=0, tiled=True)
    key_all, value_all, reach = earlier(own_keys, value_own)
    query_places = block_start + jnp.arange(block_length, dtype=jnp.int32)
    key_places = block_start - reach + jnp.arange(reach + block_length, dtype=jnp.int32)
    outcome = attend(
        query_block.reshape(block_length, key_value_count, per_kv, HEAD_SIZE),
        key_all,
        value_all,
        query_places,
        key_places,
        bounds,
    )
    return lax.all_to_all(
        outcome.reshape(block_length, local_heads * HEAD_SIZE),
        "heads",
        split_axis=0,
        concat_axis=1,
        tiled=True,
    )


def solution(mesh):
    in_specs = (
        P(("docs", "heads"), None),
        P(("docs", "heads"), None),
        P(("docs", "heads"), None),
        P(),
    )
    out_specs = P(("docs", "heads"), None)
    return jax.shard_map(
        per_device, mesh=mesh, in_specs=in_specs, out_specs=out_specs, check_vma=False
    )
```

profile of v0, /device:TPU:32, one launch (start us, length us, event | category | flops | bytes accessed | tf_op | source)
XLA Modules:
  0.0 334.1 jit_solution(3083976959477679330)
XLA Ops:
  6.5 1.7 copy.82
  8.3 1.7 copy.78
  10.0 2.0 copy.80
  12.0 10.4 %all-to-all-start = ((bf16[128,16,128]{0,2,1:T(8,128)(2,1)}), bf16[128,16,128]{0,2,1:T(8,128)(2,1)S(1)}, u32[]{:S(2)}, u32[]{:S(2)}) async-start(bf16[128,16,128]{0,2,1:T(8,128)(2,1)} %bitcast.4), calls=%async_computation | async-start | bytes 1048576 | tf_op jit(solution)/shard_map/all_to_all | solution.py:118
  23.1 39.4 %all-gather.5.cloned.1.call-done = bf16[2048,512]{0,1:T(8,128)(2,1)} async-done(((bf16[128,512]{0,1:T(8,128)(2,1)}), bf16[2048,512]{0,1:T(8,128)(2,1)}) %all-gather.5.cloned.1.call-update) | async-done | bytes 2097168 | tf_op jit(solution)/shard_map/all_gather | solution.py:104
  63.6 4.9 %collective-permute-start.2 = (bf16[2048,1,128]{0,2,1:T(8,128)(2,1)S(1)}, bf16[2048,1,128]{0,2,1:T(8,128)(2,1)S(1)}, u32[]{:S(2)}, u32[]{:S(2)}) collective-permute-start(bf16[2048,1,128]{0,2,1:T(8,128)(2,1)S(1)} %constant_dynamic-slice_fusion.8), channel_id=1, source_target_pairs={{0,32},{16,48},{32,64},{48,80},{64,96},{80,112},{96,128},{112,144}... | collective-permute-start | bytes 1572872 | tf_op jit(solution)/shard_map/ppermute | solution.py:16
  68.5 2.5 collective-permute-start.3
  74.3 32.4 %all-gather.3.cloned.1.call-done = bf16[2048,512]{0,1:T(8,128)(2,1)} async-done(((bf16[128,512]{0,1:T(8,128)(2,1)}), bf16[2048,512]{0,1:T(8,128)(2,1)}) %all-gather.3.cloned.1.call-update) | async-done | bytes 2097168 | tf_op jit(solution)/shard_map/all_gather | solution.py:103
  107.8 4.9 %collective-permute-start = (bf16[2048,1,128]{0,2,1:T(8,128)(2,1)S(1)}, bf16[2048,1,128]{0,2,1:T(8,128)(2,1)}, u32[]{:S(2)}, u32[]{:S(2)}) collective-permute-start(bf16[2048,1,128]{0,2,1:T(8,128)(2,1)S(1)} %constant_dynamic-slice_fusion.9), channel_id=1, source_target_pairs={{0,32},{16,48},{32,64},{48,80},{64,96},{80,112},{96,128},{112,144}... | collective-permute-start | bytes 1572872 | tf_op jit(solution)/shard_map/ppermute | solution.py:16
  112.7 2.5 collective-permute-start.1
  116.4 1.6 copy.83
  118.0 9.7 %collective-permute-done = bf16[2048,1,128]{0,2,1:T(8,128)(2,1)} collective-permute-done((bf16[2048,1,128]{0,2,1:T(8,128)(2,1)S(1)}, bf16[2048,1,128]{0,2,1:T(8,128)(2,1)}, u32[]{:S(2)}, u32[]{:S(2)}) %collective-permute-start) | collective-permute-done | bytes 524320 | tf_op jit(solution)/shard_map/ppermute | solution.py:16
  127.7 11.7 %collective-permute-done.1 = bf16[2048,1,128]{0,2,1:T(8,128)(2,1)} collective-permute-done((bf16[2048,1,128]{0,2,1:T(8,128)(2,1)S(1)}, bf16[2048,1,128]{0,2,1:T(8,128)(2,1)}, u32[]{:S(2)}, u32[]{:S(2)}) %collective-permute-start.1) | collective-permute-done | bytes 524320 | tf_op jit(solution)/shard_map/ppermute | solution.py:16
  141.6 46.9 %while.60 = (s32[]{:T(128)}, f32[1,1,512]{2,1,0:T(1,128)S(1)}, f32[1,1,512]{2,1,0:T(1,128)S(1)}, f32[1,1,512,128]{3,2,1,0:T(8,128)}, s32[12,512]{1,0:T(8,128)S(1...) while((s32[]{:T(128)}, f32[1,1,512]{2,1,0:T(1,128)S(1)}, ...), condition=%wide.region_6.7_spmd.clone, body=%wide.region_3.6_spmd.clone.sunk | while | flops 139135488 | bytes 6226633 | solution.py:81
  151.2 1.5 fusion.141
  159.0 1.5 fusion.141
  188.5 38.4 %while.61 = (s32[]{:T(128)}, f32[1,1,512]{2,1,0:T(1,128)S(1)}, f32[1,1,512]{2,1,0:T(1,128)S(1)}, f32[1,1,512,128]{3,2,1,0:T(8,128)S(1)}, s32[12,512]{1,0:T(8,128...) while((s32[]{:T(128)}, f32[1,1,512]{2,1,0:T(1,128)S(1)}, ...), condition=%wide.region_10.11_spmd.clone, body=%wide.region_7.10_spmd.clone.sunk | while | flops 139135488 | bytes 4129425 | solution.py:81
  190.2 1.5 fusion.148
  193.4 1.5 fusion.148
  196.6 1.5 fusion.148
  199.8 1.5 fusion.148
  203.0 1.5 fusion.148
  206.2 1.5 fusion.148
  209.4 1.5 fusion.148
  212.6 1.5 fusion.148
  215.8 1.5 fusion.148
  219.0 1.5 fusion.148
  222.2 1.5 fusion.148
  225.4 1.5 fusion.148
  226.9 38.3 %while.62 = (s32[]{:T(128)}, f32[1,1,512]{2,1,0:T(1,128)S(1)}, f32[1,1,512]{2,1,0:T(1,128)S(1)}, f32[1,1,512,128]{3,2,1,0:T(8,128)S(1)}, s32[12,512]{1,0:T(8,128...) while((s32[]{:T(128)}, f32[1,1,512]{2,1,0:T(1,128)S(1)}, ...), condition=%wide.region_14.15_spmd.clone, body=%wide.region_11.14_spmd.clone.sunk | while | flops 139135488 | bytes 4129425 | solution.py:81
  265.2 38.3 %while.63 = (s32[]{:T(128)}, f32[1,1,512]{2,1,0:T(1,128)S(1)}, f32[1,1,512]{2,1,0:T(1,128)S(1)}, f32[1,1,512,128]{3,2,1,0:T(8,128)S(1)}, s32[12,512]{1,0:T(8,128...) while((s32[]{:T(128)}, f32[1,1,512]{2,1,0:T(1,128)S(1)}, ...), condition=%wide.region_18.19_spmd.clone, body=%wide.region_15.18_spmd.clone.sunk | while | flops 139135488 | bytes 4129425 | solution.py:81
  305.1 20.8 %all_to_all.35 = bf16[16,128,128]{2,1,0:T(8,128)(2,1)S(1)} all-to-all(bf16[16,128,128]{2,1,0:T(8,128)(2,1)S(1)} %bitcast.254), channel_id=1, replica_groups=mesh['docs'=32,'heads'=16] {'heads'}, dimensions={0} | all-to-all | bytes 1048576 | tf_op jit(solution)/shard_map/all_to_all | solution.py:130
  (423 shorter events, 150.5 us)
Async XLA Ops:
  6.5 15.9 %copy-start.4 = (s32[32]{0:T(128)S(1)}, s32[32]{0:T(128)}, u32[]{:S(2)}) copy-start(s32[32]{0:T(128)} %param.15) | copy-start | bytes 388
  6.5 56.0 %all-gather.5.cloned.1.call-start = ((), (), s32[]{:S(2)}) async-start(), calls=%async_computation.3 | async-start | bytes 2228224 | tf_op jit(solution)/shard_map/all_gather | solution.py:104
  8.2 98.5 %all-gather.3.cloned.1.call-start = ((), (), s32[]{:S(2)}) async-start(), calls=%async_computation.2 | async-start | bytes 2228224 | tf_op jit(solution)/shard_map/all_gather | solution.py:103
  12.0 59.2 %all-to-all-start = ((bf16[128,16,128]{0,2,1:T(8,128)(2,1)}), bf16[128,16,128]{0,2,1:T(8,128)(2,1)S(1)}, u32[]{:S(2)}, u32[]{:S(2)}) async-start(bf16[128,16,128]{0,2,1:T(8,128)(2,1)} %bitcast.4), calls=%async_computation | async-start | bytes 1048576 | tf_op jit(solution)/shard_map/all_to_all | solution.py:118
  63.6 51.6 %collective-permute-start.2 = (bf16[2048,1,128]{0,2,1:T(8,128)(2,1)S(1)}, bf16[2048,1,128]{0,2,1:T(8,128)(2,1)S(1)}, u32[]{:S(2)}, u32[]{:S(2)}) collective-permute-start(bf16[2048,1,128]{0,2,1:T(8,128)(2,1)S(1)} %constant_dynamic-slice_fusion.8), channel_id=1, source_target_pairs={{0,32},{16,48},{32,64},{48,80},{64,96},{80,112},{96,128},{112,144}... | collective-permute-start | bytes 1572872 | tf_op jit(solution)/shard_map/ppermute | solution.py:16
  68.5 46.7 %collective-permute-start.3 = (bf16[2048,1,128]{0,2,1:T(8,128)(2,1)S(1)}, bf16[2048,1,128]{0,2,1:T(8,128)(2,1)}, u32[]{:S(2)}, u32[]{:S(2)}) collective-permute-start(bf16[2048,1,128]{0,2,1:T(8,128)(2,1)S(1)} %constant_dynamic-slice_fusion.8), channel_id=1, source_target_pairs={{0,16},{16,32},{32,48},{48,64},{64,80},{80,96},{96,112},{112,128},... | collective-permute-start | bytes 1572872 | tf_op jit(solution)/shard_map/ppermute | solution.py:16
  107.8 19.8 %collective-permute-start = (bf16[2048,1,128]{0,2,1:T(8,128)(2,1)S(1)}, bf16[2048,1,128]{0,2,1:T(8,128)(2,1)}, u32[]{:S(2)}, u32[]{:S(2)}) collective-permute-start(bf16[2048,1,128]{0,2,1:T(8,128)(2,1)S(1)} %constant_dynamic-slice_fusion.9), channel_id=1, source_target_pairs={{0,32},{16,48},{32,64},{48,80},{64,96},{80,112},{96,128},{112,144}... | collective-permute-start | bytes 1572872 | tf_op jit(solution)/shard_map/ppermute | solution.py:16
  112.7 26.6 %collective-permute-start.1 = (bf16[2048,1,128]{0,2,1:T(8,128)(2,1)S(1)}, bf16[2048,1,128]{0,2,1:T(8,128)(2,1)}, u32[]{:S(2)}, u32[]{:S(2)}) collective-permute-start(bf16[2048,1,128]{0,2,1:T(8,128)(2,1)S(1)} %constant_dynamic-slice_fusion.9), channel_id=1, source_target_pairs={{0,16},{16,32},{32,48},{48,64},{64,80},{80,96},{96,112},{112,128},... | collective-permute-start | bytes 1572872 | tf_op jit(solution)/shard_map/ppermute | solution.py:16
  141.6 46.9 %copy-start.1 = (f32[1,1,512,128]{3,2,1,0:T(8,128)S(1)}, f32[1,1,512,128]{3,2,1,0:T(8,128)}, u32[]{:S(2)}) copy-start(f32[1,1,512,128]{3,2,1,0:T(8,128)} %custom-call.5) | copy-start | bytes 786436
  141.6 1.8 copy-start.2
  144.9 0.7 copy-start.3
  145.6 1.7 copy-start.2
  148.8 0.7 copy-start.3
  149.5 1.7 copy-start.2
  152.7 0.7 copy-start.3
  153.4 1.7 copy-start.2
  156.6 0.7 copy-start.3
  157.3 1.7 copy-start.2
  160.5 0.7 copy-start.3
  161.2 1.7 copy-start.2
  164.4 0.7 copy-start.3
  165.1 1.7 copy-start.2
  168.3 0.7 copy-start.3
  169.0 1.7 copy-start.2
  172.2 0.7 copy-start.3
  172.9 1.7 copy-start.2
  176.8 1.7 copy-start.2
  180.0 0.7 copy-start.3
  180.7 1.7 copy-start.2
  184.6 1.7 copy-start.2
  187.8 0.7 copy-start.3
  188.5 38.4 %copy-start = (f32[1,1,512,128]{3,2,1,0:T(8,128)S(1)}, f32[1,1,512,128]{3,2,1,0:T(8,128)}, u32[]{:S(2)}) copy-start(f32[1,1,512,128]{3,2,1,0:T(8,128)} %custom-call.8) | copy-start | bytes 786436
  (2 other events, 1.4 us)
Sparse Core Ops, SparseCore 0:
  9.4 53.0 all-gather.4
  64.6 42.1 all-gather.2
where the time goes:
time: 338 us; the launch traced here: 334 us
  matrix products  134 us (40%)
  waiting for transfers between devices  93.2 us (28%)
  starting transfers between devices  25.3 us (7%)
  local copies, waits for them, and re-layouts  23.3 us (7%)
  other arithmetic  21 us (6%)
  blocking collectives  20.8 us (6%)
  between operations  13.8 us (4%)
    dot_general x48, matrix products, update(): jnp.einsum('gsqk,kgd->gsqd', weights.astype(jnp.bfloat16), value_tile_row...  71.3 us
    dot_general x48, matrix products, update(): jnp.einsum('qgsd,kgd->gsqk', query_tile_rows, key_tile_rows, preferred_el...  62.6 us
    all_gather x1, waiting for transfers between devices, per_device(): lax.all_gather(values, 'heads', axis=0, tiled=True)  39.4 us
    all_gather x1, waiting for transfers between devices, per_device(): lax.all_gather(keys, 'heads', axis=0, tiled=True)  32.4 us
    ppermute x4, waiting for transfers between devices, from_behind(): return lax.ppermute(x, axis, pairs)  21.4 us
    all_to_all x1, blocking collectives, per_device(): lax.all_to_all(outcome.reshape(block_length, local_heads * HEAD_SIZE), 'h...  20.8 us
    reduce_sum x48, other arithmetic, update(): running_sum = running_sum * factor + jnp.sum(weights, axis=-1)  15.2 us
    ppermute x4, starting transfers between devices, from_behind(): return lax.ppermute(x, axis, pairs)  14.8 us
  transfers between devices with their start and end apart: 7, of which 4 were waited for; matrix products, arithmetic and copies ran while one was open for 4% of the time, Pallas kernels for 0%

commit v1 on v0

v1 whole, which is shorter than its diff:
```python
import math

import jax
import jax.numpy as jnp
from jax import lax
from jax.experimental import pallas as pl
from jax.experimental.pallas import tpu as pltpu
from jax.sharding import Mesh, PartitionSpec as P

QUERY_HEADS = 16
KEY_VALUE_HEADS = 4
HEAD_SIZE = 128
GROUP = QUERY_HEADS // KEY_VALUE_HEADS
ROWS = 128
PIECE = 4 * ROWS
WIDTH = GROUP * HEAD_SIZE
REACH = 6
EXPONENT_SCALE = math.log2(math.e) / math.sqrt(HEAD_SIZE)
MASKED = -1e30
ALL = ("docs", "sub", "chip", "core")
TEAM = ("chip", "core")


def columns(x, index, width):
    return x[:, index * width : (index + 1) * width]


def shift(x, by, count):
    pairs = [(i, (i + by * 4) % count) for i in range(count)]
    return lax.ppermute(x, ALL, pairs)


def attend_kernel(info, low_ref, q_ref, *refs):
    pieces = refs[: REACH + 1]
    out_ref = refs[REACH + 1]
    kv, top, total, acc, sems = refs[REACH + 2 :]
    copies = [pltpu.make_async_copy(pieces[n], kv.at[n], sems.at[n]) for n in range(REACH + 1)]
    for copy in copies:
        copy.start()
    for copy in copies:
        copy.wait()
    base = info[0]

    def update(block, piece, masked):
        key_rows = kv[piece, :, :, 0:HEAD_SIZE].reshape(PIECE, HEAD_SIZE)
        value_rows = kv[piece, :, :, HEAD_SIZE : 2 * HEAD_SIZE].reshape(PIECE, HEAD_SIZE)
        if masked:
            key_place = base - piece * PIECE + lax.broadcasted_iota(jnp.int32, (ROWS, PIECE), 1)
            place = base + block * ROWS + lax.broadcasted_iota(jnp.int32, (ROWS, PIECE), 0)
            low = low_ref[pl.ds(block * ROWS, ROWS), :]
            low = jnp.concatenate([low] * (PIECE // 128), axis=1)
            visible = (key_place >= low) & (key_place <= place)
        for head in range(GROUP):
            query = q_ref[block, :, head * HEAD_SIZE : (head + 1) * HEAD_SIZE]
            scores = lax.dot_general(
                query, key_rows, (((1,), (1,)), ((), ())), preferred_element_type=jnp.float32
            )
            if masked:
                scores = jnp.where(visible, scores, MASKED)
            old = top[head]
            new = jnp.maximum(old, jnp.max(scores, axis=1, keepdims=True))
            wide = jnp.concatenate([new] * (PIECE // 128), axis=1)
            expo = jnp.exp2((scores - wide) * EXPONENT_SCALE)
            factor = jnp.exp2((old - new) * EXPONENT_SCALE)
            part = expo[:, 0:128]
            for n in range(1, PIECE // 128):
                part = part + expo[:, n * 128 : (n + 1) * 128]
            total[head] = total[head] * factor + part
            acc[head] = acc[head] * factor + jnp.dot(
                expo.astype(jnp.bfloat16), value_rows, preferred_element_type=jnp.float32
            )
            top[head] = new

    def one_block(block, unused):
        first_low = info[1 + block]
        last_low = info[5 + block]
        top[...] = jnp.full_like(top, MASKED)
        total[...] = jnp.zeros_like(total)
        acc[...] = jnp.zeros_like(acc)

        def one_piece(piece, unused):
            start = base - piece * PIECE
            needed = start + PIECE > first_low
            whole = (piece > 0) & (start >= last_low)

            @pl.when(needed & whole)
            def _():
                update(block, piece, False)

            @pl.when(needed & jnp.logical_not(whole))
            def _():
                update(block, piece, True)

            return unused

        lax.fori_loop(0, REACH + 1, one_piece, 0)
        for head in range(GROUP):
            denominator = jnp.sum(total[head], axis=1, keepdims=True)
            out_ref[block, :, head * HEAD_SIZE : (head + 1) * HEAD_SIZE] = (
                acc[head] / denominator
            ).astype(jnp.bfloat16)
        return unused

    lax.fori_loop(0, PIECE // ROWS, one_block, 0)


def attend(info, low, query_team, pieces):
    vmem = pl.BlockSpec(memory_space=pltpu.VMEM)
    return pl.pallas_call(
        attend_kernel,
        out_shape=jax.ShapeDtypeStruct((4, ROWS, WIDTH), jnp.bfloat16),
        in_specs=[pl.BlockSpec(memory_space=pltpu.SMEM), vmem, vmem]
        + [pl.BlockSpec(memory_space=pl.ANY)] * len(pieces),
        out_specs=vmem,
        scratch_shapes=[
            pltpu.VMEM((REACH + 1, 4, ROWS, 2 * HEAD_SIZE), jnp.bfloat16),
            pltpu.VMEM((GROUP, ROWS, 128), jnp.float32),
            pltpu.VMEM((GROUP, ROWS, 128), jnp.float32),
            pltpu.VMEM((GROUP, ROWS, HEAD_SIZE), jnp.float32),
            pltpu.SemaphoreType.DMA((REACH + 1,)),
        ],
        compiler_params=pltpu.CompilerParams(vmem_limit_bytes=24 * 1024 * 1024),
        cost_estimate=pl.CostEstimate(
            flops=3_000_000_000, bytes_accessed=4_000_000, transcendentals=6_000_000
        ),
        name="attend",
    )(info, low, query_team, *pieces)


def per_device(queries, keys, values, lengths):
    count = lax.axis_size("docs") * 16
    base = (lax.axis_index("docs") * 4 + lax.axis_index("sub")) * PIECE
    bounds = jnp.cumsum(lengths)
    place = base + jnp.arange(PIECE, dtype=jnp.int32)
    low = jnp.max(jnp.where(bounds[None, :] <= place[:, None], bounds[None, :], 0), axis=1)
    info = jnp.concatenate([base[None], low[0::ROWS], low[ROWS - 1 :: ROWS]]).astype(jnp.int32)
    low = jnp.broadcast_to(low[:, None], (PIECE, 128))

    key_value = jnp.stack(
        [
            jnp.concatenate([columns(keys, n, HEAD_SIZE), columns(values, n, HEAD_SIZE)], axis=1)
            for n in range(KEY_VALUE_HEADS)
        ]
    )
    own = lax.all_to_all(key_value, TEAM, 0, 0, tiled=True)
    query_team = jnp.stack([columns(queries, n, WIDTH) for n in range(KEY_VALUE_HEADS)])
    query_team = lax.all_to_all(query_team, TEAM, 0, 0, tiled=True)
    back1, back2, back3, back4 = (shift(own, by, count) for by in (1, 2, 3, 4))
    back5 = shift(back1, 4, count)
    back6 = shift(back2, 4, count)
    outcome = attend(info, low, query_team, (own, back1, back2, back3, back4, back5, back6))
    outcome = lax.all_to_all(outcome, TEAM, 0, 0, tiled=True)
    return jnp.concatenate([outcome[n] for n in range(KEY_VALUE_HEADS)], axis=1)


def solution(mesh):
    docs = mesh.shape["docs"]
    fine = Mesh(mesh.devices.reshape(docs, 4, 2, 2), ALL)
    rows = P(ALL, None)
    return jax.shard_map(
        per_device,
        mesh=fine,
        in_specs=(rows, rows, rows, P()),
        out_specs=rows,
        check_vma=False,
    )
```

time: 338 us -> 114 us (0.34)
  the two profiles are of different devices: /device:TPU:32 before, /device:TPU:62 now
where the time goes in v1:
time: 114 us
  starting transfers between devices  34.4 us (30%)
  waiting for transfers between devices  31.9 us (28%)
  Pallas kernels  31.1 us (27%)
  blocking collectives  11.2 us (10%)
  other arithmetic  2.85 us (2%)
  local copies, waits for them, and re-layouts  2.11 us (2%)
    pallas_call x1, Pallas kernels, attend(): pl.pallas_call(attend_kernel, out_shape=jax.ShapeDtypeStruct((4, ROWS, WI...  31.1 us
    ppermute x6, starting transfers between devices, shift(): return lax.ppermute(x, ALL, pairs)  27.3 us
    ppermute x6, waiting for transfers between devices, shift(): return lax.ppermute(x, ALL, pairs)  26.8 us
    all_to_all x1, blocking collectives, per_device(): outcome = lax.all_to_all(outcome, TEAM, 0, 0, tiled=True)  11.2 us
    all_to_all x1, waiting for transfers between devices, per_device(): own = lax.all_to_all(key_value, TEAM, 0, 0, tiled=True)  5.13 us
    all_to_all x1, starting transfers between devices, per_device(): own = lax.all_to_all(key_value, TEAM, 0, 0, tiled=True)  3.64 us
    all_to_all x1, starting transfers between devices, per_device(): query_team = lax.all_to_all(query_team, TEAM, 0, 0, tiled=True)  3.47 us
  transfers between devices with their start and end apart: 8, of which 6 were waited for; matrix products, arithmetic and copies ran while one was open for 1% of the time, Pallas kernels for 0%

profile of v1, /device:TPU:62, one launch (start us, length us, event | category | flops | bytes accessed | tf_op | source)
XLA Modules:
  0.0 113.8 jit_solution(16443934127756815934)
XLA Ops:
  0.0 0.9 fusion
  0.9 0.1 copy-done.1
  1.0 0.0 copy-start
  1.1 0.7 pad_maximum_fusion.2
  1.8 3.6 %all-to-all-start.1 = ((bf16[4,128,256]{2,1,0:T(8,128)(2,1)}), bf16[4,128,256]{2,1,0:T(8,128)(2,1)S(1)}, u32[]{:S(2)}, u32[]{:S(2)}) async-start(bf16[4,128,256]{2,1,0:T(8,128)(2,1)} %pad_maximum_fusion.2), calls=%async_computation.1 | async-start | bytes 524288 | tf_op jit(solution)/shard_map/all_to_all | solution.py:145
  5.5 0.9 pad_maximum_fusion
  6.4 5.1 %all-to-all-done.1.refs_0_ = bf16[4,128,256]{2,1,0:T(8,128)(2,1)S(1)} async-done(((bf16[4,128,256]{2,1,0:T(8,128)(2,1)}), bf16[4,128,256]{2,1,0:T(8,128)(2,1)S(1)}, u32[]{:S(2)}, u32[]{:S(2)}) %all-to-all-start.1) | async-done | bytes 262176 | tf_op jit(solution)/shard_map/all_to_all | solution.py:145
  11.5 3.5 %all-to-all-start = ((bf16[4,128,512]{2,1,0:T(8,128)(2,1)}), bf16[4,128,512]{2,1,0:T(8,128)(2,1)S(1)}, u32[]{:S(2)}, u32[]{:S(2)}) async-start(bf16[4,128,512]{2,1,0:T(8,128)(2,1)} %pad_maximum_fusion), calls=%async_computation | async-start | bytes 1048576 | tf_op jit(solution)/shard_map/all_to_all | solution.py:147
  15.0 6.1 %collective-permute-start = (bf16[4,128,256]{2,1,0:T(8,128)(2,1)S(1)}, bf16[4,128,256]{2,1,0:T(8,128)(2,1)S(1)}, u32[]{:S(2)}, u32[]{:S(2)}) collective-permute-start(bf16[4,128,256]{2,1,0:T(8,128)(2,1)S(1)} %all-to-all-done.1.refs_0_), channel_id=1, source_target_pairs={{0,4},{1,5},{2,6},{3,7},{4,8},{5,9},{6,10},{7,11},{8,12},{9,13},{1... | collective-permute-start | bytes 786440 | tf_op jit(solution)/shard_map/ppermute | solution.py:30
  21.1 8.9 %collective-permute-start.1 = (bf16[4,128,256]{2,1,0:T(8,128)(2,1)S(1)}, bf16[4,128,256]{2,1,0:T(8,128)(2,1)S(1)}, u32[]{:S(2)}, u32[]{:S(2)}) collective-permute-start(bf16[4,128,256]{2,1,0:T(8,128)(2,1)S(1)} %all-to-all-done.1.refs_0_), channel_id=1, source_target_pairs={{0,8},{1,9},{2,10},{3,11},{4,12},{5,13},{6,14},{7,15},{8,16},{9,17... | collective-permute-start | bytes 786440 | tf_op jit(solution)/shard_map/ppermute | solution.py:30
  29.9 2.8 %collective-permute-start.2 = (bf16[4,128,256]{2,1,0:T(8,128)(2,1)S(1)}, bf16[4,128,256]{2,1,0:T(8,128)(2,1)S(1)}, u32[]{:S(2)}, u32[]{:S(2)}) collective-permute-start(bf16[4,128,256]{2,1,0:T(8,128)(2,1)S(1)} %all-to-all-done.1.refs_0_), channel_id=1, source_target_pairs={{0,12},{1,13},{2,14},{3,15},{4,16},{5,17},{6,18},{7,19},{8,20},{9,... | collective-permute-start | bytes 786440 | tf_op jit(solution)/shard_map/ppermute | solution.py:30
  32.7 3.4 %collective-permute-start.3 = (bf16[4,128,256]{2,1,0:T(8,128)(2,1)S(1)}, bf16[4,128,256]{2,1,0:T(8,128)(2,1)S(1)}, u32[]{:S(2)}, u32[]{:S(2)}) collective-permute-start(bf16[4,128,256]{2,1,0:T(8,128)(2,1)S(1)} %all-to-all-done.1.refs_0_), channel_id=1, source_target_pairs={{0,16},{1,17},{2,18},{3,19},{4,20},{5,21},{6,22},{7,23},{8,24},{9,... | collective-permute-start | bytes 786440 | tf_op jit(solution)/shard_map/ppermute | solution.py:30
  36.1 11.3 %collective-permute-done.refs_1_ = bf16[4,128,256]{2,1,0:T(8,128)(2,1)S(1)} collective-permute-done((bf16[4,128,256]{2,1,0:T(8,128)(2,1)S(1)}, bf16[4,128,256]{2,1,0:T(8,128)(2,1)S(1)}, u32[]{:S(2)}, u32[]{:S(2)}) %collective-permute-start) | collective-permute-done | bytes 262176 | tf_op jit(solution)/shard_map/ppermute | solution.py:30
  47.4 3.2 %collective-permute-start.4 = (bf16[4,128,256]{2,1,0:T(8,128)(2,1)S(1)}, bf16[4,128,256]{2,1,0:T(8,128)(2,1)S(1)}, u32[]{:S(2)}, u32[]{:S(2)}) collective-permute-start(bf16[4,128,256]{2,1,0:T(8,128)(2,1)S(1)} %collective-permute-done.refs_1_), channel_id=1, source_target_pairs={{0,16},{1,17},{2,18},{3,19},{4,20},{5,21},{6,22},{7,23},{8,24},{9,... | collective-permute-start | bytes 786440 | tf_op jit(solution)/shard_map/ppermute | solution.py:30
  50.6 4.2 %collective-permute-done.1.refs_2_ = bf16[4,128,256]{2,1,0:T(8,128)(2,1)S(1)} collective-permute-done((bf16[4,128,256]{2,1,0:T(8,128)(2,1)S(1)}, bf16[4,128,256]{2,1,0:T(8,128)(2,1)S(1)}, u32[]{:S(2)}, u32[]{:S(2)}) %collective-permute-start.1) | collective-permute-done | bytes 262176 | tf_op jit(solution)/shard_map/ppermute | solution.py:30
  54.8 2.9 %collective-permute-start.5 = (bf16[4,128,256]{2,1,0:T(8,128)(2,1)S(1)}, bf16[4,128,256]{2,1,0:T(8,128)(2,1)S(1)}, u32[]{:S(2)}, u32[]{:S(2)}) collective-permute-start(bf16[4,128,256]{2,1,0:T(8,128)(2,1)S(1)} %collective-permute-done.1.refs_2_), channel_id=1, source_target_pairs={{0,16},{1,17},{2,18},{3,19},{4,20},{5,21},{6,22},{7,23},{8,24},{9,... | collective-permute-start | bytes 786440 | tf_op jit(solution)/shard_map/ppermute | solution.py:30
  57.7 0.0 copy-start.2
  57.7 0.6 copy-done.2
  58.4 0.1 copy.7
  58.5 0.1 reduce-window.8
  58.5 0.1 reduce
  58.6 0.1 select_reduce_fusion
  58.7 0.1 slice.54
  58.8 0.1 slice.55
  58.9 0.1 pad_add_fusion.info
  59.0 0.2 collective-permute-done.3.refs_4_
  59.2 5.6 %collective-permute-done.4.refs_5_ = bf16[4,128,256]{2,1,0:T(8,128)(2,1)S(1)} collective-permute-done((bf16[4,128,256]{2,1,0:T(8,128)(2,1)S(1)}, bf16[4,128,256]{2,1,0:T(8,128)(2,1)S(1)}, u32[]{:S(2)}, u32[]{:S(2)}) %collective-permute-start.4) | collective-permute-done | bytes 262176 | tf_op jit(solution)/shard_map/ppermute | solution.py:30
  64.9 5.5 %collective-permute-done.5.refs_6_ = bf16[4,128,256]{2,1,0:T(8,128)(2,1)S(1)} collective-permute-done((bf16[4,128,256]{2,1,0:T(8,128)(2,1)S(1)}, bf16[4,128,256]{2,1,0:T(8,128)(2,1)S(1)}, u32[]{:S(2)}, u32[]{:S(2)}) %collective-permute-start.5) | collective-permute-done | bytes 262176 | tf_op jit(solution)/shard_map/ppermute | solution.py:30
  70.4 0.1 broadcast_in_dim.24.low_ref
  70.5 31.1 %attend.1 = bf16[4,128,512]{2,1,0:T(8,128)(2,1)S(1)} custom-call(s32[9]{0:T(128)S(1)} %pad_add_fusion.info, s32[512,128]{1,0:T(8,128)S(1)} %broadcast_in_dim.24.low_ref, bf16[4,128,512]{2,1,0:T(8,128)(2,1)S(1)} %all-to-all-done.q_ref, bf16[4,128,256]{2,1,0:T(8,128)(2,1)S(1)} %all-to-all-done.1.refs_0_, ...), custom_call_target="tpu_custom_call" | custom-call | flops 3000000000 | bytes 4000000 | tf_op jit(solution)/shard_map/attend/pallas_call | solution.py:109
  101.7 11.2 %all_to_all.15 = bf16[4,128,512]{2,1,0:T(8,128)(2,1)S(1)} all-to-all(bf16[4,128,512]{2,1,0:T(8,128)(2,1)S(1)} %attend.1), channel_id=1, replica_groups=mesh['docs'=32,'sub'=4,'chip'=2,'core'=2] {'chip','core'}, dimensions={0} | all-to-all | bytes 1048576 | tf_op jit(solution)/shard_map/all_to_all | solution.py:152
  112.9 0.8 pad_maximum_fusion.1
  (10 shorter events, 0.1 us)
Async XLA Ops:
  0.0 1.0 copy-start.1
  1.0 4.4 %copy-start = (bf16[128,2048]{1,0:T(8,128)(2,1)S(1)}, bf16[128,2048]{1,0:T(8,128)(2,1)}, u32[]{:S(2)}) copy-start(bf16[128,2048]{1,0:T(8,128)(2,1)} %param.4) | copy-start | bytes 1572868
  1.8 9.7 %all-to-all-start.1 = ((bf16[4,128,256]{2,1,0:T(8,128)(2,1)}), bf16[4,128,256]{2,1,0:T(8,128)(2,1)S(1)}, u32[]{:S(2)}, u32[]{:S(2)}) async-start(bf16[4,128,256]{2,1,0:T(8,128)(2,1)} %pad_maximum_fusion.2), calls=%async_computation.1 | async-start | bytes 524288 | tf_op jit(solution)/shard_map/all_to_all | solution.py:145
  11.5 47.8 %all-to-all-start = ((bf16[4,128,512]{2,1,0:T(8,128)(2,1)}), bf16[4,128,512]{2,1,0:T(8,128)(2,1)S(1)}, u32[]{:S(2)}, u32[]{:S(2)}) async-start(bf16[4,128,512]{2,1,0:T(8,128)(2,1)} %pad_maximum_fusion), calls=%async_computation | async-start | bytes 1048576 | tf_op jit(solution)/shard_map/all_to_all | solution.py:147
  15.0 32.4 %collective-permute-start = (bf16[4,128,256]{2,1,0:T(8,128)(2,1)S(1)}, bf16[4,128,256]{2,1,0:T(8,128)(2,1)S(1)}, u32[]{:S(2)}, u32[]{:S(2)}) collective-permute-start(bf16[4,128,256]{2,1,0:T(8,128)(2,1)S(1)} %all-to-all-done.1.refs_0_), channel_id=1, source_target_pairs={{0,4},{1,5},{2,6},{3,7},{4,8},{5,9},{6,10},{7,11},{8,12},{9,13},{1... | collective-permute-start | bytes 786440 | tf_op jit(solution)/shard_map/ppermute | solution.py:30
  21.1 33.7 %collective-permute-start.1 = (bf16[4,128,256]{2,1,0:T(8,128)(2,1)S(1)}, bf16[4,128,256]{2,1,0:T(8,128)(2,1)S(1)}, u32[]{:S(2)}, u32[]{:S(2)}) collective-permute-start(bf16[4,128,256]{2,1,0:T(8,128)(2,1)S(1)} %all-to-all-done.1.refs_0_), channel_id=1, source_target_pairs={{0,8},{1,9},{2,10},{3,11},{4,12},{5,13},{6,14},{7,15},{8,16},{9,17... | collective-permute-start | bytes 786440 | tf_op jit(solution)/shard_map/ppermute | solution.py:30
  29.9 29.1 %collective-permute-start.2 = (bf16[4,128,256]{2,1,0:T(8,128)(2,1)S(1)}, bf16[4,128,256]{2,1,0:T(8,128)(2,1)S(1)}, u32[]{:S(2)}, u32[]{:S(2)}) collective-permute-start(bf16[4,128,256]{2,1,0:T(8,128)(2,1)S(1)} %all-to-all-done.1.refs_0_), channel_id=1, source_target_pairs={{0,12},{1,13},{2,14},{3,15},{4,16},{5,17},{6,18},{7,19},{8,20},{9,... | collective-permute-start | bytes 786440 | tf_op jit(solution)/shard_map/ppermute | solution.py:30
  32.7 26.5 %collective-permute-start.3 = (bf16[4,128,256]{2,1,0:T(8,128)(2,1)S(1)}, bf16[4,128,256]{2,1,0:T(8,128)(2,1)S(1)}, u32[]{:S(2)}, u32[]{:S(2)}) collective-permute-start(bf16[4,128,256]{2,1,0:T(8,128)(2,1)S(1)} %all-to-all-done.1.refs_0_), channel_id=1, source_target_pairs={{0,16},{1,17},{2,18},{3,19},{4,20},{5,21},{6,22},{7,23},{8,24},{9,... | collective-permute-start | bytes 786440 | tf_op jit(solution)/shard_map/ppermute | solution.py:30
  47.4 17.5 %collective-permute-start.4 = (bf16[4,128,256]{2,1,0:T(8,128)(2,1)S(1)}, bf16[4,128,256]{2,1,0:T(8,128)(2,1)S(1)}, u32[]{:S(2)}, u32[]{:S(2)}) collective-permute-start(bf16[4,128,256]{2,1,0:T(8,128)(2,1)S(1)} %collective-permute-done.refs_1_), channel_id=1, source_target_pairs={{0,16},{1,17},{2,18},{3,19},{4,20},{5,21},{6,22},{7,23},{8,24},{9,... | collective-permute-start | bytes 786440 | tf_op jit(solution)/shard_map/ppermute | solution.py:30
  54.8 15.6 %collective-permute-start.5 = (bf16[4,128,256]{2,1,0:T(8,128)(2,1)S(1)}, bf16[4,128,256]{2,1,0:T(8,128)(2,1)S(1)}, u32[]{:S(2)}, u32[]{:S(2)}) collective-permute-start(bf16[4,128,256]{2,1,0:T(8,128)(2,1)S(1)} %collective-permute-done.1.refs_2_), channel_id=1, source_target_pairs={{0,16},{1,17},{2,18},{3,19},{4,20},{5,21},{6,22},{7,23},{8,24},{9,... | collective-permute-start | bytes 786440 | tf_op jit(solution)/shard_map/ppermute | solution.py:30
  57.7 0.7 copy-start.2

commit v2 on v1

v2 whole, which is shorter than its diff:
```python
import math

import jax
import jax.numpy as jnp
from jax import lax
from jax.experimental import pallas as pl
from jax.experimental.pallas import tpu as pltpu
from jax.sharding import Mesh, PartitionSpec as P

QUERY_HEADS = 16
KEY_VALUE_HEADS = 4
HEAD_SIZE = 128
GROUP = QUERY_HEADS // KEY_VALUE_HEADS
ROWS = 128
PIECE = 4 * ROWS
WIDTH = GROUP * HEAD_SIZE
REACH = 6
EXPONENT_SCALE = math.log2(math.e) / math.sqrt(HEAD_SIZE)
MASKED = -1e30
ALL = ("docs", "hi", "lo")


def permute(x, docs, target):
    pairs = []
    for doc in range(docs):
        for hi in range(4):
            for lo in range(4):
                to_doc, to_hi, to_lo = target(doc, hi, lo)
                pairs.append((doc * 16 + hi * 4 + lo, (to_doc % docs) * 16 + to_hi * 4 + to_lo))
    return lax.ppermute(x, ALL, pairs)


def to_worker(x, turn, docs):
    return permute(x, docs, lambda doc, hi, lo: (doc, (lo + turn) % 4, hi))


def to_owner(x, turn, docs):
    return permute(x, docs, lambda doc, hi, lo: (doc, lo, (hi - turn) % 4))


def chips_on(x, by, docs):
    def target(doc, hi, lo):
        chip = 2 * doc + lo // 2 + by
        return chip // 2, hi, 2 * (chip % 2) + lo % 2

    return permute(x, docs, target)


def other_core(x, docs):
    return permute(x, docs, lambda doc, hi, lo: (doc, hi, lo ^ 1))


def attend_kernel(info, place_ref, low_ref, column_ref, q_ref, *refs):
    pieces = refs[: REACH + 1]
    out_ref = refs[REACH + 1]
    kv, top, total, acc, sems = refs[REACH + 2 :]
    copies = [pltpu.make_async_copy(pieces[n], kv.at[n], sems.at[n]) for n in range(REACH + 1)]
    for copy in copies:
        copy.start()
    top[...] = jnp.full_like(top, MASKED)
    total[...] = jnp.zeros_like(total)
    acc[...] = jnp.zeros_like(acc)
    for copy in copies:
        copy.wait()
    first_low, last_low = info[REACH + 1], info[REACH + 2]

    def update(piece, masked):
        key_rows = kv[piece, :, :, 0:HEAD_SIZE].reshape(PIECE, HEAD_SIZE)
        value_rows = kv[piece, :, :, HEAD_SIZE : 2 * HEAD_SIZE].reshape(PIECE, HEAD_SIZE)

        def scores_of(head):
            query = q_ref[:, :, head * HEAD_SIZE : (head + 1) * HEAD_SIZE].reshape(PIECE, HEAD_SIZE)
            return lax.dot_general(
                query, key_rows, (((1,), (1,)), ((), ())), preferred_element_type=jnp.float32
            )

        if masked:
            key_place = column_ref[0:1, :] + info[piece]
            low = jnp.concatenate([low_ref[...]] * (PIECE // 128), axis=1)
            place = jnp.concatenate([place_ref[...]] * (PIECE // 128), axis=1)
            visible = (key_place >= low) & (key_place <= place)
        ahead = scores_of(0)
        for head in range(GROUP):
            scores = ahead
            if head + 1 < GROUP:
                ahead = scores_of(head + 1)
            if masked:
                scores = jnp.where(visible, scores, MASKED)
            old = top[head]
            new = jnp.maximum(old, jnp.max(scores, axis=1, keepdims=True))
            wide = jnp.concatenate([new] * (PIECE // 128), axis=1)
            expo = jnp.exp2((scores - wide) * EXPONENT_SCALE)
            factor = jnp.exp2((old - new) * EXPONENT_SCALE)
            part = expo[:, 0:128]
            for n in range(1, PIECE // 128):
                part = part + expo[:, n * 128 : (n + 1) * 128]
            total[head] = total[head] * factor + part
            acc[head] = acc[head] * factor + jnp.dot(
                expo.astype(jnp.bfloat16), value_rows, preferred_element_type=jnp.float32
            )
            top[head] = new

    def one_piece(piece, unused):
        start = info[piece]
        needed = start + PIECE > first_low
        whole = (piece > 0) & (start >= last_low)

        @pl.when(needed & whole)
        def _():
            update(piece, False)

        @pl.when(needed & jnp.logical_not(whole))
        def _():
            update(piece, True)

        return unused

    lax.fori_loop(0, REACH + 1, one_piece, 0)
    for head in range(GROUP):
        denominator = jnp.sum(total[head], axis=1, keepdims=True)
        out_ref[:, :, head * HEAD_SIZE : (head + 1) * HEAD_SIZE] = (
            (acc[head] / denominator).astype(jnp.bfloat16).reshape(4, ROWS, HEAD_SIZE)
        )


def attend(info, place, low, column, query_team, pieces):
    vmem = pl.BlockSpec(memory_space=pltpu.VMEM)
    return pl.pallas_call(
        attend_kernel,
        out_shape=jax.ShapeDtypeStruct((4, ROWS, WIDTH), jnp.bfloat16),
        in_specs=[pl.BlockSpec(memory_space=pltpu.SMEM), vmem, vmem, vmem, vmem]
        + [pl.BlockSpec(memory_space=pl.ANY)] * len(pieces),
        out_specs=vmem,
        scratch_shapes=[
            pltpu.VMEM((REACH + 1, 4, ROWS, 2 * HEAD_SIZE), jnp.bfloat16),
            pltpu.VMEM((GROUP, PIECE, 128), jnp.float32),
            pltpu.VMEM((GROUP, PIECE, 128), jnp.float32),
            pltpu.VMEM((GROUP, PIECE, HEAD_SIZE), jnp.float32),
            pltpu.SemaphoreType.DMA((REACH + 1,)),
        ],
        compiler_params=pltpu.CompilerParams(vmem_limit_bytes=40 * 1024 * 1024),
        cost_estimate=pl.CostEstimate(
            flops=3_000_000_000, bytes_accessed=4_000_000, transcendentals=6_000_000
        ),
        name="attend",
    )(info, place, low, column, query_team, *pieces)


def per_device(queries, keys, values, lengths):
    docs = lax.axis_size("docs")
    hi, lo = lax.axis_index("hi"), lax.axis_index("lo")

    def head_of(turn):
        return lax.rem(lo + turn, 4)

    def columns(x, turn, width):
        return lax.dynamic_slice_in_dim(x, head_of(turn) * width, width, 1)

    own = jnp.stack(
        [
            to_worker(
                jnp.concatenate(
                    [columns(keys, turn, HEAD_SIZE), columns(values, turn, HEAD_SIZE)], axis=1
                ),
                turn,
                docs,
            )
            for turn in range(4)
        ]
    )
    query_team = jnp.stack(
        [to_worker(columns(queries, turn, WIDTH), turn, docs) for turn in range(4)]
    )

    back = [chips_on(own, by, docs) for by in (1, 2, 3)]
    near, far = other_core(back[0], docs), other_core(back[1], docs)
    core = lax.rem(lo, 2)
    mixed = other_core(jnp.where(core == 0, own, back[2]), docs)

    base = (lax.axis_index("docs") * 4 + lo) * PIECE
    behind = jnp.stack([0, 2, 4, 6, 1 + 2 * core, 3 + 2 * core, 5 - 4 * core]).astype(jnp.int32)
    quarter = lax.rem(hi - jnp.arange(4, dtype=jnp.int32) + 4, 4)
    column = (quarter[:, None] * ROWS + jnp.arange(ROWS, dtype=jnp.int32)[None, :]).reshape(PIECE)
    place = base + column
    bounds = jnp.cumsum(lengths)
    low = jnp.max(jnp.where(bounds[None, :] <= place[:, None], bounds[None, :], 0), axis=1)
    info = jnp.concatenate(
        [base - behind * PIECE, jnp.min(low)[None], jnp.max(low)[None]]
    ).astype(jnp.int32)
    outcome = attend(
        info,
        jnp.broadcast_to(place[:, None], (PIECE, 128)),
        jnp.broadcast_to(low[:, None], (PIECE, 128)),
        jnp.broadcast_to(column[None, :], (8, PIECE)),
        query_team,
        (own, *back, near, far, mixed),
    )
    outcome = [to_owner(outcome[turn], turn, docs) for turn in range(4)]
    twice = jnp.concatenate(outcome + outcome, axis=1)
    return lax.dynamic_slice_in_dim(twice, lax.rem(4 - lo, 4) * WIDTH, QUERY_HEADS * HEAD_SIZE, 1)


def solution(mesh):
    docs = mesh.shape["docs"]
    fine = Mesh(mesh.devices.reshape(docs, 4, 4), ALL)
    rows = P(ALL, None)
    return jax.shard_map(
        per_device,
        mesh=fine,
        in_specs=(rows, rows, rows, P()),
        out_specs=rows,
        check_vma=False,
    )
```

time: 114 us -> 98.5 us (0.86)
  the two profiles are of different devices: /device:TPU:62 before, /device:TPU:63 now
where the time goes in v2:
time: 98.5 us; the launch traced here: 97.9 us
  starting transfers between devices  71.8 us (73%)
  waiting for transfers between devices  14.2 us (14%)
  Pallas kernels  5.08 us (5%)
  other arithmetic  3.27 us (3%)
  local copies, waits for them, and re-layouts  3.03 us (3%)
    ppermute x18, starting transfers between devices, permute(): return lax.ppermute(x, ALL, pairs)  71.8 us
    ppermute x18, waiting for transfers between devices, permute(): return lax.ppermute(x, ALL, pairs)  14.2 us
    pallas_call x1, Pallas kernels, attend(): pl.pallas_call(attend_kernel, out_shape=jax.ShapeDtypeStruct((4, ROWS, WI...  5.08 us
  transfers between devices with their start and end apart: 18, of which 4 were waited for; matrix products, arithmetic and copies ran while one was open for 4% of the time, Pallas kernels for 0%

profile of v2, /device:TPU:63, one launch (start us, length us, event | category | flops | bytes accessed | tf_op | source)
XLA Modules:
  0.0 97.9 jit_solution(3492895714395560125)
XLA Ops:
  0.0 1.0 constant_dynamic-slice_fusion.7
  1.0 11.2 %collective-permute-start.6 = (bf16[128,256]{1,0:T(8,128)(2,1)S(1)}, bf16[128,256]{1,0:T(8,128)(2,1)S(1)}, u32[]{:S(2)}, u32[]{:S(2)}) collective-permute-start(bf16[128,256]{1,0:T(8,128)(2,1)S(1)} %pad_maximum_fusion.4), channel_id=1, source_target_pairs={{0,8},{1,12},{2,0},{3,4},{4,9},{5,13},{6,1},{7,5},{8,10},{9,14},{1... | collective-permute-start | bytes 196616 | tf_op jit(solution)/shard_map/ppermute | solution.py:30
  12.2 2.3 %collective-permute-start.7 = (bf16[128,256]{1,0:T(8,128)(2,1)S(1)}, bf16[128,256]{1,0:T(8,128)(2,1)S(1)}, u32[]{:S(2)}, u32[]{:S(2)}) collective-permute-start(bf16[128,256]{1,0:T(8,128)(2,1)S(1)} %pad_maximum_fusion.5), channel_id=1, source_target_pairs={{0,12},{1,0},{2,4},{3,8},{4,13},{5,1},{6,5},{7,9},{8,14},{9,2},{10... | collective-permute-start | bytes 196616 | tf_op jit(solution)/shard_map/ppermute | solution.py:30
  14.5 4.8 %collective-permute-start.5 = (bf16[128,256]{1,0:T(8,128)(2,1)S(1)}, bf16[128,256]{1,0:T(8,128)(2,1)S(1)}, u32[]{:S(2)}, u32[]{:S(2)}) collective-permute-start(bf16[128,256]{1,0:T(8,128)(2,1)S(1)} %pad_maximum_fusion.3), channel_id=1, source_target_pairs={{0,4},{1,8},{2,12},{3,0},{4,5},{5,9},{6,13},{7,1},{8,6},{9,10},{10... | collective-permute-start | bytes 196616 | tf_op jit(solution)/shard_map/ppermute | solution.py:30
  19.4 1.9 %collective-permute-start.4 = (bf16[128,256]{1,0:T(8,128)(2,1)S(1)}, bf16[128,256]{1,0:T(8,128)(2,1)S(1)}, u32[]{:S(2)}, u32[]{:S(2)}) collective-permute-start(bf16[128,256]{1,0:T(8,128)(2,1)S(1)} %pad_maximum_fusion.2), channel_id=1, source_target_pairs={{0,0},{1,4},{2,8},{3,12},{4,1},{5,5},{6,9},{7,13},{8,2},{9,6},{10,... | collective-permute-start | bytes 196616 | tf_op jit(solution)/shard_map/ppermute | solution.py:30
  21.4 4.5 %collective-permute-start = (bf16[128,512]{1,0:T(8,128)(2,1)S(1)}, bf16[128,512]{1,0:T(8,128)(2,1)S(1)}, u32[]{:S(2)}, u32[]{:S(2)}) collective-permute-start(bf16[128,512]{1,0:T(8,128)(2,1)S(1)} %get-tuple-element.11), channel_id=1, source_target_pairs={{0,0},{1,4},{2,8},{3,12},{4,1},{5,5},{6,9},{7,13},{8,2},{9,6},{10,... | collective-permute-start | bytes 393224 | tf_op jit(solution)/shard_map/ppermute | solution.py:30
  26.0 6.7 %collective-permute-start.1 = (bf16[128,512]{1,0:T(8,128)(2,1)S(1)}, bf16[128,512]{1,0:T(8,128)(2,1)S(1)}, u32[]{:S(2)}, u32[]{:S(2)}) collective-permute-start(bf16[128,512]{1,0:T(8,128)(2,1)S(1)} %get-tuple-element.12), channel_id=1, source_target_pairs={{0,4},{1,8},{2,12},{3,0},{4,5},{5,9},{6,13},{7,1},{8,6},{9,10},{10... | collective-permute-start | bytes 393224 | tf_op jit(solution)/shard_map/ppermute | solution.py:30
  32.8 1.9 %collective-permute-start.10 = (bf16[4,128,256]{2,1,0:T(8,128)(2,1)S(1)}, bf16[4,128,256]{2,1,0:T(8,128)(2,1)S(1)}, u32[]{:S(2)}, u32[]{:S(2)}) collective-permute-start(bf16[4,128,256]{2,1,0:T(8,128)(2,1)S(1)} %pad_maximum_fusion.1.refs_0_), channel_id=1, source_target_pairs={{0,18},{1,19},{2,32},{3,33},{4,22},{5,23},{6,36},{7,37},{8,26},{9,... | collective-permute-start | bytes 786440 | tf_op jit(solution)/shard_map/ppermute | solution.py:30
  34.9 1.9 %collective-permute-start.9 = (bf16[4,128,256]{2,1,0:T(8,128)(2,1)S(1)}, bf16[4,128,256]{2,1,0:T(8,128)(2,1)S(1)}, u32[]{:S(2)}, u32[]{:S(2)}) collective-permute-start(bf16[4,128,256]{2,1,0:T(8,128)(2,1)S(1)} %pad_maximum_fusion.1.refs_0_), channel_id=1, source_target_pairs={{0,16},{1,17},{2,18},{3,19},{4,20},{5,21},{6,22},{7,23},{8,24},{9,... | collective-permute-start | bytes 786440 | tf_op jit(solution)/shard_map/ppermute | solution.py:30
  36.8 5.2 %collective-permute-start.8 = (bf16[4,128,256]{2,1,0:T(8,128)(2,1)S(1)}, bf16[4,128,256]{2,1,0:T(8,128)(2,1)S(1)}, u32[]{:S(2)}, u32[]{:S(2)}) collective-permute-start(bf16[4,128,256]{2,1,0:T(8,128)(2,1)S(1)} %pad_maximum_fusion.1.refs_0_), channel_id=1, source_target_pairs={{0,2},{1,3},{2,16},{3,17},{4,6},{5,7},{6,20},{7,21},{8,10},{9,11},... | collective-permute-start | bytes 786440 | tf_op jit(solution)/shard_map/ppermute | solution.py:30
  42.0 0.6 copy-done.1
  42.8 0.1 reduce.1
  42.9 0.9 collective-permute-done.10.refs_3_
  43.9 1.9 %collective-permute-start.3 = (bf16[128,512]{1,0:T(8,128)(2,1)S(1)}, bf16[128,512]{1,0:T(8,128)(2,1)S(1)}, u32[]{:S(2)}, u32[]{:S(2)}) collective-permute-start(bf16[128,512]{1,0:T(8,128)(2,1)S(1)} %get-tuple-element.13), channel_id=1, source_target_pairs={{0,12},{1,0},{2,4},{3,8},{4,13},{5,1},{6,5},{7,9},{8,14},{9,2},{10... | collective-permute-start | bytes 393224 | tf_op jit(solution)/shard_map/ppermute | solution.py:30
  45.8 2.5 %collective-permute-start.2 = (bf16[128,512]{1,0:T(8,128)(2,1)S(1)}, bf16[128,512]{1,0:T(8,128)(2,1)S(1)}, u32[]{:S(2)}, u32[]{:S(2)}) collective-permute-start(bf16[128,512]{1,0:T(8,128)(2,1)S(1)} %get-tuple-element.14), channel_id=1, source_target_pairs={{0,8},{1,12},{2,0},{3,4},{4,9},{5,13},{6,1},{7,5},{8,10},{9,14},{1... | collective-permute-start | bytes 393224 | tf_op jit(solution)/shard_map/ppermute | solution.py:30
  48.4 4.3 %collective-permute-start.13 = (bf16[4,128,256]{2,1,0:T(8,128)(2,1)S(1)}, bf16[4,128,256]{2,1,0:T(8,128)(2,1)S(1)}, u32[]{:S(2)}, u32[]{:S(2)}) collective-permute-start(bf16[4,128,256]{2,1,0:T(8,128)(2,1)S(1)} %broadcast_select_fusion), channel_id=1, source_target_pairs={{0,1},{1,0},{2,3},{3,2},{4,5},{5,4},{6,7},{7,6},{8,9},{9,8},{10,11... | collective-permute-start | bytes 786440 | tf_op jit(solution)/shard_map/ppermute | solution.py:30
  52.7 2.6 %collective-permute-done.9.refs_2_ = bf16[4,128,256]{2,1,0:T(8,128)(2,1)S(1)} collective-permute-done((bf16[4,128,256]{2,1,0:T(8,128)(2,1)S(1)}, bf16[4,128,256]{2,1,0:T(8,128)(2,1)S(1)}, u32[]{:S(2)}, u32[]{:S(2)}) %collective-permute-start.9) | collective-permute-done | bytes 262176 | tf_op jit(solution)/shard_map/ppermute | solution.py:30
  55.2 2.4 %collective-permute-start.12 = (bf16[4,128,256]{2,1,0:T(8,128)(2,1)S(1)}, bf16[4,128,256]{2,1,0:T(8,128)(2,1)S(1)}, u32[]{:S(2)}, u32[]{:S(2)}) collective-permute-start(bf16[4,128,256]{2,1,0:T(8,128)(2,1)S(1)} %collective-permute-done.9.refs_2_), channel_id=1, source_target_pairs={{0,1},{1,0},{2,3},{3,2},{4,5},{5,4},{6,7},{7,6},{8,9},{9,8},{10,11... | collective-permute-start | bytes 786440 | tf_op jit(solution)/shard_map/ppermute | solution.py:30
  57.7 1.9 %collective-permute-start.11 = (bf16[4,128,256]{2,1,0:T(8,128)(2,1)S(1)}, bf16[4,128,256]{2,1,0:T(8,128)(2,1)S(1)}, u32[]{:S(2)}, u32[]{:S(2)}) collective-permute-start(bf16[4,128,256]{2,1,0:T(8,128)(2,1)S(1)} %collective-permute-done.8.refs_1_), channel_id=1, source_target_pairs={{0,1},{1,0},{2,3},{3,2},{4,5},{5,4},{6,7},{7,6},{8,9},{9,8},{10,11... | collective-permute-start | bytes 786440 | tf_op jit(solution)/shard_map/ppermute | solution.py:30
  59.6 0.7 select_reduce_fusion.1
  60.3 0.7 reduce_min.9
  61.0 1.3 %pad_add_fusion.info = s32[9]{0:T(128)S(1)} fusion(s32[1]{0:T(128)} %bitcast.6, s32[1]{0:T(128)} %bitcast.5, s32[7]{0:T(128)S(1)} %multiply_subtract_fusion), kind=kLoop, calls=%fused_computation.40 | loop fusion | flops 18 | bytes 72 | tf_op jit(solution)/shard_map/concatenate | solution.py:187
  62.5 0.1 broadcast_in_dim.24.low_ref
  62.6 0.1 broadcast_in_dim.23.place_ref
  62.7 5.1 %attend.1 = bf16[4,128,512]{2,1,0:T(8,128)(2,1)S(1)} custom-call(s32[9]{0:T(128)S(1)} %pad_add_fusion.info, s32[512,128]{1,0:T(8,128)S(1)} %broadcast_in_dim.23.place_ref, s32[512,128]{1,0:T(8,128)S(1)} %broadcast_in_dim.24.low_ref, s32[8,512]{1,0:T(8,128)S(1)} %broadcast_in_dim.25.column_ref, bf16[4,128,512]{2,1,0:T(8,128)(2,1)S(1)} %pad_maximum_fusion.q_ref, ...), custom_call_target="tpu_custom_call" | custom-call | flops 3000000000 | bytes 4000000 | tf_op jit(solution)/shard_map/attend/pallas_call | solution.py:128
  67.9 11.1 %collective-permute-start.14 = (bf16[128,512]{1,0:T(8,128)(2,1)S(1)}, bf16[128,512]{1,0:T(8,128)(2,1)S(1)}, u32[]{:S(2)}, u32[]{:S(2)}) collective-permute-start(bf16[128,512]{1,0:T(8,128)(2,1)S(1)} %get-tuple-element.10), channel_id=1, source_target_pairs={{0,0},{1,4},{2,8},{3,12},{4,1},{5,5},{6,9},{7,13},{8,2},{9,6},{10,... | collective-permute-start | bytes 393224 | tf_op jit(solution)/shard_map/ppermute | solution.py:30
  78.9 1.9 %collective-permute-start.15 = (bf16[128,512]{1,0:T(8,128)(2,1)S(1)}, bf16[128,512]{1,0:T(8,128)(2,1)S(1)}, u32[]{:S(2)}, u32[]{:S(2)}) collective-permute-start(bf16[128,512]{1,0:T(8,128)(2,1)S(1)} %get-tuple-element.9), channel_id=1, source_target_pairs={{0,3},{1,7},{2,11},{3,15},{4,0},{5,4},{6,8},{7,12},{8,1},{9,5},{10... | collective-permute-start | bytes 393224 | tf_op jit(solution)/shard_map/ppermute | solution.py:30
  80.9 2.0 %collective-permute-start.17 = (bf16[128,512]{1,0:T(8,128)(2,1)S(1)}, bf16[128,512]{1,0:T(8,128)(2,1)S(1)}, u32[]{:S(2)}, u32[]{:S(2)}) collective-permute-start(bf16[128,512]{1,0:T(8,128)(2,1)S(1)} %get-tuple-element.7), channel_id=1, source_target_pairs={{0,1},{1,5},{2,9},{3,13},{4,2},{5,6},{6,10},{7,14},{8,3},{9,7},{10... | collective-permute-start | bytes 393224 | tf_op jit(solution)/shard_map/ppermute | solution.py:30
  82.9 3.2 %collective-permute-start.16 = (bf16[128,512]{1,0:T(8,128)(2,1)S(1)}, bf16[128,512]{1,0:T(8,128)(2,1)S(1)}, u32[]{:S(2)}, u32[]{:S(2)}) collective-permute-start(bf16[128,512]{1,0:T(8,128)(2,1)S(1)} %get-tuple-element.8), channel_id=1, source_target_pairs={{0,2},{1,6},{2,10},{3,14},{4,3},{5,7},{6,11},{7,15},{8,0},{9,4},{1... | collective-permute-start | bytes 393224 | tf_op jit(solution)/shard_map/ppermute | solution.py:30
  86.2 3.6 %collective-permute-done.15 = bf16[128,512]{1,0:T(8,128)(2,1)S(1)} collective-permute-done((bf16[128,512]{1,0:T(8,128)(2,1)S(1)}, bf16[128,512]{1,0:T(8,128)(2,1)S(1)}, u32[]{:S(2)}, u32[]{:S(2)}) %collective-permute-start.15) | collective-permute-done | bytes 131104 | tf_op jit(solution)/shard_map/ppermute | solution.py:30
  89.7 7.2 %collective-permute-done.16 = bf16[128,512]{1,0:T(8,128)(2,1)S(1)} collective-permute-done((bf16[128,512]{1,0:T(8,128)(2,1)S(1)}, bf16[128,512]{1,0:T(8,128)(2,1)S(1)}, u32[]{:S(2)}, u32[]{:S(2)}) %collective-permute-start.16) | collective-permute-done | bytes 131104 | tf_op jit(solution)/shard_map/ppermute | solution.py:30
  97.0 0.8 constant_dynamic-slice_fusion
  (42 shorter events, 0.8 us)
Async XLA Ops:
  0.0 21.3 %copy-start = (bf16[128,2048]{1,0:T(8,128)(2,1)S(1)}, bf16[128,2048]{1,0:T(8,128)(2,1)}, u32[]{:S(2)}) copy-start(bf16[128,2048]{1,0:T(8,128)(2,1)} %param.4) | copy-start | bytes 1572868
  1.0 25.1 %collective-permute-start.6 = (bf16[128,256]{1,0:T(8,128)(2,1)S(1)}, bf16[128,256]{1,0:T(8,128)(2,1)S(1)}, u32[]{:S(2)}, u32[]{:S(2)}) collective-permute-start(bf16[128,256]{1,0:T(8,128)(2,1)S(1)} %pad_maximum_fusion.4), channel_id=1, source_target_pairs={{0,8},{1,12},{2,0},{3,4},{4,9},{5,13},{6,1},{7,5},{8,10},{9,14},{1... | collective-permute-start | bytes 196616 | tf_op jit(solution)/shard_map/ppermute | solution.py:30
  12.2 20.5 %collective-permute-start.7 = (bf16[128,256]{1,0:T(8,128)(2,1)S(1)}, bf16[128,256]{1,0:T(8,128)(2,1)S(1)}, u32[]{:S(2)}, u32[]{:S(2)}) collective-permute-start(bf16[128,256]{1,0:T(8,128)(2,1)S(1)} %pad_maximum_fusion.5), channel_id=1, source_target_pairs={{0,12},{1,0},{2,4},{3,8},{4,13},{5,1},{6,5},{7,9},{8,14},{9,2},{10... | collective-permute-start | bytes 196616 | tf_op jit(solution)/shard_map/ppermute | solution.py:30
  14.5 18.2 %collective-permute-start.5 = (bf16[128,256]{1,0:T(8,128)(2,1)S(1)}, bf16[128,256]{1,0:T(8,128)(2,1)S(1)}, u32[]{:S(2)}, u32[]{:S(2)}) collective-permute-start(bf16[128,256]{1,0:T(8,128)(2,1)S(1)} %pad_maximum_fusion.3), channel_id=1, source_target_pairs={{0,4},{1,8},{2,12},{3,0},{4,5},{5,9},{6,13},{7,1},{8,6},{9,10},{10... | collective-permute-start | bytes 196616 | tf_op jit(solution)/shard_map/ppermute | solution.py:30
  19.4 13.4 %collective-permute-start.4 = (bf16[128,256]{1,0:T(8,128)(2,1)S(1)}, bf16[128,256]{1,0:T(8,128)(2,1)S(1)}, u32[]{:S(2)}, u32[]{:S(2)}) collective-permute-start(bf16[128,256]{1,0:T(8,128)(2,1)S(1)} %pad_maximum_fusion.2), channel_id=1, source_target_pairs={{0,0},{1,4},{2,8},{3,12},{4,1},{5,5},{6,9},{7,13},{8,2},{9,6},{10,... | collective-permute-start | bytes 196616 | tf_op jit(solution)/shard_map/ppermute | solution.py:30
  21.4 24.4 %collective-permute-start = (bf16[128,512]{1,0:T(8,128)(2,1)S(1)}, bf16[128,512]{1,0:T(8,128)(2,1)S(1)}, u32[]{:S(2)}, u32[]{:S(2)}) collective-permute-start(bf16[128,512]{1,0:T(8,128)(2,1)S(1)} %get-tuple-element.11), channel_id=1, source_target_pairs={{0,0},{1,4},{2,8},{3,12},{4,1},{5,5},{6,9},{7,13},{8,2},{9,6},{10,... | collective-permute-start | bytes 393224 | tf_op jit(solution)/shard_map/ppermute | solution.py:30
  26.0 22.3 %collective-permute-start.1 = (bf16[128,512]{1,0:T(8,128)(2,1)S(1)}, bf16[128,512]{1,0:T(8,128)(2,1)S(1)}, u32[]{:S(2)}, u32[]{:S(2)}) collective-permute-start(bf16[128,512]{1,0:T(8,128)(2,1)S(1)} %get-tuple-element.12), channel_id=1, source_target_pairs={{0,4},{1,8},{2,12},{3,0},{4,5},{5,9},{6,13},{7,1},{8,6},{9,10},{10... | collective-permute-start | bytes 393224 | tf_op jit(solution)/shard_map/ppermute | solution.py:30
  32.8 11.1 %collective-permute-start.10 = (bf16[4,128,256]{2,1,0:T(8,128)(2,1)S(1)}, bf16[4,128,256]{2,1,0:T(8,128)(2,1)S(1)}, u32[]{:S(2)}, u32[]{:S(2)}) collective-permute-start(bf16[4,128,256]{2,1,0:T(8,128)(2,1)S(1)} %pad_maximum_fusion.1.refs_0_), channel_id=1, source_target_pairs={{0,18},{1,19},{2,32},{3,33},{4,22},{5,23},{6,36},{7,37},{8,26},{9,... | collective-permute-start | bytes 786440 | tf_op jit(solution)/shard_map/ppermute | solution.py:30
  34.9 20.4 %collective-permute-start.9 = (bf16[4,128,256]{2,1,0:T(8,128)(2,1)S(1)}, bf16[4,128,256]{2,1,0:T(8,128)(2,1)S(1)}, u32[]{:S(2)}, u32[]{:S(2)}) collective-permute-start(bf16[4,128,256]{2,1,0:T(8,128)(2,1)S(1)} %pad_maximum_fusion.1.refs_0_), channel_id=1, source_target_pairs={{0,16},{1,17},{2,18},{3,19},{4,20},{5,21},{6,22},{7,23},{8,24},{9,... | collective-permute-start | bytes 786440 | tf_op jit(solution)/shard_map/ppermute | solution.py:30
  36.8 20.9 %collective-permute-start.8 = (bf16[4,128,256]{2,1,0:T(8,128)(2,1)S(1)}, bf16[4,128,256]{2,1,0:T(8,128)(2,1)S(1)}, u32[]{:S(2)}, u32[]{:S(2)}) collective-permute-start(bf16[4,128,256]{2,1,0:T(8,128)(2,1)S(1)} %pad_maximum_fusion.1.refs_0_), channel_id=1, source_target_pairs={{0,2},{1,3},{2,16},{3,17},{4,6},{5,7},{6,20},{7,21},{8,10},{9,11},... | collective-permute-start | bytes 786440 | tf_op jit(solution)/shard_map/ppermute | solution.py:30
  42.0 0.7 copy-start.1
  43.9 18.5 %collective-permute-start.3 = (bf16[128,512]{1,0:T(8,128)(2,1)S(1)}, bf16[128,512]{1,0:T(8,128)(2,1)S(1)}, u32[]{:S(2)}, u32[]{:S(2)}) collective-permute-start(bf16[128,512]{1,0:T(8,128)(2,1)S(1)} %get-tuple-element.13), channel_id=1, source_target_pairs={{0,12},{1,0},{2,4},{3,8},{4,13},{5,1},{6,5},{7,9},{8,14},{9,2},{10... | collective-permute-start | bytes 393224 | tf_op jit(solution)/shard_map/ppermute | solution.py:30
  45.8 16.5 %collective-permute-start.2 = (bf16[128,512]{1,0:T(8,128)(2,1)S(1)}, bf16[128,512]{1,0:T(8,128)(2,1)S(1)}, u32[]{:S(2)}, u32[]{:S(2)}) collective-permute-start(bf16[128,512]{1,0:T(8,128)(2,1)S(1)} %get-tuple-element.14), channel_id=1, source_target_pairs={{0,8},{1,12},{2,0},{3,4},{4,9},{5,13},{6,1},{7,5},{8,10},{9,14},{1... | collective-permute-start | bytes 393224 | tf_op jit(solution)/shard_map/ppermute | solution.py:30
  48.4 14.0 %collective-permute-start.13 = (bf16[4,128,256]{2,1,0:T(8,128)(2,1)S(1)}, bf16[4,128,256]{2,1,0:T(8,128)(2,1)S(1)}, u32[]{:S(2)}, u32[]{:S(2)}) collective-permute-start(bf16[4,128,256]{2,1,0:T(8,128)(2,1)S(1)} %broadcast_select_fusion), channel_id=1, source_target_pairs={{0,1},{1,0},{2,3},{3,2},{4,5},{5,4},{6,7},{7,6},{8,9},{9,8},{10,11... | collective-permute-start | bytes 786440 | tf_op jit(solution)/shard_map/ppermute | solution.py:30
  55.2 7.2 %collective-permute-start.12 = (bf16[4,128,256]{2,1,0:T(8,128)(2,1)S(1)}, bf16[4,128,256]{2,1,0:T(8,128)(2,1)S(1)}, u32[]{:S(2)}, u32[]{:S(2)}) collective-permute-start(bf16[4,128,256]{2,1,0:T(8,128)(2,1)S(1)} %collective-permute-done.9.refs_2_), channel_id=1, source_target_pairs={{0,1},{1,0},{2,3},{3,2},{4,5},{5,4},{6,7},{7,6},{8,9},{9,8},{10,11... | collective-permute-start | bytes 786440 | tf_op jit(solution)/shard_map/ppermute | solution.py:30
  57.7 4.8 %collective-permute-start.11 = (bf16[4,128,256]{2,1,0:T(8,128)(2,1)S(1)}, bf16[4,128,256]{2,1,0:T(8,128)(2,1)S(1)}, u32[]{:S(2)}, u32[]{:S(2)}) collective-permute-start(bf16[4,128,256]{2,1,0:T(8,128)(2,1)S(1)} %collective-permute-done.8.refs_1_), channel_id=1, source_target_pairs={{0,1},{1,0},{2,3},{3,2},{4,5},{5,4},{6,7},{7,6},{8,9},{9,8},{10,11... | collective-permute-start | bytes 786440 | tf_op jit(solution)/shard_map/ppermute | solution.py:30
  67.9 18.3 %collective-permute-start.14 = (bf16[128,512]{1,0:T(8,128)(2,1)S(1)}, bf16[128,512]{1,0:T(8,128)(2,1)S(1)}, u32[]{:S(2)}, u32[]{:S(2)}) collective-permute-start(bf16[128,512]{1,0:T(8,128)(2,1)S(1)} %get-tuple-element.10), channel_id=1, source_target_pairs={{0,0},{1,4},{2,8},{3,12},{4,1},{5,5},{6,9},{7,13},{8,2},{9,6},{10,... | collective-permute-start | bytes 393224 | tf_op jit(solution)/shard_map/ppermute | solution.py:30
  78.9 10.8 %collective-permute-start.15 = (bf16[128,512]{1,0:T(8,128)(2,1)S(1)}, bf16[128,512]{1,0:T(8,128)(2,1)S(1)}, u32[]{:S(2)}, u32[]{:S(2)}) collective-permute-start(bf16[128,512]{1,0:T(8,128)(2,1)S(1)} %get-tuple-element.9), channel_id=1, source_target_pairs={{0,3},{1,7},{2,11},{3,15},{4,0},{5,4},{6,8},{7,12},{8,1},{9,5},{10... | collective-permute-start | bytes 393224 | tf_op jit(solution)/shard_map/ppermute | solution.py:30
  80.9 16.0 %collective-permute-start.17 = (bf16[128,512]{1,0:T(8,128)(2,1)S(1)}, bf16[128,512]{1,0:T(8,128)(2,1)S(1)}, u32[]{:S(2)}, u32[]{:S(2)}) collective-permute-start(bf16[128,512]{1,0:T(8,128)(2,1)S(1)} %get-tuple-element.7), channel_id=1, source_target_pairs={{0,1},{1,5},{2,9},{3,13},{4,2},{5,6},{6,10},{7,14},{8,3},{9,7},{10... | collective-permute-start | bytes 393224 | tf_op jit(solution)/shard_map/ppermute | solution.py:30
  82.9 14.0 %collective-permute-start.16 = (bf16[128,512]{1,0:T(8,128)(2,1)S(1)}, bf16[128,512]{1,0:T(8,128)(2,1)S(1)}, u32[]{:S(2)}, u32[]{:S(2)}) collective-permute-start(bf16[128,512]{1,0:T(8,128)(2,1)S(1)} %get-tuple-element.8), channel_id=1, source_target_pairs={{0,2},{1,6},{2,10},{3,14},{4,3},{5,7},{6,11},{7,15},{8,0},{9,4},{1... | collective-permute-start | bytes 393224 | tf_op jit(solution)/shard_map/ppermute | solution.py:30

commit v3 on v1

v3 whole, which is shorter than its diff:
```python
import functools
import math

import jax
import jax.numpy as jnp
from jax import lax
from jax.experimental import pallas as pl
from jax.experimental.pallas import tpu as pltpu
from jax.sharding import Mesh, PartitionSpec as P

QUERY_HEADS = 16
KEY_VALUE_HEADS = 4
HEAD_SIZE = 128
GROUP = QUERY_HEADS // KEY_VALUE_HEADS
ROWS = 128
PIECE = 4 * ROWS
WIDTH = GROUP * HEAD_SIZE
REACH = 6
EXPONENT_SCALE = math.log2(math.e) / math.sqrt(HEAD_SIZE)
MASKED = -1e30
ALL = ("docs", "sub", "chip", "core")
TEAM = ("chip", "core")


def shift(x, by, docs):
    count = docs * 16
    return lax.ppermute(x, ALL, [(i, (i + by * 4) % count) for i in range(count)])


def rearrange(kernel, shape, *operands):
    return pl.pallas_call(
        kernel,
        out_shape=jax.ShapeDtypeStruct(shape, jnp.bfloat16),
        in_specs=[pl.BlockSpec(memory_space=pltpu.VMEM)] * len(operands),
        out_specs=pl.BlockSpec(memory_space=pltpu.VMEM),
        name=kernel.__name__,
    )(*operands)


def pack_key_value(keys, values, out):
    for n in range(KEY_VALUE_HEADS):
        columns = slice(n * HEAD_SIZE, (n + 1) * HEAD_SIZE)
        out[n, :, 0:HEAD_SIZE] = keys[:, columns]
        out[n, :, HEAD_SIZE : 2 * HEAD_SIZE] = values[:, columns]


def pack_queries(queries, out):
    for n in range(KEY_VALUE_HEADS):
        out[n] = queries[:, n * WIDTH : (n + 1) * WIDTH]


def unpack(outcome, out):
    for n in range(KEY_VALUE_HEADS):
        out[:, n * WIDTH : (n + 1) * WIDTH] = outcome[n]


def attend_kernel(behind, first, last, info, low_ref, q_ref, *refs):
    refs = list(refs)
    pieces = [refs.pop(0) for _ in behind]
    state_in = [] if first else [refs.pop(0) for _ in range(3)]
    out_refs = [refs.pop(0) for _ in range(1 if last else 3)]
    kv, sems = refs[:2]
    top, total, acc = refs[2:] if last else out_refs
    copies = [
        pltpu.make_async_copy(piece, kv.at[n], sems.at[n]) for n, piece in enumerate(pieces)
    ]
    for copy in copies:
        copy.start()
    if first:
        top[...] = jnp.full_like(top, MASKED)
        total[...] = jnp.zeros_like(total)
        acc[...] = jnp.zeros_like(acc)
    else:
        for held, given in zip((top, total, acc), state_in):
            held[...] = given[...]
    for copy in copies:
        copy.wait()
    base, first_low, last_low = info[0], info[1], info[2]

    def update(n, start, masked):
        key_rows = kv[n, :, :, 0:HEAD_SIZE].reshape(PIECE, HEAD_SIZE)
        value_rows = kv[n, :, :, HEAD_SIZE : 2 * HEAD_SIZE].reshape(PIECE, HEAD_SIZE)

        def scores_of(head):
            query = q_ref[:, :, head * HEAD_SIZE : (head + 1) * HEAD_SIZE].reshape(PIECE, HEAD_SIZE)
            return lax.dot_general(
                query, key_rows, (((1,), (1,)), ((), ())), preferred_element_type=jnp.float32
            )

        if masked:
            key_place = start + lax.broadcasted_iota(jnp.int32, (PIECE, PIECE), 1)
            place = base + lax.broadcasted_iota(jnp.int32, (PIECE, PIECE), 0)
            low = jnp.concatenate([low_ref[...]] * (PIECE // 128), axis=1)
            visible = (key_place >= low) & (key_place <= place)
        ahead = scores_of(0)
        for head in range(GROUP):
            scores = ahead
            if head + 1 < GROUP:
                ahead = scores_of(head + 1)
            if masked:
                scores = jnp.where(visible, scores, MASKED)
            old = top[head]
            new = jnp.maximum(old, jnp.max(scores, axis=1, keepdims=True))
            wide = jnp.concatenate([new] * (PIECE // 128), axis=1)
            expo = jnp.exp2((scores - wide) * EXPONENT_SCALE)
            factor = jnp.exp2((old - new) * EXPONENT_SCALE)
            part = expo[:, 0:128]
            for k in range(1, PIECE // 128):
                part = part + expo[:, k * 128 : (k + 1) * 128]
            total[head] = total[head] * factor + part
            acc[head] = acc[head] * factor + jnp.dot(
                expo.astype(jnp.bfloat16), value_rows, preferred_element_type=jnp.float32
            )
            top[head] = new

    def one_piece(n, unused):
        back = n + behind[0]
        start = base - back * PIECE
        needed = start + PIECE > first_low
        whole = (back > 0) & (start >= last_low)

        @pl.when(needed & whole)
        def _():
            update(n, start, False)

        @pl.when(needed & jnp.logical_not(whole))
        def _():
            update(n, start, True)

        return unused

    lax.fori_loop(0, len(behind), one_piece, 0)
    if last:
        for head in range(GROUP):
            denominator = jnp.sum(total[head], axis=1, keepdims=True)
            out_refs[0][:, :, head * HEAD_SIZE : (head + 1) * HEAD_SIZE] = (
                (acc[head] / denominator).astype(jnp.bfloat16).reshape(4, ROWS, HEAD_SIZE)
            )


def attend(info, low, queries, pieces, behind, state, last):
    vmem = pl.BlockSpec(memory_space=pltpu.VMEM)
    part = (GROUP, PIECE, 128)
    held = [jax.ShapeDtypeStruct(part, jnp.float32)] * 3
    done = [jax.ShapeDtypeStruct((4, ROWS, WIDTH), jnp.bfloat16)]
    share = len(behind) / (REACH + 1)
    return pl.pallas_call(
        functools.partial(attend_kernel, behind, not state, last),
        out_shape=done if last else held,
        in_specs=[pl.BlockSpec(memory_space=pltpu.SMEM), vmem, vmem]
        + [pl.BlockSpec(memory_space=pl.ANY)] * len(pieces)
        + [vmem] * len(state),
        out_specs=[vmem] * (1 if last else 3),
        scratch_shapes=[
            pltpu.VMEM((len(behind), 4, ROWS, 2 * HEAD_SIZE), jnp.bfloat16),
            pltpu.SemaphoreType.DMA((len(behind),)),
        ]
        + ([pltpu.VMEM(part, jnp.float32)] * 3 if last else []),
        compiler_params=pltpu.CompilerParams(vmem_limit_bytes=40 * 1024 * 1024),
        cost_estimate=pl.CostEstimate(
            flops=int(3e9 * share), bytes_accessed=4_000_000, transcendentals=int(6e6 * share)
        ),
        name="attend",
    )(info, low, queries, *pieces, *state)


def per_device(queries, keys, values, lengths):
    docs = lax.axis_size("docs")
    base = (lax.axis_index("docs") * 4 + lax.axis_index("sub")) * PIECE
    bounds = jnp.cumsum(lengths)
    place = base + jnp.arange(PIECE, dtype=jnp.int32)
    low = jnp.max(jnp.where(bounds[None, :] <= place[:, None], bounds[None, :], 0), axis=1)
    info = jnp.stack([base, low[0], low[-1]]).astype(jnp.int32)
    low = jnp.broadcast_to(low[:, None], (PIECE, 128))

    key_value = rearrange(pack_key_value, (4, ROWS, 2 * HEAD_SIZE), keys, values)
    own = lax.all_to_all(key_value, TEAM, 0, 0, tiled=True)
    info, low, own = lax.optimization_barrier((info, low, own))
    query_team = rearrange(pack_queries, (4, ROWS, WIDTH), queries)
    query_team = lax.all_to_all(query_team, TEAM, 0, 0, tiled=True)
    back1 = shift(own, 1, docs)
    back3 = shift(own, 3, docs)
    back2 = shift(own, 2, docs)
    back4 = shift(own, 4, docs)
    back5 = shift(back1, 4, docs)
    back6 = shift(back2, 4, docs)
    state = attend(info, low, query_team, (own, back1, back2, back3, back4), range(0, 5), (), False)
    (outcome,) = attend(info, low, query_team, (back5, back6), range(5, 7), state, True)
    outcome = lax.all_to_all(outcome, TEAM, 0, 0, tiled=True)
    return rearrange(unpack, (ROWS, QUERY_HEADS * HEAD_SIZE), outcome)


def solution(mesh):
    docs = mesh.shape["docs"]
    fine = Mesh(mesh.devices.reshape(docs, 4, 2, 2), ALL)
    rows = P(ALL, None)
    return jax.shard_map(
        per_device,
        mesh=fine,
        in_specs=(rows, rows, rows, P()),
        out_specs=rows,
        check_vma=False,
    )
```

time: 114 us -> 91.3 us (0.80)
  the two profiles are of different devices: /device:TPU:62 before, /device:TPU:432 now
where the time goes in v3:
time: 91.3 us; the launch traced here: 90.8 us
  waiting for transfers between devices  31 us (34%)
  starting transfers between devices  27.8 us (30%)
  Pallas kernels  16.8 us (18%)
  blocking collectives  11.9 us (13%)
  other arithmetic  1.59 us (2%)
  local copies, waits for them, and re-layouts  1.52 us (2%)
    ppermute x6, waiting for transfers between devices, shift(): lax.ppermute(x, ALL, [(i, (i + by * 4) % count) for i in range(count)])  26.9 us
    ppermute x6, starting transfers between devices, shift(): lax.ppermute(x, ALL, [(i, (i + by * 4) % count) for i in range(count)])  21 us
    all_to_all x1, blocking collectives, per_device(): outcome = lax.all_to_all(outcome, TEAM, 0, 0, tiled=True)  11.9 us
    pallas_call x2, Pallas kernels, attend(): pl.pallas_call(functools.partial(attend_kernel, behind, not state, last),...  11.3 us
    pallas_call x3, Pallas kernels, rearrange(): pl.pallas_call(kernel, out_shape=jax.ShapeDtypeStruct(shape, jnp.bfloat16...  5.44 us
    all_to_all x1, waiting for transfers between devices, per_device(): own = lax.all_to_all(key_value, TEAM, 0, 0, tiled=True)  4.13 us
    all_to_all x1, starting transfers between devices, per_device(): query_team = lax.all_to_all(query_team, TEAM, 0, 0, tiled=True)  3.47 us
    all_to_all x1, starting transfers between devices, per_device(): own = lax.all_to_all(key_value, TEAM, 0, 0, tiled=True)  3.4 us
  transfers between devices with their start and end apart: 8, of which 6 were waited for; matrix products, arithmetic and copies ran while one was open for 3% of the time, Pallas kernels for 13%

profile of v3, /device:TPU:432, one launch (start us, length us, event | category | flops | bytes accessed | tf_op | source)
XLA Modules:
  0.0 90.8 jit_solution(711135506434218096)
XLA Ops:
  0.0 1.7 %pack_key_value.1 = bf16[4,128,256]{2,1,0:T(8,128)(2,1)} custom-call(bf16[128,512]{1,0:T(8,128)(2,1)} %keys.1, bf16[128,512]{1,0:T(8,128)(2,1)} %values.1), custom_call_target="tpu_custom_call" | custom-call | tf_op jit(solution)/shard_map/pack_key_value/pallas_call | solution.py:31
  1.7 3.4 %all-to-all-start = ((bf16[4,128,256]{2,1,0:T(8,128)(2,1)}), bf16[4,128,256]{2,1,0:T(8,128)(2,1)S(1)}, u32[]{:S(2)}, u32[]{:S(2)}) async-start(bf16[4,128,256]{2,1,0:T(8,128)(2,1)} %pack_key_value.1), calls=%async_computation | async-start | bytes 524288 | tf_op jit(solution)/shard_map/all_to_all | solution.py:177
  5.1 1.9 %pack_queries.1 = bf16[4,128,512]{2,1,0:T(8,128)(2,1)} custom-call(bf16[128,2048]{1,0:T(8,128)(2,1)} %queries.1), custom_call_target="tpu_custom_call" | custom-call | tf_op jit(solution)/shard_map/pack_queries/pallas_call | solution.py:31
  7.0 4.1 %all-to-all-done.refs_0_ = bf16[4,128,256]{2,1,0:T(8,128)(2,1)S(1)} async-done(((bf16[4,128,256]{2,1,0:T(8,128)(2,1)}), bf16[4,128,256]{2,1,0:T(8,128)(2,1)S(1)}, u32[]{:S(2)}, u32[]{:S(2)}) %all-to-all-start) | async-done | bytes 262176 | tf_op jit(solution)/shard_map/all_to_all | solution.py:177
  11.1 3.5 %all-to-all-start.1 = ((bf16[4,128,512]{2,1,0:T(8,128)(2,1)}), bf16[4,128,512]{2,1,0:T(8,128)(2,1)S(1)}, u32[]{:S(2)}, u32[]{:S(2)}) async-start(bf16[4,128,512]{2,1,0:T(8,128)(2,1)} %pack_queries.1), calls=%async_computation.1 | async-start | bytes 1048576 | tf_op jit(solution)/shard_map/all_to_all | solution.py:180
  14.6 0.0 copy-start
  14.6 0.6 copy-done
  15.3 0.1 copy.7
  15.4 0.1 reduce-window.8
  15.4 0.1 reduce
  15.5 0.1 select_reduce_fusion
  15.6 0.7 fusion
  16.3 1.3 %pad_add_fusion.info = s32[3]{0:T(128)S(1)} fusion(s32[1]{0:T(128)} %get-tuple-element.18, s32[1]{0:T(128)} %get-tuple-element.17, s32[1]{0:T(128)} %bitcast), kind=kLoop, calls=%fused_computation.2 | loop fusion | flops 6 | bytes 24 | tf_op jit(solution)/shard_map/stack | solution.py:173
  17.6 0.1 broadcast_in_dim.13.low_ref
  17.7 1.9 %collective-permute-start = (bf16[4,128,256]{2,1,0:T(8,128)(2,1)S(1)}, bf16[4,128,256]{2,1,0:T(8,128)(2,1)S(1)}, u32[]{:S(2)}, u32[]{:S(2)}) collective-permute-start(bf16[4,128,256]{2,1,0:T(8,128)(2,1)S(1)} %all-to-all-done.refs_0_), channel_id=1, source_target_pairs={{0,4},{1,5},{2,6},{3,7},{4,8},{5,9},{6,10},{7,11},{8,12},{9,13},{1... | collective-permute-start | bytes 786440 | tf_op jit(solution)/shard_map/ppermute | solution.py:27
  19.7 6.9 %collective-permute-start.2 = (bf16[4,128,256]{2,1,0:T(8,128)(2,1)S(1)}, bf16[4,128,256]{2,1,0:T(8,128)(2,1)S(1)}, u32[]{:S(2)}, u32[]{:S(2)}) collective-permute-start(bf16[4,128,256]{2,1,0:T(8,128)(2,1)S(1)} %all-to-all-done.refs_0_), channel_id=1, source_target_pairs={{0,8},{1,9},{2,10},{3,11},{4,12},{5,13},{6,14},{7,15},{8,16},{9,17... | collective-permute-start | bytes 786440 | tf_op jit(solution)/shard_map/ppermute | solution.py:27
  26.6 1.9 %collective-permute-start.4 = (bf16[4,128,256]{2,1,0:T(8,128)(2,1)S(1)}, bf16[4,128,256]{2,1,0:T(8,128)(2,1)S(1)}, u32[]{:S(2)}, u32[]{:S(2)}) collective-permute-start(bf16[4,128,256]{2,1,0:T(8,128)(2,1)S(1)} %all-to-all-done.refs_0_), channel_id=1, source_target_pairs={{0,12},{1,13},{2,14},{3,15},{4,16},{5,17},{6,18},{7,19},{8,20},{9,... | collective-permute-start | bytes 786440 | tf_op jit(solution)/shard_map/ppermute | solution.py:27
  28.6 3.4 %collective-permute-start.5 = (bf16[4,128,256]{2,1,0:T(8,128)(2,1)S(1)}, bf16[4,128,256]{2,1,0:T(8,128)(2,1)S(1)}, u32[]{:S(2)}, u32[]{:S(2)}) collective-permute-start(bf16[4,128,256]{2,1,0:T(8,128)(2,1)S(1)} %all-to-all-done.refs_0_), channel_id=1, source_target_pairs={{0,16},{1,17},{2,18},{3,19},{4,20},{5,21},{6,22},{7,23},{8,24},{9,... | collective-permute-start | bytes 786440 | tf_op jit(solution)/shard_map/ppermute | solution.py:27
  32.0 1.3 %collective-permute-done.refs_1_ = bf16[4,128,256]{2,1,0:T(8,128)(2,1)S(1)} collective-permute-done((bf16[4,128,256]{2,1,0:T(8,128)(2,1)S(1)}, bf16[4,128,256]{2,1,0:T(8,128)(2,1)S(1)}, u32[]{:S(2)}, u32[]{:S(2)}) %collective-permute-start) | collective-permute-done | bytes 262176 | tf_op jit(solution)/shard_map/ppermute | solution.py:27
  33.3 3.4 %collective-permute-start.1 = (bf16[4,128,256]{2,1,0:T(8,128)(2,1)S(1)}, bf16[4,128,256]{2,1,0:T(8,128)(2,1)S(1)}, u32[]{:S(2)}, u32[]{:S(2)}) collective-permute-start(bf16[4,128,256]{2,1,0:T(8,128)(2,1)S(1)} %collective-permute-done.refs_1_), channel_id=1, source_target_pairs={{0,16},{1,17},{2,18},{3,19},{4,20},{5,21},{6,22},{7,23},{8,24},{9,... | collective-permute-start | bytes 786440 | tf_op jit(solution)/shard_map/ppermute | solution.py:27
  36.7 10.5 %collective-permute-done.2.refs_2_ = bf16[4,128,256]{2,1,0:T(8,128)(2,1)S(1)} collective-permute-done((bf16[4,128,256]{2,1,0:T(8,128)(2,1)S(1)}, bf16[4,128,256]{2,1,0:T(8,128)(2,1)S(1)}, u32[]{:S(2)}, u32[]{:S(2)}) %collective-permute-start.2) | collective-permute-done | bytes 262176 | tf_op jit(solution)/shard_map/ppermute | solution.py:27
  47.2 3.4 %collective-permute-start.3 = (bf16[4,128,256]{2,1,0:T(8,128)(2,1)S(1)}, bf16[4,128,256]{2,1,0:T(8,128)(2,1)S(1)}, u32[]{:S(2)}, u32[]{:S(2)}) collective-permute-start(bf16[4,128,256]{2,1,0:T(8,128)(2,1)S(1)} %collective-permute-done.2.refs_2_), channel_id=1, source_target_pairs={{0,16},{1,17},{2,18},{3,19},{4,20},{5,21},{6,22},{7,23},{8,24},{9,... | collective-permute-start | bytes 786440 | tf_op jit(solution)/shard_map/ppermute | solution.py:27
  50.6 1.8 %collective-permute-done.4.refs_3_ = bf16[4,128,256]{2,1,0:T(8,128)(2,1)S(1)} collective-permute-done((bf16[4,128,256]{2,1,0:T(8,128)(2,1)S(1)}, bf16[4,128,256]{2,1,0:T(8,128)(2,1)S(1)}, u32[]{:S(2)}, u32[]{:S(2)}) %collective-permute-start.4) | collective-permute-done | bytes 262176 | tf_op jit(solution)/shard_map/ppermute | solution.py:27
  52.4 12.4 %collective-permute-done.5.refs_4_ = bf16[4,128,256]{2,1,0:T(8,128)(2,1)S(1)} collective-permute-done((bf16[4,128,256]{2,1,0:T(8,128)(2,1)S(1)}, bf16[4,128,256]{2,1,0:T(8,128)(2,1)S(1)}, u32[]{:S(2)}, u32[]{:S(2)}) %collective-permute-start.5) | collective-permute-done | bytes 262176 | tf_op jit(solution)/shard_map/ppermute | solution.py:27
  64.8 0.0 all-to-all-done.1.q_ref
  64.8 10.1 %attend.2 = (f32[4,512,128]{2,1,0:T(8,128)S(1)}, f32[4,512,128]{2,1,0:T(8,128)S(1)}, f32[4,512,128]{2,1,0:T(8,128)S(1)}) custom-call(s32[3]{0:T(128)S(1)} %pad_add_fusion.info, s32[512,128]{1,0:T(8,128)S(1)} %broadcast_in_dim.13.low_ref, bf16[4,128,512]{2,1,0:T(8,128)(2,1)S(1)} %all-to-all-done.1.q_ref, bf16[4,128,256]{2,1,0:T(8,128)(2,1)S(1)} %all-to-all-done.refs_0_, ...), custom_call_target="tpu_custom_call" | custom-call | flops 2142857088 | bytes 4000000 | tf_op jit(solution)/shard_map/attend/pallas_call | solution.py:147
  74.9 0.0 collective-permute-done.1.refs_0_
  74.9 0.9 collective-permute-done.3.refs_1_
  75.8 1.2 %attend.3 = bf16[4,128,512]{2,1,0:T(8,128)(2,1)S(1)} custom-call(s32[3]{0:T(128)S(1)} %pad_add_fusion.info, s32[512,128]{1,0:T(8,128)S(1)} %broadcast_in_dim.13.low_ref, bf16[4,128,512]{2,1,0:T(8,128)(2,1)S(1)} %all-to-all-done.1.q_ref, bf16[4,128,256]{2,1,0:T(8,128)(2,1)S(1)} %collective-permute-done.1.refs_0_, ...), custom_call_target="tpu_custom_call" | custom-call | flops 857142848 | bytes 4000000 | tf_op jit(solution)/shard_map/attend/pallas_call | solution.py:147
  77.0 11.9 %all_to_all.15.outcome = bf16[4,128,512]{2,1,0:T(8,128)(2,1)} all-to-all(bf16[4,128,512]{2,1,0:T(8,128)(2,1)S(1)} %attend.3), channel_id=1, replica_groups=mesh['docs'=32,'sub'=4,'chip'=2,'core'=2] {'chip','core'}, dimensions={0} | all-to-all | bytes 1048576 | tf_op jit(solution)/shard_map/all_to_all | solution.py:189
  88.9 1.9 %unpack.1 = bf16[128,2048]{1,0:T(8,128)(2,1)} custom-call(bf16[4,128,512]{2,1,0:T(8,128)(2,1)} %all_to_all.15.outcome), custom_call_target="tpu_custom_call" | custom-call | tf_op jit(solution)/shard_map/unpack/pallas_call | solution.py:31
  (1 shorter events, 0.0 us)
Async XLA Ops:
  1.7 9.4 %all-to-all-start = ((bf16[4,128,256]{2,1,0:T(8,128)(2,1)}), bf16[4,128,256]{2,1,0:T(8,128)(2,1)S(1)}, u32[]{:S(2)}, u32[]{:S(2)}) async-start(bf16[4,128,256]{2,1,0:T(8,128)(2,1)} %pack_key_value.1), calls=%async_computation | async-start | bytes 524288 | tf_op jit(solution)/shard_map/all_to_all | solution.py:177
  11.1 53.7 %all-to-all-start.1 = ((bf16[4,128,512]{2,1,0:T(8,128)(2,1)}), bf16[4,128,512]{2,1,0:T(8,128)(2,1)S(1)}, u32[]{:S(2)}, u32[]{:S(2)}) async-start(bf16[4,128,512]{2,1,0:T(8,128)(2,1)} %pack_queries.1), calls=%async_computation.1 | async-start | bytes 1048576 | tf_op jit(solution)/shard_map/all_to_all | solution.py:180
  14.6 0.7 copy-start
  17.7 15.5 %collective-permute-start = (bf16[4,128,256]{2,1,0:T(8,128)(2,1)S(1)}, bf16[4,128,256]{2,1,0:T(8,128)(2,1)S(1)}, u32[]{:S(2)}, u32[]{:S(2)}) collective-permute-start(bf16[4,128,256]{2,1,0:T(8,128)(2,1)S(1)} %all-to-all-done.refs_0_), channel_id=1, source_target_pairs={{0,4},{1,5},{2,6},{3,7},{4,8},{5,9},{6,10},{7,11},{8,12},{9,13},{1... | collective-permute-start | bytes 786440 | tf_op jit(solution)/shard_map/ppermute | solution.py:27
  19.7 27.5 %collective-permute-start.2 = (bf16[4,128,256]{2,1,0:T(8,128)(2,1)S(1)}, bf16[4,128,256]{2,1,0:T(8,128)(2,1)S(1)}, u32[]{:S(2)}, u32[]{:S(2)}) collective-permute-start(bf16[4,128,256]{2,1,0:T(8,128)(2,1)S(1)} %all-to-all-done.refs_0_), channel_id=1, source_target_pairs={{0,8},{1,9},{2,10},{3,11},{4,12},{5,13},{6,14},{7,15},{8,16},{9,17... | collective-permute-start | bytes 786440 | tf_op jit(solution)/shard_map/ppermute | solution.py:27
  26.6 25.7 %collective-permute-start.4 = (bf16[4,128,256]{2,1,0:T(8,128)(2,1)S(1)}, bf16[4,128,256]{2,1,0:T(8,128)(2,1)S(1)}, u32[]{:S(2)}, u32[]{:S(2)}) collective-permute-start(bf16[4,128,256]{2,1,0:T(8,128)(2,1)S(1)} %all-to-all-done.refs_0_), channel_id=1, source_target_pairs={{0,12},{1,13},{2,14},{3,15},{4,16},{5,17},{6,18},{7,19},{8,20},{9,... | collective-permute-start | bytes 786440 | tf_op jit(solution)/shard_map/ppermute | solution.py:27
  28.6 36.2 %collective-permute-start.5 = (bf16[4,128,256]{2,1,0:T(8,128)(2,1)S(1)}, bf16[4,128,256]{2,1,0:T(8,128)(2,1)S(1)}, u32[]{:S(2)}, u32[]{:S(2)}) collective-permute-start(bf16[4,128,256]{2,1,0:T(8,128)(2,1)S(1)} %all-to-all-done.refs_0_), channel_id=1, source_target_pairs={{0,16},{1,17},{2,18},{3,19},{4,20},{5,21},{6,22},{7,23},{8,24},{9,... | collective-permute-start | bytes 786440 | tf_op jit(solution)/shard_map/ppermute | solution.py:27
  33.3 41.6 %collective-permute-start.1 = (bf16[4,128,256]{2,1,0:T(8,128)(2,1)S(1)}, bf16[4,128,256]{2,1,0:T(8,128)(2,1)S(1)}, u32[]{:S(2)}, u32[]{:S(2)}) collective-permute-start(bf16[4,128,256]{2,1,0:T(8,128)(2,1)S(1)} %collective-permute-done.refs_1_), channel_id=1, source_target_pairs={{0,16},{1,17},{2,18},{3,19},{4,20},{5,21},{6,22},{7,23},{8,24},{9,... | collective-permute-start | bytes 786440 | tf_op jit(solution)/shard_map/ppermute | solution.py:27
  47.2 28.6 %collective-permute-start.3 = (bf16[4,128,256]{2,1,0:T(8,128)(2,1)S(1)}, bf16[4,128,256]{2,1,0:T(8,128)(2,1)S(1)}, u32[]{:S(2)}, u32[]{:S(2)}) collective-permute-start(bf16[4,128,256]{2,1,0:T(8,128)(2,1)S(1)} %collective-permute-done.2.refs_2_), channel_id=1, source_target_pairs={{0,16},{1,17},{2,18},{3,19},{4,20},{5,21},{6,22},{7,23},{8,24},{9,... | collective-permute-start | bytes 786440 | tf_op jit(solution)/shard_map/ppermute | solution.py:27

commit v4 on v3

--- a/solution.py
+++ b/solution.py
@@ -22,45 +22,33 @@
 TEAM = ("chip", "core")
 
 
+def columns(x, index, width):
+    return x[:, index * width : (index + 1) * width]
+
+
 def shift(x, by, docs):
     count = docs * 16
-    return lax.ppermute(x, ALL, [(i, (i + by * 4) % count) for i in range(count)])
-
-
-def rearrange(kernel, shape, *operands):
-    return pl.pallas_call(
-        kernel,
-        out_shape=jax.ShapeDtypeStruct(shape, jnp.bfloat16),
-        in_specs=[pl.BlockSpec(memory_space=pltpu.VMEM)] * len(operands),
-        out_specs=pl.BlockSpec(memory_space=pltpu.VMEM),
-        name=kernel.__name__,
-    )(*operands)
-
-
-def pack_key_value(keys, values, out):
-    for n in range(KEY_VALUE_HEADS):
-        columns = slice(n * HEAD_SIZE, (n + 1) * HEAD_SIZE)
-        out[n, :, 0:HEAD_SIZE] = keys[:, columns]
-        out[n, :, HEAD_SIZE : 2 * HEAD_SIZE] = values[:, columns]
-
-
-def pack_queries(queries, out):
-    for n in range(KEY_VALUE_HEADS):
-        out[n] = queries[:, n * WIDTH : (n + 1) * WIDTH]
-
-
-def unpack(outcome, out):
-    for n in range(KEY_VALUE_HEADS):
-        out[:, n * WIDTH : (n + 1) * WIDTH] = outcome[n]
+    return lax.ppermute(x, ALL, [(i, i + by * 4) for i in range(count - by * 4)])
+
+
+def turn_back(x, docs):
+    pairs = [
+        (doc * 16 + sub * 4 + n, doc * 16 + (sub + 3) % 4 * 4 + n)
+        for doc in range(docs)
+        for sub in range(4)
+        for n in range(4)
+    ]
+    return lax.ppermute(x, ALL, pairs)
 
 
 def attend_kernel(behind, first, last, info, low_ref, q_ref, *refs):
     refs = list(refs)
     pieces = [refs.pop(0) for _ in behind]
-    state_in = [] if first else [refs.pop(0) for _ in range(3)]
-    out_refs = [refs.pop(0) for _ in range(1 if last else 3)]
-    kv, sems = refs[:2]
-    top, total, acc = refs[2:] if last else out_refs
+    if not first:
+        del refs[:3]
+    top, total, acc = [refs.pop(0) for _ in range(3)]
+    out_ref = refs.pop(0) if last else None
+    kv, sems = refs
     copies = [
         pltpu.make_async_copy(piece, kv.at[n], sems.at[n]) for n, piece in enumerate(pieces)
     ]
@@ -70,9 +58,6 @@
         top[...] = jnp.full_like(top, MASKED)
         total[...] = jnp.zeros_like(total)
         acc[...] = jnp.zeros_like(acc)
-    else:
-        for held, given in zip((top, total, acc), state_in):
-            held[...] = given[...]
     for copy in copies:
         copy.wait()
     base, first_low, last_low = info[0], info[1], info[2]
@@ -114,7 +99,9 @@
             top[head] = new
 
     def one_piece(n, unused):
-        back = n + behind[0]
+        back = behind[0]
+        for k in range(1, len(behind)):
+            back = jnp.where(n == k, behind[k], back)
         start = base - back * PIECE
         needed = start + PIECE > first_low
         whole = (back > 0) & (start >= last_low)
@@ -133,32 +120,32 @@
     if last:
         for head in range(GROUP):
             denominator = jnp.sum(total[head], axis=1, keepdims=True)
-            out_refs[0][:, :, head * HEAD_SIZE : (head + 1) * HEAD_SIZE] = (
+            out_ref[:, :, head * HEAD_SIZE : (head + 1) * HEAD_SIZE] = (
                 (acc[head] / denominator).astype(jnp.bfloat16).reshape(4, ROWS, HEAD_SIZE)
             )
 
 
 def attend(info, low, queries, pieces, behind, state, last):
     vmem = pl.BlockSpec(memory_space=pltpu.VMEM)
-    part = (GROUP, PIECE, 128)
-    held = [jax.ShapeDtypeStruct(part, jnp.float32)] * 3
-    done = [jax.ShapeDtypeStruct((4, ROWS, WIDTH), jnp.bfloat16)]
+    held = [jax.ShapeDtypeStruct((GROUP, PIECE, 128), jnp.float32)] * 3
+    done = [jax.ShapeDtypeStruct((4, ROWS, WIDTH), jnp.bfloat16)] if last else []
     share = len(behind) / (REACH + 1)
+    given = 3 + len(pieces)
     return pl.pallas_call(
         functools.partial(attend_kernel, behind, not state, last),
-        out_shape=done if last else held,
+        out_shape=held + done,
         in_specs=[pl.BlockSpec(memory_space=pltpu.SMEM), vmem, vmem]
         + [pl.BlockSpec(memory_space=pl.ANY)] * len(pieces)
         + [vmem] * len(state),
-        out_specs=[vmem] * (1 if last else 3),
+        out_specs=[vmem] * len(held + done),
         scratch_shapes=[
             pltpu.VMEM((len(behind), 4, ROWS, 2 * HEAD_SIZE), jnp.bfloat16),
             pltpu.SemaphoreType.DMA((len(behind),)),
-        ]
-        + ([pltpu.VMEM(part, jnp.float32)] * 3 if last else []),
+        ],
+        input_output_aliases={given + n: n for n in range(len(state))},
         compiler_params=pltpu.CompilerParams(vmem_limit_bytes=40 * 1024 * 1024),
         cost_estimate=pl.CostEstimate(
-            flops=int(3e9 * share), bytes_accessed=4_000_000, transcendentals=int(6e6 * share)
+            flops=int(12e9 * share), bytes_accessed=4_000_000, transcendentals=int(6e6 * share)
         ),
         name="attend",
     )(info, low, queries, *pieces, *state)
@@ -173,21 +160,31 @@
     info = jnp.stack([base, low[0], low[-1]]).astype(jnp.int32)
     low = jnp.broadcast_to(low[:, None], (PIECE, 128))
 
-    key_value = rearrange(pack_key_value, (4, ROWS, 2 * HEAD_SIZE), keys, values)
+    key_value = jnp.stack(
+        [
+            jnp.concatenate([columns(keys, n, HEAD_SIZE), columns(values, n, HEAD_SIZE)], axis=1)
+            for n in range(KEY_VALUE_HEADS)
+        ]
+    )
     own = lax.all_to_all(key_value, TEAM, 0, 0, tiled=True)
     info, low, own = lax.optimization_barrier((info, low, own))
-    query_team = rearrange(pack_queries, (4, ROWS, WIDTH), queries)
-    query_team = lax.all_to_all(query_team, TEAM, 0, 0, tiled=True)
+    sub = lax.axis_index("sub")
     back1 = shift(own, 1, docs)
-    back3 = shift(own, 3, docs)
     back2 = shift(own, 2, docs)
     back4 = shift(own, 4, docs)
+    query_team = jnp.stack([columns(queries, n, WIDTH) for n in range(KEY_VALUE_HEADS)])
+    query_team = lax.all_to_all(query_team, TEAM, 0, 0, tiled=True)
+    back3 = turn_back(jnp.where(sub == 0, own, back4), docs)
+    state = attend(info, low, query_team, (own, back4), (0, 4), (), False)
+    back2, *state = lax.optimization_barrier((back2, *state))
+    back6 = shift(back2, 4, docs)
+    state = attend(info, low, query_team, (back2, back3), (2, 3), state, False)
+    back1, *state = lax.optimization_barrier((back1, *state))
     back5 = shift(back1, 4, docs)
-    back6 = shift(back2, 4, docs)
-    state = attend(info, low, query_team, (own, back1, back2, back3, back4), range(0, 5), (), False)
-    (outcome,) = attend(info, low, query_team, (back5, back6), range(5, 7), state, True)
+    state = attend(info, low, query_team, (back1,), (1,), state, False)
+    outcome = attend(info, low, query_team, (back5, back6), (5, 6), state, True)[3]
     outcome = lax.all_to_all(outcome, TEAM, 0, 0, tiled=True)
-    return rearrange(unpack, (ROWS, QUERY_HEADS * HEAD_SIZE), outcome)
+    return jnp.concatenate([outcome[n] for n in range(KEY_VALUE_HEADS)], axis=1)
 
 
 def solution(mesh):

time: 91.3 us -> 89.2 us (0.977)
  the two profiles are of different devices: /device:TPU:432 before, /device:TPU:32 now
where the time goes in v4:
time: 89.2 us; the launch traced here: 88.7 us
  starting transfers between devices  35.9 us (40%)
  waiting for transfers between devices  25.9 us (29%)
  blocking collectives  11.2 us (13%)
  Pallas kernels  8.87 us (10%)
  other arithmetic  4.11 us (5%)
  local copies, waits for them, and re-layouts  2.54 us (3%)
    ppermute x5, starting transfers between devices, shift(): lax.ppermute(x, ALL, [(i, i + by * 4) for i in range(count - by * 4)])  22.2 us
    ppermute x5, waiting for transfers between devices, shift(): lax.ppermute(x, ALL, [(i, i + by * 4) for i in range(count - by * 4)])  20 us
    all_to_all x1, blocking collectives, per_device(): outcome = lax.all_to_all(outcome, TEAM, 0, 0, tiled=True)  11.2 us
    pallas_call x4, Pallas kernels, attend(): pl.pallas_call(functools.partial(attend_kernel, behind, not state, last),...  8.87 us
    ppermute x1, starting transfers between devices, turn_back(): return lax.ppermute(x, ALL, pairs)  6.61 us
    all_to_all x1, waiting for transfers between devices, per_device(): own = lax.all_to_all(key_value, TEAM, 0, 0, tiled=True)  4.21 us
    all_to_all x1, starting transfers between devices, per_device(): own = lax.all_to_all(key_value, TEAM, 0, 0, tiled=True)  3.64 us
    all_to_all x1, starting transfers between devices, per_device(): query_team = lax.all_to_all(query_team, TEAM, 0, 0, tiled=True)  3.47 us
  transfers between devices with their start and end apart: 8, of which 5 were waited for; matrix products, arithmetic and copies ran while one was open for 4% of the time, Pallas kernels for 9%

profile of v4, /device:TPU:32, one launch (start us, length us, event | category | flops | bytes accessed | tf_op | source)
XLA Modules:
  0.0 88.7 jit_solution(4758550824241914541)
XLA Ops:
  0.0 0.9 fusion
  0.9 0.1 copy-done.1
  1.0 0.0 copy-start
  1.1 0.7 pad_maximum_fusion.2
  1.8 3.6 %all-to-all-start = ((bf16[4,128,256]{2,1,0:T(8,128)(2,1)}), bf16[4,128,256]{2,1,0:T(8,128)(2,1)S(1)}, u32[]{:S(2)}, u32[]{:S(2)}) async-start(bf16[4,128,256]{2,1,0:T(8,128)(2,1)} %pad_maximum_fusion.2), calls=%async_computation | async-start | bytes 524288 | tf_op jit(solution)/shard_map/all_to_all | solution.py:169
  5.4 0.7 copy-done.2
  6.1 0.1 copy.16
  6.2 0.1 reduce-window.8
  6.2 0.1 reduce
  6.4 0.9 pad_maximum_fusion
  7.3 4.2 %all-to-all-done.refs_0_ = bf16[4,128,256]{2,1,0:T(8,128)(2,1)S(1)} async-done(((bf16[4,128,256]{2,1,0:T(8,128)(2,1)}), bf16[4,128,256]{2,1,0:T(8,128)(2,1)S(1)}, u32[]{:S(2)}, u32[]{:S(2)}) %all-to-all-start) | async-done | bytes 262176 | tf_op jit(solution)/shard_map/all_to_all | solution.py:169
  11.5 3.5 %all-to-all-start.1 = ((bf16[4,128,512]{2,1,0:T(8,128)(2,1)}), bf16[4,128,512]{2,1,0:T(8,128)(2,1)S(1)}, u32[]{:S(2)}, u32[]{:S(2)}) async-start(bf16[4,128,512]{2,1,0:T(8,128)(2,1)} %pad_maximum_fusion), calls=%async_computation.1 | async-start | bytes 1048576 | tf_op jit(solution)/shard_map/all_to_all | solution.py:176
  15.0 0.1 select_reduce_fusion
  15.1 0.6 fusion.2
  15.7 1.3 %pad_add_fusion.info = s32[3]{0:T(128)S(1)} fusion(s32[1]{0:T(128)} %get-tuple-element.64, s32[1]{0:T(128)} %get-tuple-element.63, s32[1]{0:T(128)} %bitcast), kind=kLoop, calls=%fused_computation.18 | loop fusion | flops 6 | bytes 24 | tf_op jit(solution)/shard_map/stack | solution.py:160
  17.0 0.1 broadcast_in_dim.13.low_ref
  17.1 3.4 %collective-permute-start.2 = (bf16[4,128,256]{2,1,0:T(8,128)(2,1)S(1)}, bf16[4,128,256]{2,1,0:T(8,128)(2,1)S(1)}, u32[]{:S(2)}, u32[]{:S(2)}) collective-permute-start(bf16[4,128,256]{2,1,0:T(8,128)(2,1)S(1)} %all-to-all-done.refs_0_), channel_id=1, source_target_pairs={{0,16},{1,17},{2,18},{3,19},{4,20},{5,21},{6,22},{7,23},{8,24},{9,... | collective-permute-start | bytes 786440 | tf_op jit(solution)/shard_map/ppermute | solution.py:31
  20.5 10.7 %collective-permute-start.1 = (bf16[4,128,256]{2,1,0:T(8,128)(2,1)S(1)}, bf16[4,128,256]{2,1,0:T(8,128)(2,1)S(1)}, u32[]{:S(2)}, u32[]{:S(2)}) collective-permute-start(bf16[4,128,256]{2,1,0:T(8,128)(2,1)S(1)} %all-to-all-done.refs_0_), channel_id=1, source_target_pairs={{0,8},{1,9},{2,10},{3,11},{4,12},{5,13},{6,14},{7,15},{8,16},{9,17... | collective-permute-start | bytes 786440 | tf_op jit(solution)/shard_map/ppermute | solution.py:31
  31.2 4.3 %collective-permute-start = (bf16[4,128,256]{2,1,0:T(8,128)(2,1)S(1)}, bf16[4,128,256]{2,1,0:T(8,128)(2,1)S(1)}, u32[]{:S(2)}, u32[]{:S(2)}) collective-permute-start(bf16[4,128,256]{2,1,0:T(8,128)(2,1)S(1)} %all-to-all-done.refs_0_), channel_id=1, source_target_pairs={{0,4},{1,5},{2,6},{3,7},{4,8},{5,9},{6,10},{7,11},{8,12},{9,13},{1... | collective-permute-start | bytes 786440 | tf_op jit(solution)/shard_map/ppermute | solution.py:31
  35.5 6.6 %collective-permute-start.3 = (bf16[4,128,256]{2,1,0:T(8,128)(2,1)S(1)}, bf16[4,128,256]{2,1,0:T(8,128)(2,1)S(1)}, u32[]{:S(2)}, u32[]{:S(2)}) collective-permute-start(bf16[4,128,256]{2,1,0:T(8,128)(2,1)S(1)} %broadcast_select_fusion), channel_id=1, source_target_pairs={{0,12},{1,13},{2,14},{3,15},{4,0},{5,1},{6,2},{7,3},{8,4},{9,5},{1... | collective-permute-start | bytes 786440 | tf_op jit(solution)/shard_map/ppermute | solution.py:41
  42.2 2.8 %attend.4 = (f32[4,512,128]{2,1,0:T(8,128)S(1)}, f32[4,512,128]{2,1,0:T(8,128)S(1)}, f32[4,512,128]{2,1,0:T(8,128)S(1)}) custom-call(s32[3]{0:T(128)S(1)} %pad_add_fusion.info, s32[512,128]{1,0:T(8,128)S(1)} %broadcast_in_dim.13.low_ref, bf16[4,128,512]{2,1,0:T(8,128)(2,1)S(1)} %all-to-all-done.1.q_ref, bf16[4,128,256]{2,1,0:T(8,128)(2,1)S(1)} %all-to-all-done.refs_0_, ...), custom_call_target="tpu_custom_call" | custom-call | flops 3428571392 | bytes 4000000 | tf_op jit(solution)/shard_map/attend/pallas_call | solution.py:134
  45.0 7.3 %collective-permute-done.1.refs_0_ = bf16[4,128,256]{2,1,0:T(8,128)(2,1)S(1)} collective-permute-done((bf16[4,128,256]{2,1,0:T(8,128)(2,1)S(1)}, bf16[4,128,256]{2,1,0:T(8,128)(2,1)S(1)}, u32[]{:S(2)}, u32[]{:S(2)}) %collective-permute-start.1) | collective-permute-done | bytes 262176 | tf_op jit(solution)/shard_map/ppermute | solution.py:31
  52.3 1.9 %collective-permute-start.5 = (bf16[4,128,256]{2,1,0:T(8,128)(2,1)S(1)}, bf16[4,128,256]{2,1,0:T(8,128)(2,1)S(1)}, u32[]{:S(2)}, u32[]{:S(2)}) collective-permute-start(bf16[4,128,256]{2,1,0:T(8,128)(2,1)S(1)} %collective-permute-done.1.refs_0_), channel_id=1, source_target_pairs={{0,16},{1,17},{2,18},{3,19},{4,20},{5,21},{6,22},{7,23},{8,24},{9,... | collective-permute-start | bytes 786440 | tf_op jit(solution)/shard_map/ppermute | solution.py:31
  54.3 1.6 %collective-permute-done.3.refs_1_ = bf16[4,128,256]{2,1,0:T(8,128)(2,1)S(1)} collective-permute-done((bf16[4,128,256]{2,1,0:T(8,128)(2,1)S(1)}, bf16[4,128,256]{2,1,0:T(8,128)(2,1)S(1)}, u32[]{:S(2)}, u32[]{:S(2)}) %collective-permute-start.3) | collective-permute-done | bytes 262176 | tf_op jit(solution)/shard_map/ppermute | solution.py:41
  55.9 2.6 %attend.5 = (f32[4,512,128]{2,1,0:T(8,128)S(1)}, f32[4,512,128]{2,1,0:T(8,128)S(1)}, f32[4,512,128]{2,1,0:T(8,128)S(1)}) custom-call(s32[3]{0:T(128)S(1)} %pad_add_fusion.info, s32[512,128]{1,0:T(8,128)S(1)} %broadcast_in_dim.13.low_ref, bf16[4,128,512]{2,1,0:T(8,128)(2,1)S(1)} %all-to-all-done.1.q_ref, ...), custom_call_target="tpu_custom_call", output_to_operand_aliasing={{0}: (5, {}), {1}: (6, {}), {2}: (7, {})} | custom-call | flops 3428571392 | bytes 4000000 | tf_op jit(solution)/shard_map/attend/pallas_call | solution.py:134
  58.5 4.7 %collective-permute-done.refs_0_ = bf16[4,128,256]{2,1,0:T(8,128)(2,1)S(1)} collective-permute-done((bf16[4,128,256]{2,1,0:T(8,128)(2,1)S(1)}, bf16[4,128,256]{2,1,0:T(8,128)(2,1)S(1)}, u32[]{:S(2)}, u32[]{:S(2)}) %collective-permute-start) | collective-permute-done | bytes 262176 | tf_op jit(solution)/shard_map/ppermute | solution.py:31
  63.3 1.9 %collective-permute-start.4 = (bf16[4,128,256]{2,1,0:T(8,128)(2,1)S(1)}, bf16[4,128,256]{2,1,0:T(8,128)(2,1)S(1)}, u32[]{:S(2)}, u32[]{:S(2)}) collective-permute-start(bf16[4,128,256]{2,1,0:T(8,128)(2,1)S(1)} %collective-permute-done.refs_0_), channel_id=1, source_target_pairs={{0,16},{1,17},{2,18},{3,19},{4,20},{5,21},{6,22},{7,23},{8,24},{9,... | collective-permute-start | bytes 786440 | tf_op jit(solution)/shard_map/ppermute | solution.py:31
  65.2 2.4 %attend.6 = (f32[4,512,128]{2,1,0:T(8,128)S(1)}, f32[4,512,128]{2,1,0:T(8,128)S(1)}, f32[4,512,128]{2,1,0:T(8,128)S(1)}) custom-call(s32[3]{0:T(128)S(1)} %pad_add_fusion.info, s32[512,128]{1,0:T(8,128)S(1)} %broadcast_in_dim.13.low_ref, bf16[4,128,512]{2,1,0:T(8,128)(2,1)S(1)} %all-to-all-done.1.q_ref, ...), custom_call_target="tpu_custom_call", output_to_operand_aliasing={{0}: (4, {}), {1}: (5, {}), {2}: (6, {})} | custom-call | flops 1714285696 | bytes 4000000 | tf_op jit(solution)/shard_map/attend/pallas_call | solution.py:134
  67.6 8.0 %collective-permute-done.4.refs_0_ = bf16[4,128,256]{2,1,0:T(8,128)(2,1)S(1)} collective-permute-done((bf16[4,128,256]{2,1,0:T(8,128)(2,1)S(1)}, bf16[4,128,256]{2,1,0:T(8,128)(2,1)S(1)}, u32[]{:S(2)}, u32[]{:S(2)}) %collective-permute-start.4) | collective-permute-done | bytes 262176 | tf_op jit(solution)/shard_map/ppermute | solution.py:31
  75.6 1.0 %attend.7 = (f32[4,512,128]{2,1,0:T(8,128)S(1)}, f32[4,512,128]{2,1,0:T(8,128)S(1)}, f32[4,512,128]{2,1,0:T(8,128)S(1)}, bf16[4,128,512]{2,1,0:T(8,128)(2,1)S(1)}) custom-call(s32[3]{0:T(128)S(1)} %pad_add_fusion.info, s32[512,128]{1,0:T(8,128)S(1)} %broadcast_in_dim.13.low_ref, ...), custom_call_target="tpu_custom_call", output_to_operand_aliasing={{0}: (5, {}), {1}: (6, {}), {2}: (7, {})} | custom-call | flops 3428571392 | bytes 4000000 | tf_op jit(solution)/shard_map/attend/pallas_call | solution.py:134
  76.6 11.2 %all_to_all.15 = bf16[4,128,512]{2,1,0:T(8,128)(2,1)S(1)} all-to-all(bf16[4,128,512]{2,1,0:T(8,128)(2,1)S(1)} %get-tuple-element.46), channel_id=1, replica_groups=mesh['docs'=32,'sub'=4,'chip'=2,'core'=2] {'chip','core'}, dimensions={0} | all-to-all | bytes 1048576 | tf_op jit(solution)/shard_map/all_to_all | solution.py:186
  87.9 0.8 pad_maximum_fusion.1
  (13 shorter events, 0.2 us)
Async XLA Ops:
  0.0 1.0 %copy-start.1 = (bf16[128,512]{1,0:T(8,128)(2,1)S(1)}, bf16[128,512]{1,0:T(8,128)(2,1)}, u32[]{:S(2)}) copy-start(bf16[128,512]{1,0:T(8,128)(2,1)} %param.6) | copy-start | bytes 393220
  1.0 5.3 %copy-start = (bf16[128,2048]{1,0:T(8,128)(2,1)S(1)}, bf16[128,2048]{1,0:T(8,128)(2,1)}, u32[]{:S(2)}) copy-start(bf16[128,2048]{1,0:T(8,128)(2,1)} %param.4) | copy-start | bytes 1572868
  1.8 9.7 %all-to-all-start = ((bf16[4,128,256]{2,1,0:T(8,128)(2,1)}), bf16[4,128,256]{2,1,0:T(8,128)(2,1)S(1)}, u32[]{:S(2)}, u32[]{:S(2)}) async-start(bf16[4,128,256]{2,1,0:T(8,128)(2,1)} %pad_maximum_fusion.2), calls=%async_computation | async-start | bytes 524288 | tf_op jit(solution)/shard_map/all_to_all | solution.py:169
  5.4 0.7 copy-start.2
  11.5 30.7 %all-to-all-start.1 = ((bf16[4,128,512]{2,1,0:T(8,128)(2,1)}), bf16[4,128,512]{2,1,0:T(8,128)(2,1)S(1)}, u32[]{:S(2)}, u32[]{:S(2)}) async-start(bf16[4,128,512]{2,1,0:T(8,128)(2,1)} %pad_maximum_fusion), calls=%async_computation.1 | async-start | bytes 1048576 | tf_op jit(solution)/shard_map/all_to_all | solution.py:176
  17.1 18.4 %collective-permute-start.2 = (bf16[4,128,256]{2,1,0:T(8,128)(2,1)S(1)}, bf16[4,128,256]{2,1,0:T(8,128)(2,1)S(1)}, u32[]{:S(2)}, u32[]{:S(2)}) collective-permute-start(bf16[4,128,256]{2,1,0:T(8,128)(2,1)S(1)} %all-to-all-done.refs_0_), channel_id=1, source_target_pairs={{0,16},{1,17},{2,18},{3,19},{4,20},{5,21},{6,22},{7,23},{8,24},{9,... | collective-permute-start | bytes 786440 | tf_op jit(solution)/shard_map/ppermute | solution.py:31
  20.5 31.8 %collective-permute-start.1 = (bf16[4,128,256]{2,1,0:T(8,128)(2,1)S(1)}, bf16[4,128,256]{2,1,0:T(8,128)(2,1)S(1)}, u32[]{:S(2)}, u32[]{:S(2)}) collective-permute-start(bf16[4,128,256]{2,1,0:T(8,128)(2,1)S(1)} %all-to-all-done.refs_0_), channel_id=1, source_target_pairs={{0,8},{1,9},{2,10},{3,11},{4,12},{5,13},{6,14},{7,15},{8,16},{9,17... | collective-permute-start | bytes 786440 | tf_op jit(solution)/shard_map/ppermute | solution.py:31
  31.2 32.1 %collective-permute-start = (bf16[4,128,256]{2,1,0:T(8,128)(2,1)S(1)}, bf16[4,128,256]{2,1,0:T(8,128)(2,1)S(1)}, u32[]{:S(2)}, u32[]{:S(2)}) collective-permute-start(bf16[4,128,256]{2,1,0:T(8,128)(2,1)S(1)} %all-to-all-done.refs_0_), channel_id=1, source_target_pairs={{0,4},{1,5},{2,6},{3,7},{4,8},{5,9},{6,10},{7,11},{8,12},{9,13},{1... | collective-permute-start | bytes 786440 | tf_op jit(solution)/shard_map/ppermute | solution.py:31
  35.5 20.3 %collective-permute-start.3 = (bf16[4,128,256]{2,1,0:T(8,128)(2,1)S(1)}, bf16[4,128,256]{2,1,0:T(8,128)(2,1)S(1)}, u32[]{:S(2)}, u32[]{:S(2)}) collective-permute-start(bf16[4,128,256]{2,1,0:T(8,128)(2,1)S(1)} %broadcast_select_fusion), channel_id=1, source_target_pairs={{0,12},{1,13},{2,14},{3,15},{4,0},{5,1},{6,2},{7,3},{8,4},{9,5},{1... | collective-permute-start | bytes 786440 | tf_op jit(solution)/shard_map/ppermute | solution.py:41
  52.3 15.3 %collective-permute-start.5 = (bf16[4,128,256]{2,1,0:T(8,128)(2,1)S(1)}, bf16[4,128,256]{2,1,0:T(8,128)(2,1)S(1)}, u32[]{:S(2)}, u32[]{:S(2)}) collective-permute-start(bf16[4,128,256]{2,1,0:T(8,128)(2,1)S(1)} %collective-permute-done.1.refs_0_), channel_id=1, source_target_pairs={{0,16},{1,17},{2,18},{3,19},{4,20},{5,21},{6,22},{7,23},{8,24},{9,... | collective-permute-start | bytes 786440 | tf_op jit(solution)/shard_map/ppermute | solution.py:31
  63.3 12.3 %collective-permute-start.4 = (bf16[4,128,256]{2,1,0:T(8,128)(2,1)S(1)}, bf16[4,128,256]{2,1,0:T(8,128)(2,1)S(1)}, u32[]{:S(2)}, u32[]{:S(2)}) collective-permute-start(bf16[4,128,256]{2,1,0:T(8,128)(2,1)S(1)} %collective-permute-done.refs_0_), channel_id=1, source_target_pairs={{0,16},{1,17},{2,18},{3,19},{4,20},{5,21},{6,22},{7,23},{8,24},{9,... | collective-permute-start | bytes 786440 | tf_op jit(solution)/shard_map/ppermute | solution.py:31

commit v5 on v4

--- a/solution.py
+++ b/solution.py
@@ -153,13 +153,9 @@
 
 def per_device(queries, keys, values, lengths):
     docs = lax.axis_size("docs")
-    base = (lax.axis_index("docs") * 4 + lax.axis_index("sub")) * PIECE
-    bounds = jnp.cumsum(lengths)
-    place = base + jnp.arange(PIECE, dtype=jnp.int32)
-    low = jnp.max(jnp.where(bounds[None, :] <= place[:, None], bounds[None, :], 0), axis=1)
-    info = jnp.stack([base, low[0], low[-1]]).astype(jnp.int32)
-    low = jnp.broadcast_to(low[:, None], (PIECE, 128))
-
+    query_team = jnp.stack([columns(queries, n, WIDTH) for n in range(KEY_VALUE_HEADS)])
+    query_team, keys, values = lax.optimization_barrier((query_team, keys, values))
+    query_team = lax.all_to_all(query_team, TEAM, 0, 0, tiled=True)
     key_value = jnp.stack(
         [
             jnp.concatenate([columns(keys, n, HEAD_SIZE), columns(values, n, HEAD_SIZE)], axis=1)
@@ -167,21 +163,23 @@
         ]
     )
     own = lax.all_to_all(key_value, TEAM, 0, 0, tiled=True)
-    info, low, own = lax.optimization_barrier((info, low, own))
     sub = lax.axis_index("sub")
     back1 = shift(own, 1, docs)
     back2 = shift(own, 2, docs)
     back4 = shift(own, 4, docs)
-    query_team = jnp.stack([columns(queries, n, WIDTH) for n in range(KEY_VALUE_HEADS)])
-    query_team = lax.all_to_all(query_team, TEAM, 0, 0, tiled=True)
+    lengths, back4 = lax.optimization_barrier((lengths, back4))
+    base = (lax.axis_index("docs") * 4 + lax.axis_index("sub")) * PIECE
+    bounds = jnp.cumsum(lengths)
+    place = base + jnp.arange(PIECE, dtype=jnp.int32)
+    low = jnp.max(jnp.where(bounds[None, :] <= place[:, None], bounds[None, :], 0), axis=1)
+    info = jnp.stack([base, low[0], low[-1]]).astype(jnp.int32)
+    low = jnp.broadcast_to(low[:, None], (PIECE, 128))
     back3 = turn_back(jnp.where(sub == 0, own, back4), docs)
     state = attend(info, low, query_team, (own, back4), (0, 4), (), False)
-    back2, *state = lax.optimization_barrier((back2, *state))
+    back1, *state = lax.optimization_barrier((back1, *state))
     back6 = shift(back2, 4, docs)
-    state = attend(info, low, query_team, (back2, back3), (2, 3), state, False)
-    back1, *state = lax.optimization_barrier((back1, *state))
     back5 = shift(back1, 4, docs)
-    state = attend(info, low, query_team, (back1,), (1,), state, False)
+    state = attend(info, low, query_team, (back1, back2, back3), (1, 2, 3), state, False)
     outcome = attend(info, low, query_team, (back5, back6), (5, 6), state, True)[3]
     outcome = lax.all_to_all(outcome, TEAM, 0, 0, tiled=True)
     return jnp.concatenate([outcome[n] for n in range(KEY_VALUE_HEADS)], axis=1)

time: 89.2 us -> 83.9 us (0.941)
  the two profiles are of different devices: /device:TPU:32 before, /device:TPU:26 now
where the time goes in v5:
time: 83.9 us; the launch traced here: 83.5 us
  starting transfers between devices  35.3 us (42%)
  blocking collectives  26.8 us (32%)
  Pallas kernels  12.5 us (15%)
  other arithmetic  3.42 us (4%)
  waiting for transfers between devices  3.05 us (4%)
  local copies, waits for them, and re-layouts  2.22 us (3%)
    ppermute x5, starting transfers between devices, shift(): lax.ppermute(x, ALL, [(i, i + by * 4) for i in range(count - by * 4)])  27.5 us
    all_to_all x1, blocking collectives, per_device(): outcome = lax.all_to_all(outcome, TEAM, 0, 0, tiled=True)  17.4 us
    pallas_call x3, Pallas kernels, attend(): pl.pallas_call(functools.partial(attend_kernel, behind, not state, last),...  12.5 us
    all_to_all x1, blocking collectives, per_device(): own = lax.all_to_all(key_value, TEAM, 0, 0, tiled=True)  9.48 us
    ppermute x1, starting transfers between devices, turn_back(): return lax.ppermute(x, ALL, pairs)  4.29 us
    all_to_all x1, starting transfers between devices, per_device(): query_team = lax.all_to_all(query_team, TEAM, 0, 0, tiled=True)  3.48 us
    ppermute x5, waiting for transfers between devices, shift(): lax.ppermute(x, ALL, [(i, i + by * 4) for i in range(count - by * 4)])  3.04 us
  transfers between devices with their start and end apart: 7, of which 2 were waited for; matrix products, arithmetic and copies ran while one was open for 3% of the time, Pallas kernels for 14%

profile of v5, /device:TPU:26, one launch (start us, length us, event | category | flops | bytes accessed | tf_op | source)
XLA Modules:
  0.0 83.5 jit_solution(5421454198875906801)
XLA Ops:
  0.0 1.1 %slice_bitcast_fusion.7 = (bf16[1,128,512]{2,1,0:T(8,128)(2,1)S(1)}, bf16[1,128,512]{2,1,0:T(8,128)(2,1)S(1)}, bf16[1,128,512]{2,1,0:T(8,128)(2,1)S(1)}, bf16[1,128,512]{2,1,0:T(8,128)(2,1)S(1)}) fusion(bf16[128,2048]{1,0:T(8,128)(2,1)} %param.4), kind=kLoop, calls=%fused_computation.11 | loop fusion | bytes 1048576 | tf_op jit(solution)/shard_map/stack | solution.py:156
  1.1 0.0 copy-start
  1.1 0.0 copy-start.1
  1.2 0.9 %pad_maximum_fusion = bf16[4,128,512]{2,1,0:T(8,128)(2,1)} fusion(bf16[1,128,512]{2,1,0:T(8,128)(2,1)S(1)} %get-tuple-element.43, bf16[1,128,512]{2,1,0:T(8,128)(2,1)S(1)} %get-tuple-element.44, bf16[1,128,512]{2,1,0:T(8,128)(2,1)S(1)} %get-tuple-element.42, bf16[1,128,512]{2,1,0:T(8,128)(2,1)S(1)} %get-tuple-element.41), kind=kLoop, calls=%fused_computation | loop fusion | flops 786432 | bytes 1048576 | tf_op jit(solution)/shard_map/stack | solution.py:156
  2.0 0.0 copy-done
  2.0 0.1 copy-done.1
  2.3 9.5 %all_to_all.15.refs_0_ = bf16[4,128,256]{2,1,0:T(8,128)(2,1)S(1)} all-to-all(bf16[4,128,256]{2,1,0:T(8,128)(2,1)S(1)} %pad_maximum_fusion.2), channel_id=1, replica_groups=mesh['docs'=32,'sub'=4,'chip'=2,'core'=2] {'chip','core'}, dimensions={0} | all-to-all | bytes 524288 | tf_op jit(solution)/shard_map/all_to_all | solution.py:165
  11.8 3.4 %collective-permute-start = (bf16[4,128,256]{2,1,0:T(8,128)(2,1)S(1)}, bf16[4,128,256]{2,1,0:T(8,128)(2,1)S(1)}, u32[]{:S(2)}, u32[]{:S(2)}) collective-permute-start(bf16[4,128,256]{2,1,0:T(8,128)(2,1)S(1)} %all_to_all.15.refs_0_), channel_id=1, source_target_pairs={{0,16},{1,17},{2,18},{3,19},{4,20},{5,21},{6,22},{7,23},{8,24},{9,... | collective-permute-start | bytes 786440 | tf_op jit(solution)/shard_map/ppermute | solution.py:31
  15.2 3.5 %all-to-all-start.1 = ((bf16[4,128,512]{2,1,0:T(8,128)(2,1)}), bf16[4,128,512]{2,1,0:T(8,128)(2,1)S(1)}, u32[]{:S(2)}, u32[]{:S(2)}) async-start(bf16[4,128,512]{2,1,0:T(8,128)(2,1)} %pad_maximum_fusion), calls=%async_computation.1 | async-start | bytes 1048576 | tf_op jit(solution)/shard_map/all_to_all | solution.py:158
  18.7 10.0 %collective-permute-start.3 = (bf16[4,128,256]{2,1,0:T(8,128)(2,1)S(1)}, bf16[4,128,256]{2,1,0:T(8,128)(2,1)S(1)}, u32[]{:S(2)}, u32[]{:S(2)}) collective-permute-start(bf16[4,128,256]{2,1,0:T(8,128)(2,1)S(1)} %all_to_all.15.refs_0_), channel_id=1, source_target_pairs={{0,8},{1,9},{2,10},{3,11},{4,12},{5,13},{6,14},{7,15},{8,16},{9,17... | collective-permute-start | bytes 786440 | tf_op jit(solution)/shard_map/ppermute | solution.py:31
  28.7 0.0 copy-start.2
  28.8 4.3 %collective-permute-start.1 = (bf16[4,128,256]{2,1,0:T(8,128)(2,1)S(1)}, bf16[4,128,256]{2,1,0:T(8,128)(2,1)S(1)}, u32[]{:S(2)}, u32[]{:S(2)}) collective-permute-start(bf16[4,128,256]{2,1,0:T(8,128)(2,1)S(1)} %all_to_all.15.refs_0_), channel_id=1, source_target_pairs={{0,4},{1,5},{2,6},{3,7},{4,8},{5,9},{6,10},{7,11},{8,12},{9,13},{1... | collective-permute-start | bytes 786440 | tf_op jit(solution)/shard_map/ppermute | solution.py:31
  33.1 0.0 collective-permute-done.refs_1_
  33.1 0.1 copy.13
  33.2 0.1 reduce-window.8
  33.2 0.1 reduce
  33.4 4.3 %collective-permute-start.5 = (bf16[4,128,256]{2,1,0:T(8,128)(2,1)S(1)}, bf16[4,128,256]{2,1,0:T(8,128)(2,1)S(1)}, u32[]{:S(2)}, u32[]{:S(2)}) collective-permute-start(bf16[4,128,256]{2,1,0:T(8,128)(2,1)S(1)} %broadcast_select_fusion), channel_id=1, source_target_pairs={{0,12},{1,13},{2,14},{3,15},{4,0},{5,1},{6,2},{7,3},{8,4},{9,5},{1... | collective-permute-start | bytes 786440 | tf_op jit(solution)/shard_map/ppermute | solution.py:41
  37.7 2.4 %collective-permute-done.3.refs_1_ = bf16[4,128,256]{2,1,0:T(8,128)(2,1)S(1)} collective-permute-done((bf16[4,128,256]{2,1,0:T(8,128)(2,1)S(1)}, bf16[4,128,256]{2,1,0:T(8,128)(2,1)S(1)}, u32[]{:S(2)}, u32[]{:S(2)}) %collective-permute-start.3) | collective-permute-done | bytes 262176 | tf_op jit(solution)/shard_map/ppermute | solution.py:31
  40.1 3.4 %collective-permute-start.4 = (bf16[4,128,256]{2,1,0:T(8,128)(2,1)S(1)}, bf16[4,128,256]{2,1,0:T(8,128)(2,1)S(1)}, u32[]{:S(2)}, u32[]{:S(2)}) collective-permute-start(bf16[4,128,256]{2,1,0:T(8,128)(2,1)S(1)} %collective-permute-done.3.refs_1_), channel_id=1, source_target_pairs={{0,16},{1,17},{2,18},{3,19},{4,20},{5,21},{6,22},{7,23},{8,24},{9,... | collective-permute-start | bytes 786440 | tf_op jit(solution)/shard_map/ppermute | solution.py:31
  43.5 0.1 select_reduce_fusion
  43.6 0.6 fusion.2
  44.2 1.3 %pad_add_fusion.info = s32[3]{0:T(128)S(1)} fusion(s32[1]{0:T(128)} %get-tuple-element.54, s32[1]{0:T(128)} %get-tuple-element.53, s32[1]{0:T(128)} %bitcast), kind=kLoop, calls=%fused_computation.18 | loop fusion | flops 6 | bytes 24 | tf_op jit(solution)/shard_map/stack | solution.py:175
  45.6 0.0 all-to-all-done.1.q_ref
  45.6 0.1 broadcast_in_dim.13.low_ref
  45.7 4.8 %attend.3 = (f32[4,512,128]{2,1,0:T(8,128)S(1)}, f32[4,512,128]{2,1,0:T(8,128)S(1)}, f32[4,512,128]{2,1,0:T(8,128)S(1)}) custom-call(s32[3]{0:T(128)S(1)} %pad_add_fusion.info, s32[512,128]{1,0:T(8,128)S(1)} %broadcast_in_dim.13.low_ref, bf16[4,128,512]{2,1,0:T(8,128)(2,1)S(1)} %all-to-all-done.1.q_ref, bf16[4,128,256]{2,1,0:T(8,128)(2,1)S(1)} %all_to_all.15.refs_0_, ...), custom_call_target="tpu_custom_call" | custom-call | flops 3428571392 | bytes 4000000 | tf_op jit(solution)/shard_map/attend/pallas_call | solution.py:134
  50.5 0.6 collective-permute-done.1.refs_0_
  51.2 6.4 %collective-permute-start.2 = (bf16[4,128,256]{2,1,0:T(8,128)(2,1)S(1)}, bf16[4,128,256]{2,1,0:T(8,128)(2,1)S(1)}, u32[]{:S(2)}, u32[]{:S(2)}) collective-permute-start(bf16[4,128,256]{2,1,0:T(8,128)(2,1)S(1)} %collective-permute-done.1.refs_0_), channel_id=1, source_target_pairs={{0,16},{1,17},{2,18},{3,19},{4,20},{5,21},{6,22},{7,23},{8,24},{9,... | collective-permute-start | bytes 786440 | tf_op jit(solution)/shard_map/ppermute | solution.py:31
  57.6 0.0 collective-permute-done.5.refs_2_
  57.6 6.7 %attend.4 = (f32[4,512,128]{2,1,0:T(8,128)S(1)}, f32[4,512,128]{2,1,0:T(8,128)S(1)}, f32[4,512,128]{2,1,0:T(8,128)S(1)}) custom-call(s32[3]{0:T(128)S(1)} %pad_add_fusion.info, s32[512,128]{1,0:T(8,128)S(1)} %broadcast_in_dim.13.low_ref, bf16[4,128,512]{2,1,0:T(8,128)(2,1)S(1)} %all-to-all-done.1.q_ref, ...), custom_call_target="tpu_custom_call", output_to_operand_aliasing={{0}: (6, {}), {1}: (7, {}), {2}: (8, {})} | custom-call | flops 5142857216 | bytes 4000000 | tf_op jit(solution)/shard_map/attend/pallas_call | solution.py:134
  64.3 1.0 %attend.5 = (f32[4,512,128]{2,1,0:T(8,128)S(1)}, f32[4,512,128]{2,1,0:T(8,128)S(1)}, f32[4,512,128]{2,1,0:T(8,128)S(1)}, bf16[4,128,512]{2,1,0:T(8,128)(2,1)S(1)}) custom-call(s32[3]{0:T(128)S(1)} %pad_add_fusion.info, s32[512,128]{1,0:T(8,128)S(1)} %broadcast_in_dim.13.low_ref, ...), custom_call_target="tpu_custom_call", output_to_operand_aliasing={{0}: (5, {}), {1}: (6, {}), {2}: (7, {})} | custom-call | flops 3428571392 | bytes 4000000 | tf_op jit(solution)/shard_map/attend/pallas_call | solution.py:134
  65.3 17.4 %all_to_all.16 = bf16[4,128,512]{2,1,0:T(8,128)(2,1)S(1)} all-to-all(bf16[4,128,512]{2,1,0:T(8,128)(2,1)S(1)} %get-tuple-element.36), channel_id=1, replica_groups=mesh['docs'=32,'sub'=4,'chip'=2,'core'=2] {'chip','core'}, dimensions={0} | all-to-all | bytes 1048576 | tf_op jit(solution)/shard_map/all_to_all | solution.py:184
  82.7 0.8 %pad_maximum_fusion.1 = bf16[128,2048]{1,0:T(8,128)(2,1)} fusion(bf16[128,512]{1,0:T(8,128)(2,1)S(1)} %get-tuple-element.38, bf16[128,512]{1,0:T(8,128)(2,1)S(1)} %get-tuple-element.39, bf16[128,512]{1,0:T(8,128)(2,1)S(1)} %get-tuple-element.40, bf16[128,512]{1,0:T(8,128)(2,1)S(1)} %get-tuple-element.37), kind=kLoop, calls=%fused_computation.1 | loop fusion | flops 2097152 | bytes 1048576 | tf_op jit(solution)/shard_map/concatenate | solution.py:185
  (12 shorter events, 0.2 us)
Async XLA Ops:
  1.1 0.9 %copy-start = (bf16[128,512]{1,0:T(8,128)(2,1)S(1)}, bf16[128,512]{1,0:T(8,128)(2,1)}, u32[]{:S(2)}) copy-start(bf16[128,512]{1,0:T(8,128)(2,1)} %param.5) | copy-start | bytes 393220
  1.1 1.0 %copy-start.1 = (bf16[128,512]{1,0:T(8,128)(2,1)S(1)}, bf16[128,512]{1,0:T(8,128)(2,1)}, u32[]{:S(2)}) copy-start(bf16[128,512]{1,0:T(8,128)(2,1)} %param.6) | copy-start | bytes 393220
  11.8 21.3 %collective-permute-start = (bf16[4,128,256]{2,1,0:T(8,128)(2,1)S(1)}, bf16[4,128,256]{2,1,0:T(8,128)(2,1)S(1)}, u32[]{:S(2)}, u32[]{:S(2)}) collective-permute-start(bf16[4,128,256]{2,1,0:T(8,128)(2,1)S(1)} %all_to_all.15.refs_0_), channel_id=1, source_target_pairs={{0,16},{1,17},{2,18},{3,19},{4,20},{5,21},{6,22},{7,23},{8,24},{9,... | collective-permute-start | bytes 786440 | tf_op jit(solution)/shard_map/ppermute | solution.py:31
  15.2 30.4 %all-to-all-start.1 = ((bf16[4,128,512]{2,1,0:T(8,128)(2,1)}), bf16[4,128,512]{2,1,0:T(8,128)(2,1)S(1)}, u32[]{:S(2)}, u32[]{:S(2)}) async-start(bf16[4,128,512]{2,1,0:T(8,128)(2,1)} %pad_maximum_fusion), calls=%async_computation.1 | async-start | bytes 1048576 | tf_op jit(solution)/shard_map/all_to_all | solution.py:158
  18.7 21.4 %collective-permute-start.3 = (bf16[4,128,256]{2,1,0:T(8,128)(2,1)S(1)}, bf16[4,128,256]{2,1,0:T(8,128)(2,1)S(1)}, u32[]{:S(2)}, u32[]{:S(2)}) collective-permute-start(bf16[4,128,256]{2,1,0:T(8,128)(2,1)S(1)} %all_to_all.15.refs_0_), channel_id=1, source_target_pairs={{0,8},{1,9},{2,10},{3,11},{4,12},{5,13},{6,14},{7,15},{8,16},{9,17... | collective-permute-start | bytes 786440 | tf_op jit(solution)/shard_map/ppermute | solution.py:31
  28.7 4.3 %copy-start.2 = (s32[32]{0:T(128)S(1)}, s32[32]{0:T(128)}, u32[]{:S(2)}) copy-start(s32[32]{0:T(128)} %param.7) | copy-start | bytes 388
  28.8 22.4 %collective-permute-start.1 = (bf16[4,128,256]{2,1,0:T(8,128)(2,1)S(1)}, bf16[4,128,256]{2,1,0:T(8,128)(2,1)S(1)}, u32[]{:S(2)}, u32[]{:S(2)}) collective-permute-start(bf16[4,128,256]{2,1,0:T(8,128)(2,1)S(1)} %all_to_all.15.refs_0_), channel_id=1, source_target_pairs={{0,4},{1,5},{2,6},{3,7},{4,8},{5,9},{6,10},{7,11},{8,12},{9,13},{1... | collective-permute-start | bytes 786440 | tf_op jit(solution)/shard_map/ppermute | solution.py:31
  33.4 24.2 %collective-permute-start.5 = (bf16[4,128,256]{2,1,0:T(8,128)(2,1)S(1)}, bf16[4,128,256]{2,1,0:T(8,128)(2,1)S(1)}, u32[]{:S(2)}, u32[]{:S(2)}) collective-permute-start(bf16[4,128,256]{2,1,0:T(8,128)(2,1)S(1)} %broadcast_select_fusion), channel_id=1, source_target_pairs={{0,12},{1,13},{2,14},{3,15},{4,0},{5,1},{6,2},{7,3},{8,4},{9,5},{1... | collective-permute-start | bytes 786440 | tf_op jit(solution)/shard_map/ppermute | solution.py:41
  40.1 24.2 %collective-permute-start.4 = (bf16[4,128,256]{2,1,0:T(8,128)(2,1)S(1)}, bf16[4,128,256]{2,1,0:T(8,128)(2,1)S(1)}, u32[]{:S(2)}, u32[]{:S(2)}) collective-permute-start(bf16[4,128,256]{2,1,0:T(8,128)(2,1)S(1)} %collective-permute-done.3.refs_1_), channel_id=1, source_target_pairs={{0,16},{1,17},{2,18},{3,19},{4,20},{5,21},{6,22},{7,23},{8,24},{9,... | collective-permute-start | bytes 786440 | tf_op jit(solution)/shard_map/ppermute | solution.py:31
  51.2 13.1 %collective-permute-start.2 = (bf16[4,128,256]{2,1,0:T(8,128)(2,1)S(1)}, bf16[4,128,256]{2,1,0:T(8,128)(2,1)S(1)}, u32[]{:S(2)}, u32[]{:S(2)}) collective-permute-start(bf16[4,128,256]{2,1,0:T(8,128)(2,1)S(1)} %collective-permute-done.1.refs_0_), channel_id=1, source_target_pairs={{0,16},{1,17},{2,18},{3,19},{4,20},{5,21},{6,22},{7,23},{8,24},{9,... | collective-permute-start | bytes 786440 | tf_op jit(solution)/shard_map/ppermute | solution.py:31

commit v6 on v5

--- a/solution.py
+++ b/solution.py
@@ -179,8 +179,8 @@
     back1, *state = lax.optimization_barrier((back1, *state))
     back6 = shift(back2, 4, docs)
     back5 = shift(back1, 4, docs)
-    state = attend(info, low, query_team, (back1, back2, back3), (1, 2, 3), state, False)
-    outcome = attend(info, low, query_team, (back5, back6), (5, 6), state, True)[3]
+    state = attend(info, low, query_team, (back1, back2, back3, back6), (1, 2, 3, 6), state, False)
+    outcome = attend(info, low, query_team, (back5,), (5,), state, True)[3]
     outcome = lax.all_to_all(outcome, TEAM, 0, 0, tiled=True)
     return jnp.concatenate([outcome[n] for n in range(KEY_VALUE_HEADS)], axis=1)
 

time: 83.9 us -> 84.1 us (level)
  the two profiles are of different devices: /device:TPU:26 before, /device:TPU:4 now
where the time goes in v6:
time: 84.1 us; the launch traced here: 83.7 us
  starting transfers between devices  33.3 us (40%)
  blocking collectives  24.7 us (29%)
  Pallas kernels  16.5 us (20%)
  other arithmetic  3.42 us (4%)
  waiting for transfers between devices  3.34 us (4%)
  local copies, waits for them, and re-layouts  2.22 us (3%)
    ppermute x5, starting transfers between devices, shift(): lax.ppermute(x, ALL, [(i, i + by * 4) for i in range(count - by * 4)])  25.2 us
    pallas_call x3, Pallas kernels, attend(): pl.pallas_call(functools.partial(attend_kernel, behind, not state, last),...  16.5 us
    all_to_all x1, blocking collectives, per_device(): outcome = lax.all_to_all(outcome, TEAM, 0, 0, tiled=True)  15.2 us
    all_to_all x1, blocking collectives, per_device(): own = lax.all_to_all(key_value, TEAM, 0, 0, tiled=True)  9.48 us
    ppermute x1, starting transfers between devices, turn_back(): return lax.ppermute(x, ALL, pairs)  4.59 us
    all_to_all x1, starting transfers between devices, per_device(): query_team = lax.all_to_all(query_team, TEAM, 0, 0, tiled=True)  3.48 us
    ppermute x5, waiting for transfers between devices, shift(): lax.ppermute(x, ALL, [(i, i + by * 4) for i in range(count - by * 4)])  3.34 us
  transfers between devices with their start and end apart: 7, of which 2 were waited for; matrix products, arithmetic and copies ran while one was open for 3% of the time, Pallas kernels for 16%

profile of v6, /device:TPU:4, one launch (start us, length us, event | category | flops | bytes accessed | tf_op | source)
XLA Modules:
  0.0 83.7 jit_solution(17981183894133619348)
XLA Ops:
  0.0 1.1 %slice_bitcast_fusion.7 = (bf16[1,128,512]{2,1,0:T(8,128)(2,1)S(1)}, bf16[1,128,512]{2,1,0:T(8,128)(2,1)S(1)}, bf16[1,128,512]{2,1,0:T(8,128)(2,1)S(1)}, bf16[1,128,512]{2,1,0:T(8,128)(2,1)S(1)}) fusion(bf16[128,2048]{1,0:T(8,128)(2,1)} %param.4), kind=kLoop, calls=%fused_computation.11 | loop fusion | bytes 1048576 | tf_op jit(solution)/shard_map/stack | solution.py:156
  1.1 0.0 copy-start
  1.1 0.0 copy-start.1
  1.2 0.9 %pad_maximum_fusion = bf16[4,128,512]{2,1,0:T(8,128)(2,1)} fusion(bf16[1,128,512]{2,1,0:T(8,128)(2,1)S(1)} %get-tuple-element.43, bf16[1,128,512]{2,1,0:T(8,128)(2,1)S(1)} %get-tuple-element.44, bf16[1,128,512]{2,1,0:T(8,128)(2,1)S(1)} %get-tuple-element.42, bf16[1,128,512]{2,1,0:T(8,128)(2,1)S(1)} %get-tuple-element.41), kind=kLoop, calls=%fused_computation | loop fusion | flops 786432 | bytes 1048576 | tf_op jit(solution)/shard_map/stack | solution.py:156
  2.0 0.0 copy-done
  2.0 0.1 copy-done.1
  2.3 9.5 %all_to_all.15.refs_0_ = bf16[4,128,256]{2,1,0:T(8,128)(2,1)S(1)} all-to-all(bf16[4,128,256]{2,1,0:T(8,128)(2,1)S(1)} %pad_maximum_fusion.2), channel_id=1, replica_groups=mesh['docs'=32,'sub'=4,'chip'=2,'core'=2] {'chip','core'}, dimensions={0} | all-to-all | bytes 524288 | tf_op jit(solution)/shard_map/all_to_all | solution.py:165
  11.8 3.1 %collective-permute-start = (bf16[4,128,256]{2,1,0:T(8,128)(2,1)S(1)}, bf16[4,128,256]{2,1,0:T(8,128)(2,1)S(1)}, u32[]{:S(2)}, u32[]{:S(2)}) collective-permute-start(bf16[4,128,256]{2,1,0:T(8,128)(2,1)S(1)} %all_to_all.15.refs_0_), channel_id=1, source_target_pairs={{0,16},{1,17},{2,18},{3,19},{4,20},{5,21},{6,22},{7,23},{8,24},{9,... | collective-permute-start | bytes 786440 | tf_op jit(solution)/shard_map/ppermute | solution.py:31
  14.9 3.5 %all-to-all-start.1 = ((bf16[4,128,512]{2,1,0:T(8,128)(2,1)}), bf16[4,128,512]{2,1,0:T(8,128)(2,1)S(1)}, u32[]{:S(2)}, u32[]{:S(2)}) async-start(bf16[4,128,512]{2,1,0:T(8,128)(2,1)} %pad_maximum_fusion), calls=%async_computation.1 | async-start | bytes 1048576 | tf_op jit(solution)/shard_map/all_to_all | solution.py:158
  18.4 10.0 %collective-permute-start.3 = (bf16[4,128,256]{2,1,0:T(8,128)(2,1)S(1)}, bf16[4,128,256]{2,1,0:T(8,128)(2,1)S(1)}, u32[]{:S(2)}, u32[]{:S(2)}) collective-permute-start(bf16[4,128,256]{2,1,0:T(8,128)(2,1)S(1)} %all_to_all.15.refs_0_), channel_id=1, source_target_pairs={{0,8},{1,9},{2,10},{3,11},{4,12},{5,13},{6,14},{7,15},{8,16},{9,17... | collective-permute-start | bytes 786440 | tf_op jit(solution)/shard_map/ppermute | solution.py:31
  28.5 0.0 copy-start.2
  28.5 4.3 %collective-permute-start.1 = (bf16[4,128,256]{2,1,0:T(8,128)(2,1)S(1)}, bf16[4,128,256]{2,1,0:T(8,128)(2,1)S(1)}, u32[]{:S(2)}, u32[]{:S(2)}) collective-permute-start(bf16[4,128,256]{2,1,0:T(8,128)(2,1)S(1)} %all_to_all.15.refs_0_), channel_id=1, source_target_pairs={{0,4},{1,5},{2,6},{3,7},{4,8},{5,9},{6,10},{7,11},{8,12},{9,13},{1... | collective-permute-start | bytes 786440 | tf_op jit(solution)/shard_map/ppermute | solution.py:31
  32.8 0.1 copy.13
  32.9 0.1 reduce-window.8
  32.9 0.1 reduce
  33.1 4.6 %collective-permute-start.4 = (bf16[4,128,256]{2,1,0:T(8,128)(2,1)S(1)}, bf16[4,128,256]{2,1,0:T(8,128)(2,1)S(1)}, u32[]{:S(2)}, u32[]{:S(2)}) collective-permute-start(bf16[4,128,256]{2,1,0:T(8,128)(2,1)S(1)} %broadcast_select_fusion), channel_id=1, source_target_pairs={{0,12},{1,13},{2,14},{3,15},{4,0},{5,1},{6,2},{7,3},{8,4},{9,5},{1... | collective-permute-start | bytes 786440 | tf_op jit(solution)/shard_map/ppermute | solution.py:41
  37.7 2.4 %collective-permute-done.3.refs_1_ = bf16[4,128,256]{2,1,0:T(8,128)(2,1)S(1)} collective-permute-done((bf16[4,128,256]{2,1,0:T(8,128)(2,1)S(1)}, bf16[4,128,256]{2,1,0:T(8,128)(2,1)S(1)}, u32[]{:S(2)}, u32[]{:S(2)}) %collective-permute-start.3) | collective-permute-done | bytes 262176 | tf_op jit(solution)/shard_map/ppermute | solution.py:31
  40.1 3.1 %collective-permute-start.5 = (bf16[4,128,256]{2,1,0:T(8,128)(2,1)S(1)}, bf16[4,128,256]{2,1,0:T(8,128)(2,1)S(1)}, u32[]{:S(2)}, u32[]{:S(2)}) collective-permute-start(bf16[4,128,256]{2,1,0:T(8,128)(2,1)S(1)} %collective-permute-done.3.refs_1_), channel_id=1, source_target_pairs={{0,16},{1,17},{2,18},{3,19},{4,20},{5,21},{6,22},{7,23},{8,24},{9,... | collective-permute-start | bytes 786440 | tf_op jit(solution)/shard_map/ppermute | solution.py:31
  43.2 0.1 select_reduce_fusion
  43.3 0.6 fusion.2
  43.9 1.3 %pad_add_fusion.info = s32[3]{0:T(128)S(1)} fusion(s32[1]{0:T(128)} %get-tuple-element.54, s32[1]{0:T(128)} %get-tuple-element.53, s32[1]{0:T(128)} %bitcast), kind=kLoop, calls=%fused_computation.18 | loop fusion | flops 6 | bytes 24 | tf_op jit(solution)/shard_map/stack | solution.py:175
  45.3 0.0 all-to-all-done.1.q_ref
  45.3 0.1 broadcast_in_dim.13.low_ref
  45.4 4.8 %attend.3 = (f32[4,512,128]{2,1,0:T(8,128)S(1)}, f32[4,512,128]{2,1,0:T(8,128)S(1)}, f32[4,512,128]{2,1,0:T(8,128)S(1)}) custom-call(s32[3]{0:T(128)S(1)} %pad_add_fusion.info, s32[512,128]{1,0:T(8,128)S(1)} %broadcast_in_dim.13.low_ref, bf16[4,128,512]{2,1,0:T(8,128)(2,1)S(1)} %all-to-all-done.1.q_ref, bf16[4,128,256]{2,1,0:T(8,128)(2,1)S(1)} %all_to_all.15.refs_0_, ...), custom_call_target="tpu_custom_call" | custom-call | flops 3428571392 | bytes 4000000 | tf_op jit(solution)/shard_map/attend/pallas_call | solution.py:134
  50.3 0.9 %collective-permute-done.1.refs_0_ = bf16[4,128,256]{2,1,0:T(8,128)(2,1)S(1)} collective-permute-done((bf16[4,128,256]{2,1,0:T(8,128)(2,1)S(1)}, bf16[4,128,256]{2,1,0:T(8,128)(2,1)S(1)}, u32[]{:S(2)}, u32[]{:S(2)}) %collective-permute-start.1) | collective-permute-done | bytes 262176 | tf_op jit(solution)/shard_map/ppermute | solution.py:31
  51.2 4.7 %collective-permute-start.2 = (bf16[4,128,256]{2,1,0:T(8,128)(2,1)S(1)}, bf16[4,128,256]{2,1,0:T(8,128)(2,1)S(1)}, u32[]{:S(2)}, u32[]{:S(2)}) collective-permute-start(bf16[4,128,256]{2,1,0:T(8,128)(2,1)S(1)} %collective-permute-done.1.refs_0_), channel_id=1, source_target_pairs={{0,16},{1,17},{2,18},{3,19},{4,20},{5,21},{6,22},{7,23},{8,24},{9,... | collective-permute-start | bytes 786440 | tf_op jit(solution)/shard_map/ppermute | solution.py:31
  55.9 0.0 collective-permute-done.4.refs_2_
  55.9 8.7 %attend.4 = (f32[4,512,128]{2,1,0:T(8,128)S(1)}, f32[4,512,128]{2,1,0:T(8,128)S(1)}, f32[4,512,128]{2,1,0:T(8,128)S(1)}) custom-call(s32[3]{0:T(128)S(1)} %pad_add_fusion.info, s32[512,128]{1,0:T(8,128)S(1)} %broadcast_in_dim.13.low_ref, bf16[4,128,512]{2,1,0:T(8,128)(2,1)S(1)} %all-to-all-done.1.q_ref, ...), custom_call_target="tpu_custom_call", output_to_operand_aliasing={{0}: (7, {}), {1}: (8, {}), {2}: (9, {})} | custom-call | flops 6857142784 | bytes 4000000 | tf_op jit(solution)/shard_map/attend/pallas_call | solution.py:134
  64.6 0.0 collective-permute-done.2.refs_0_
  64.6 2.9 %attend.5 = (f32[4,512,128]{2,1,0:T(8,128)S(1)}, f32[4,512,128]{2,1,0:T(8,128)S(1)}, f32[4,512,128]{2,1,0:T(8,128)S(1)}, bf16[4,128,512]{2,1,0:T(8,128)(2,1)S(1)}) custom-call(s32[3]{0:T(128)S(1)} %pad_add_fusion.info, s32[512,128]{1,0:T(8,128)S(1)} %broadcast_in_dim.13.low_ref, ...), custom_call_target="tpu_custom_call", output_to_operand_aliasing={{0}: (4, {}), {1}: (5, {}), {2}: (6, {})} | custom-call | flops 1714285696 | bytes 4000000 | tf_op jit(solution)/shard_map/attend/pallas_call | solution.py:134
  67.6 15.2 %all_to_all.16 = bf16[4,128,512]{2,1,0:T(8,128)(2,1)S(1)} all-to-all(bf16[4,128,512]{2,1,0:T(8,128)(2,1)S(1)} %get-tuple-element.36), channel_id=1, replica_groups=mesh['docs'=32,'sub'=4,'chip'=2,'core'=2] {'chip','core'}, dimensions={0} | all-to-all | bytes 1048576 | tf_op jit(solution)/shard_map/all_to_all | solution.py:184
  82.8 0.8 %pad_maximum_fusion.1 = bf16[128,2048]{1,0:T(8,128)(2,1)} fusion(bf16[128,512]{1,0:T(8,128)(2,1)S(1)} %get-tuple-element.38, bf16[128,512]{1,0:T(8,128)(2,1)S(1)} %get-tuple-element.39, bf16[128,512]{1,0:T(8,128)(2,1)S(1)} %get-tuple-element.40, bf16[128,512]{1,0:T(8,128)(2,1)S(1)} %get-tuple-element.37), kind=kLoop, calls=%fused_computation.1 | loop fusion | flops 2097152 | bytes 1048576 | tf_op jit(solution)/shard_map/concatenate | solution.py:185
  (12 shorter events, 0.2 us)
Async XLA Ops:
  1.1 0.9 %copy-start = (bf16[128,512]{1,0:T(8,128)(2,1)S(1)}, bf16[128,512]{1,0:T(8,128)(2,1)}, u32[]{:S(2)}) copy-start(bf16[128,512]{1,0:T(8,128)(2,1)} %param.5) | copy-start | bytes 393220
  1.1 1.0 %copy-start.1 = (bf16[128,512]{1,0:T(8,128)(2,1)S(1)}, bf16[128,512]{1,0:T(8,128)(2,1)}, u32[]{:S(2)}) copy-start(bf16[128,512]{1,0:T(8,128)(2,1)} %param.6) | copy-start | bytes 393220
  11.8 21.0 %collective-permute-start = (bf16[4,128,256]{2,1,0:T(8,128)(2,1)S(1)}, bf16[4,128,256]{2,1,0:T(8,128)(2,1)S(1)}, u32[]{:S(2)}, u32[]{:S(2)}) collective-permute-start(bf16[4,128,256]{2,1,0:T(8,128)(2,1)S(1)} %all_to_all.15.refs_0_), channel_id=1, source_target_pairs={{0,16},{1,17},{2,18},{3,19},{4,20},{5,21},{6,22},{7,23},{8,24},{9,... | collective-permute-start | bytes 786440 | tf_op jit(solution)/shard_map/ppermute | solution.py:31
  14.9 30.4 %all-to-all-start.1 = ((bf16[4,128,512]{2,1,0:T(8,128)(2,1)}), bf16[4,128,512]{2,1,0:T(8,128)(2,1)S(1)}, u32[]{:S(2)}, u32[]{:S(2)}) async-start(bf16[4,128,512]{2,1,0:T(8,128)(2,1)} %pad_maximum_fusion), calls=%async_computation.1 | async-start | bytes 1048576 | tf_op jit(solution)/shard_map/all_to_all | solution.py:158
  18.4 21.7 %collective-permute-start.3 = (bf16[4,128,256]{2,1,0:T(8,128)(2,1)S(1)}, bf16[4,128,256]{2,1,0:T(8,128)(2,1)S(1)}, u32[]{:S(2)}, u32[]{:S(2)}) collective-permute-start(bf16[4,128,256]{2,1,0:T(8,128)(2,1)S(1)} %all_to_all.15.refs_0_), channel_id=1, source_target_pairs={{0,8},{1,9},{2,10},{3,11},{4,12},{5,13},{6,14},{7,15},{8,16},{9,17... | collective-permute-start | bytes 786440 | tf_op jit(solution)/shard_map/ppermute | solution.py:31
  28.5 4.3 %copy-start.2 = (s32[32]{0:T(128)S(1)}, s32[32]{0:T(128)}, u32[]{:S(2)}) copy-start(s32[32]{0:T(128)} %param.7) | copy-start | bytes 388
  28.5 22.7 %collective-permute-start.1 = (bf16[4,128,256]{2,1,0:T(8,128)(2,1)S(1)}, bf16[4,128,256]{2,1,0:T(8,128)(2,1)S(1)}, u32[]{:S(2)}, u32[]{:S(2)}) collective-permute-start(bf16[4,128,256]{2,1,0:T(8,128)(2,1)S(1)} %all_to_all.15.refs_0_), channel_id=1, source_target_pairs={{0,4},{1,5},{2,6},{3,7},{4,8},{5,9},{6,10},{7,11},{8,12},{9,13},{1... | collective-permute-start | bytes 786440 | tf_op jit(solution)/shard_map/ppermute | solution.py:31
  33.1 22.8 %collective-permute-start.4 = (bf16[4,128,256]{2,1,0:T(8,128)(2,1)S(1)}, bf16[4,128,256]{2,1,0:T(8,128)(2,1)S(1)}, u32[]{:S(2)}, u32[]{:S(2)}) collective-permute-start(bf16[4,128,256]{2,1,0:T(8,128)(2,1)S(1)} %broadcast_select_fusion), channel_id=1, source_target_pairs={{0,12},{1,13},{2,14},{3,15},{4,0},{5,1},{6,2},{7,3},{8,4},{9,5},{1... | collective-permute-start | bytes 786440 | tf_op jit(solution)/shard_map/ppermute | solution.py:41
  40.1 15.8 %collective-permute-start.5 = (bf16[4,128,256]{2,1,0:T(8,128)(2,1)S(1)}, bf16[4,128,256]{2,1,0:T(8,128)(2,1)S(1)}, u32[]{:S(2)}, u32[]{:S(2)}) collective-permute-start(bf16[4,128,256]{2,1,0:T(8,128)(2,1)S(1)} %collective-permute-done.3.refs_1_), channel_id=1, source_target_pairs={{0,16},{1,17},{2,18},{3,19},{4,20},{5,21},{6,22},{7,23},{8,24},{9,... | collective-permute-start | bytes 786440 | tf_op jit(solution)/shard_map/ppermute | solution.py:31
  51.2 13.5 %collective-permute-start.2 = (bf16[4,128,256]{2,1,0:T(8,128)(2,1)S(1)}, bf16[4,128,256]{2,1,0:T(8,128)(2,1)S(1)}, u32[]{:S(2)}, u32[]{:S(2)}) collective-permute-start(bf16[4,128,256]{2,1,0:T(8,128)(2,1)S(1)} %collective-permute-done.1.refs_0_), channel_id=1, source_target_pairs={{0,16},{1,17},{2,18},{3,19},{4,20},{5,21},{6,22},{7,23},{8,24},{9,... | collective-permute-start | bytes 786440 | tf_op jit(solution)/shard_map/ppermute | solution.py:31

commit v7 on v6

--- a/solution.py
+++ b/solution.py
@@ -39,6 +39,38 @@
         for n in range(4)
     ]
     return lax.ppermute(x, ALL, pairs)
+
+
+def pack_kernel(queries, keys, values, query_out, key_value_out, sems):
+    copies = []
+    for n in range(KEY_VALUE_HEADS):
+        narrow = pl.ds(n * HEAD_SIZE, HEAD_SIZE)
+        parts = (
+            (keys.at[:, narrow], key_value_out.at[n, :, pl.ds(0, HEAD_SIZE)]),
+            (values.at[:, narrow], key_value_out.at[n, :, pl.ds(HEAD_SIZE, HEAD_SIZE)]),
+            (queries.at[:, pl.ds(n * WIDTH, WIDTH)], query_out.at[n]),
+        )
+        for k, (source, target) in enumerate(parts):
+            copies.append(pltpu.make_async_copy(source, target, sems.at[n, k]))
+    for copy in copies:
+        copy.start()
+    for copy in copies:
+        copy.wait()
+
+
+def pack(queries, keys, values):
+    anywhere = pl.BlockSpec(memory_space=pl.ANY)
+    return pl.pallas_call(
+        pack_kernel,
+        out_shape=[
+            jax.ShapeDtypeStruct((KEY_VALUE_HEADS, ROWS, WIDTH), jnp.bfloat16),
+            jax.ShapeDtypeStruct((KEY_VALUE_HEADS, ROWS, 2 * HEAD_SIZE), jnp.bfloat16),
+        ],
+        in_specs=[anywhere] * 3,
+        out_specs=[pl.BlockSpec(memory_space=pltpu.VMEM)] * 2,
+        scratch_shapes=[pltpu.SemaphoreType.DMA((KEY_VALUE_HEADS, 3))],
+        name="pack",
+    )(queries, keys, values)
 
 
 def attend_kernel(behind, first, last, info, low_ref, q_ref, *refs):
@@ -153,15 +185,8 @@
 
 def per_device(queries, keys, values, lengths):
     docs = lax.axis_size("docs")
-    query_team = jnp.stack([columns(queries, n, WIDTH) for n in range(KEY_VALUE_HEADS)])
-    query_team, keys, values = lax.optimization_barrier((query_team, keys, values))
+    query_team, key_value = pack(queries, keys, values)
     query_team = lax.all_to_all(query_team, TEAM, 0, 0, tiled=True)
-    key_value = jnp.stack(
-        [
-            jnp.concatenate([columns(keys, n, HEAD_SIZE), columns(values, n, HEAD_SIZE)], axis=1)
-            for n in range(KEY_VALUE_HEADS)
-        ]
-    )
     own = lax.all_to_all(key_value, TEAM, 0, 0, tiled=True)
     sub = lax.axis_index("sub")
     back1 = shift(own, 1, docs)

time: 84.1 us -> 84.6 us (level)
  the two profiles are of different devices: /device:TPU:4 before, /device:TPU:32 now
where the time goes in v7:
time: 84.6 us; the launch traced here: 83.8 us
  starting transfers between devices  30.2 us (36%)
  blocking collectives  20.9 us (25%)
  waiting for transfers between devices  20.4 us (24%)
  Pallas kernels  8.7 us (10%)
  other arithmetic  2.46 us (3%)
  local copies, waits for them, and re-layouts  0.91 us (1%)
    ppermute x5, starting transfers between devices, shift(): lax.ppermute(x, ALL, [(i, i + by * 4) for i in range(count - by * 4)])  22.1 us
    ppermute x5, waiting for transfers between devices, shift(): lax.ppermute(x, ALL, [(i, i + by * 4) for i in range(count - by * 4)])  20.4 us
    all_to_all x1, blocking collectives, per_device(): outcome = lax.all_to_all(outcome, TEAM, 0, 0, tiled=True)  11.2 us
    all_to_all x1, blocking collectives, per_device(): own = lax.all_to_all(key_value, TEAM, 0, 0, tiled=True)  9.69 us
    pallas_call x3, Pallas kernels, attend(): pl.pallas_call(functools.partial(attend_kernel, behind, not state, last),...  6.5 us
    ppermute x1, starting transfers between devices, turn_back(): return lax.ppermute(x, ALL, pairs)  4.59 us
    all_to_all x1, starting transfers between devices, per_device(): query_team = lax.all_to_all(query_team, TEAM, 0, 0, tiled=True)  3.48 us
    pallas_call x1, Pallas kernels, pack(): pl.pallas_call(pack_kernel, out_shape=[jax.ShapeDtypeStruct((KEY_VALUE_HE...  2.21 us
  transfers between devices with their start and end apart: 7, of which 4 were waited for; matrix products, arithmetic and copies ran while one was open for 3% of the time, Pallas kernels for 7%

profile of v7, /device:TPU:32, one launch (start us, length us, event | category | flops | bytes accessed | tf_op | source)
XLA Modules:
  0.0 83.8 jit_solution(7646440961732714130)
XLA Ops:
  0.0 2.2 %pack.1 = (bf16[4,128,512]{2,1,0:T(8,128)(2,1)}, bf16[4,128,256]{2,1,0:T(8,128)(2,1)}) custom-call(bf16[128,2048]{1,0:T(8,128)(2,1)} %queries.1, bf16[128,512]{1,0:T(8,128)(2,1)} %keys.1, bf16[128,512]{1,0:T(8,128)(2,1)} %values.1), custom_call_target="tpu_custom_call" | custom-call | tf_op jit(solution)/shard_map/pack/pallas_call | solution.py:63
  2.2 9.7 %all_to_all.15.refs_0_ = bf16[4,128,256]{2,1,0:T(8,128)(2,1)S(1)} all-to-all(bf16[4,128,256]{2,1,0:T(8,128)(2,1)} %get-tuple-element.20), channel_id=1, replica_groups=mesh['docs'=32,'sub'=4,'chip'=2,'core'=2] {'chip','core'}, dimensions={0} | all-to-all | bytes 524288 | tf_op jit(solution)/shard_map/all_to_all | solution.py:190
  11.9 3.4 %collective-permute-start = (bf16[4,128,256]{2,1,0:T(8,128)(2,1)S(1)}, bf16[4,128,256]{2,1,0:T(8,128)(2,1)S(1)}, u32[]{:S(2)}, u32[]{:S(2)}) collective-permute-start(bf16[4,128,256]{2,1,0:T(8,128)(2,1)S(1)} %all_to_all.15.refs_0_), channel_id=1, source_target_pairs={{0,16},{1,17},{2,18},{3,19},{4,20},{5,21},{6,22},{7,23},{8,24},{9,... | collective-permute-start | bytes 786440 | tf_op jit(solution)/shard_map/ppermute | solution.py:31
  15.3 3.5 %all-to-all-start.1 = ((bf16[4,128,512]{2,1,0:T(8,128)(2,1)}), bf16[4,128,512]{2,1,0:T(8,128)(2,1)S(1)}, u32[]{:S(2)}, u32[]{:S(2)}) async-start(bf16[4,128,512]{2,1,0:T(8,128)(2,1)} %get-tuple-element.22), calls=%async_computation.1 | async-start | bytes 1048576 | tf_op jit(solution)/shard_map/all_to_all | solution.py:189
  18.8 10.6 %collective-permute-start.3 = (bf16[4,128,256]{2,1,0:T(8,128)(2,1)S(1)}, bf16[4,128,256]{2,1,0:T(8,128)(2,1)S(1)}, u32[]{:S(2)}, u32[]{:S(2)}) collective-permute-start(bf16[4,128,256]{2,1,0:T(8,128)(2,1)S(1)} %all_to_all.15.refs_0_), channel_id=1, source_target_pairs={{0,8},{1,9},{2,10},{3,11},{4,12},{5,13},{6,14},{7,15},{8,16},{9,17... | collective-permute-start | bytes 786440 | tf_op jit(solution)/shard_map/ppermute | solution.py:31
  29.5 0.0 copy-start
  29.5 4.3 %collective-permute-start.1 = (bf16[4,128,256]{2,1,0:T(8,128)(2,1)S(1)}, bf16[4,128,256]{2,1,0:T(8,128)(2,1)S(1)}, u32[]{:S(2)}, u32[]{:S(2)}) collective-permute-start(bf16[4,128,256]{2,1,0:T(8,128)(2,1)S(1)} %all_to_all.15.refs_0_), channel_id=1, source_target_pairs={{0,4},{1,5},{2,6},{3,7},{4,8},{5,9},{6,10},{7,11},{8,12},{9,13},{1... | collective-permute-start | bytes 786440 | tf_op jit(solution)/shard_map/ppermute | solution.py:31
  33.8 0.0 collective-permute-done.refs_1_
  33.8 0.0 copy-done
  33.8 0.1 copy.13
  33.9 0.1 reduce-window.8
  34.0 0.1 reduce
  34.1 4.6 %collective-permute-start.4 = (bf16[4,128,256]{2,1,0:T(8,128)(2,1)S(1)}, bf16[4,128,256]{2,1,0:T(8,128)(2,1)S(1)}, u32[]{:S(2)}, u32[]{:S(2)}) collective-permute-start(bf16[4,128,256]{2,1,0:T(8,128)(2,1)S(1)} %broadcast_select_fusion), channel_id=1, source_target_pairs={{0,12},{1,13},{2,14},{3,15},{4,0},{5,1},{6,2},{7,3},{8,4},{9,5},{1... | collective-permute-start | bytes 786440 | tf_op jit(solution)/shard_map/ppermute | solution.py:41
  38.7 9.1 %collective-permute-done.3.refs_1_ = bf16[4,128,256]{2,1,0:T(8,128)(2,1)S(1)} collective-permute-done((bf16[4,128,256]{2,1,0:T(8,128)(2,1)S(1)}, bf16[4,128,256]{2,1,0:T(8,128)(2,1)S(1)}, u32[]{:S(2)}, u32[]{:S(2)}) %collective-permute-start.3) | collective-permute-done | bytes 262176 | tf_op jit(solution)/shard_map/ppermute | solution.py:31
  47.8 1.9 %collective-permute-start.5 = (bf16[4,128,256]{2,1,0:T(8,128)(2,1)S(1)}, bf16[4,128,256]{2,1,0:T(8,128)(2,1)S(1)}, u32[]{:S(2)}, u32[]{:S(2)}) collective-permute-start(bf16[4,128,256]{2,1,0:T(8,128)(2,1)S(1)} %collective-permute-done.3.refs_1_), channel_id=1, source_target_pairs={{0,16},{1,17},{2,18},{3,19},{4,20},{5,21},{6,22},{7,23},{8,24},{9,... | collective-permute-start | bytes 786440 | tf_op jit(solution)/shard_map/ppermute | solution.py:31
  49.8 0.1 select_reduce_fusion
  49.9 0.7 fusion
  50.5 1.3 %pad_add_fusion.info = s32[3]{0:T(128)S(1)} fusion(s32[1]{0:T(128)} %get-tuple-element.40, s32[1]{0:T(128)} %get-tuple-element.39, s32[1]{0:T(128)} %bitcast), kind=kLoop, calls=%fused_computation.8 | loop fusion | flops 6 | bytes 24 | tf_op jit(solution)/shard_map/stack | solution.py:200
  51.8 0.0 all-to-all-done.1.q_ref
  51.8 0.1 broadcast_in_dim.13.low_ref
  52.0 2.8 %attend.3 = (f32[4,512,128]{2,1,0:T(8,128)S(1)}, f32[4,512,128]{2,1,0:T(8,128)S(1)}, f32[4,512,128]{2,1,0:T(8,128)S(1)}) custom-call(s32[3]{0:T(128)S(1)} %pad_add_fusion.info, s32[512,128]{1,0:T(8,128)S(1)} %broadcast_in_dim.13.low_ref, bf16[4,128,512]{2,1,0:T(8,128)(2,1)S(1)} %all-to-all-done.1.q_ref, bf16[4,128,256]{2,1,0:T(8,128)(2,1)S(1)} %all_to_all.15.refs_0_, ...), custom_call_target="tpu_custom_call" | custom-call | flops 3428571392 | bytes 4000000 | tf_op jit(solution)/shard_map/attend/pallas_call | solution.py:166
  54.8 3.2 %collective-permute-done.1.refs_0_ = bf16[4,128,256]{2,1,0:T(8,128)(2,1)S(1)} collective-permute-done((bf16[4,128,256]{2,1,0:T(8,128)(2,1)S(1)}, bf16[4,128,256]{2,1,0:T(8,128)(2,1)S(1)}, u32[]{:S(2)}, u32[]{:S(2)}) %collective-permute-start.1) | collective-permute-done | bytes 262176 | tf_op jit(solution)/shard_map/ppermute | solution.py:31
  58.0 1.9 %collective-permute-start.2 = (bf16[4,128,256]{2,1,0:T(8,128)(2,1)S(1)}, bf16[4,128,256]{2,1,0:T(8,128)(2,1)S(1)}, u32[]{:S(2)}, u32[]{:S(2)}) collective-permute-start(bf16[4,128,256]{2,1,0:T(8,128)(2,1)S(1)} %collective-permute-done.1.refs_0_), channel_id=1, source_target_pairs={{0,16},{1,17},{2,18},{3,19},{4,20},{5,21},{6,22},{7,23},{8,24},{9,... | collective-permute-start | bytes 786440 | tf_op jit(solution)/shard_map/ppermute | solution.py:31
  59.9 2.3 %collective-permute-done.5.refs_3_ = bf16[4,128,256]{2,1,0:T(8,128)(2,1)S(1)} collective-permute-done((bf16[4,128,256]{2,1,0:T(8,128)(2,1)S(1)}, bf16[4,128,256]{2,1,0:T(8,128)(2,1)S(1)}, u32[]{:S(2)}, u32[]{:S(2)}) %collective-permute-start.5) | collective-permute-done | bytes 262176 | tf_op jit(solution)/shard_map/ppermute | solution.py:31
  62.2 0.0 collective-permute-done.4.refs_2_
  62.2 2.7 %attend.4 = (f32[4,512,128]{2,1,0:T(8,128)S(1)}, f32[4,512,128]{2,1,0:T(8,128)S(1)}, f32[4,512,128]{2,1,0:T(8,128)S(1)}) custom-call(s32[3]{0:T(128)S(1)} %pad_add_fusion.info, s32[512,128]{1,0:T(8,128)S(1)} %broadcast_in_dim.13.low_ref, bf16[4,128,512]{2,1,0:T(8,128)(2,1)S(1)} %all-to-all-done.1.q_ref, ...), custom_call_target="tpu_custom_call", output_to_operand_aliasing={{0}: (7, {}), {1}: (8, {}), {2}: (9, {})} | custom-call | flops 6857142784 | bytes 4000000 | tf_op jit(solution)/shard_map/attend/pallas_call | solution.py:166
  64.9 5.8 %collective-permute-done.2.refs_0_ = bf16[4,128,256]{2,1,0:T(8,128)(2,1)S(1)} collective-permute-done((bf16[4,128,256]{2,1,0:T(8,128)(2,1)S(1)}, bf16[4,128,256]{2,1,0:T(8,128)(2,1)S(1)}, u32[]{:S(2)}, u32[]{:S(2)}) %collective-permute-start.2) | collective-permute-done | bytes 262176 | tf_op jit(solution)/shard_map/ppermute | solution.py:31
  70.7 0.9 %attend.5 = (f32[4,512,128]{2,1,0:T(8,128)S(1)}, f32[4,512,128]{2,1,0:T(8,128)S(1)}, f32[4,512,128]{2,1,0:T(8,128)S(1)}, bf16[4,128,512]{2,1,0:T(8,128)(2,1)S(1)}) custom-call(s32[3]{0:T(128)S(1)} %pad_add_fusion.info, s32[512,128]{1,0:T(8,128)S(1)} %broadcast_in_dim.13.low_ref, ...), custom_call_target="tpu_custom_call", output_to_operand_aliasing={{0}: (4, {}), {1}: (5, {}), {2}: (6, {})} | custom-call | flops 1714285696 | bytes 4000000 | tf_op jit(solution)/shard_map/attend/pallas_call | solution.py:166
  71.7 11.2 %all_to_all.16 = bf16[4,128,512]{2,1,0:T(8,128)(2,1)S(1)} all-to-all(bf16[4,128,512]{2,1,0:T(8,128)(2,1)S(1)} %get-tuple-element.34), channel_id=1, replica_groups=mesh['docs'=32,'sub'=4,'chip'=2,'core'=2] {'chip','core'}, dimensions={0} | all-to-all | bytes 1048576 | tf_op jit(solution)/shard_map/all_to_all | solution.py:209
  83.0 0.8 %pad_maximum_fusion = bf16[128,2048]{1,0:T(8,128)(2,1)} fusion(bf16[128,512]{1,0:T(8,128)(2,1)S(1)} %get-tuple-element.36, bf16[128,512]{1,0:T(8,128)(2,1)S(1)} %get-tuple-element.37, bf16[128,512]{1,0:T(8,128)(2,1)S(1)} %get-tuple-element.38, bf16[128,512]{1,0:T(8,128)(2,1)S(1)} %get-tuple-element.35), kind=kLoop, calls=%fused_computation | loop fusion | flops 2097152 | bytes 1048576 | tf_op jit(solution)/shard_map/concatenate | solution.py:210
  (3 shorter events, 0.1 us)
Async XLA Ops:
  11.9 21.9 %collective-permute-start = (bf16[4,128,256]{2,1,0:T(8,128)(2,1)S(1)}, bf16[4,128,256]{2,1,0:T(8,128)(2,1)S(1)}, u32[]{:S(2)}, u32[]{:S(2)}) collective-permute-start(bf16[4,128,256]{2,1,0:T(8,128)(2,1)S(1)} %all_to_all.15.refs_0_), channel_id=1, source_target_pairs={{0,16},{1,17},{2,18},{3,19},{4,20},{5,21},{6,22},{7,23},{8,24},{9,... | collective-permute-start | bytes 786440 | tf_op jit(solution)/shard_map/ppermute | solution.py:31
  15.3 36.5 %all-to-all-start.1 = ((bf16[4,128,512]{2,1,0:T(8,128)(2,1)}), bf16[4,128,512]{2,1,0:T(8,128)(2,1)S(1)}, u32[]{:S(2)}, u32[]{:S(2)}) async-start(bf16[4,128,512]{2,1,0:T(8,128)(2,1)} %get-tuple-element.22), calls=%async_computation.1 | async-start | bytes 1048576 | tf_op jit(solution)/shard_map/all_to_all | solution.py:189
  18.8 29.0 %collective-permute-start.3 = (bf16[4,128,256]{2,1,0:T(8,128)(2,1)S(1)}, bf16[4,128,256]{2,1,0:T(8,128)(2,1)S(1)}, u32[]{:S(2)}, u32[]{:S(2)}) collective-permute-start(bf16[4,128,256]{2,1,0:T(8,128)(2,1)S(1)} %all_to_all.15.refs_0_), channel_id=1, source_target_pairs={{0,8},{1,9},{2,10},{3,11},{4,12},{5,13},{6,14},{7,15},{8,16},{9,17... | collective-permute-start | bytes 786440 | tf_op jit(solution)/shard_map/ppermute | solution.py:31
  29.5 4.3 %copy-start = (s32[32]{0:T(128)S(1)}, s32[32]{0:T(128)}, u32[]{:S(2)}) copy-start(s32[32]{0:T(128)} %param.7) | copy-start | bytes 388
  29.5 28.5 %collective-permute-start.1 = (bf16[4,128,256]{2,1,0:T(8,128)(2,1)S(1)}, bf16[4,128,256]{2,1,0:T(8,128)(2,1)S(1)}, u32[]{:S(2)}, u32[]{:S(2)}) collective-permute-start(bf16[4,128,256]{2,1,0:T(8,128)(2,1)S(1)} %all_to_all.15.refs_0_), channel_id=1, source_target_pairs={{0,4},{1,5},{2,6},{3,7},{4,8},{5,9},{6,10},{7,11},{8,12},{9,13},{1... | collective-permute-start | bytes 786440 | tf_op jit(solution)/shard_map/ppermute | solution.py:31
  34.1 28.1 %collective-permute-start.4 = (bf16[4,128,256]{2,1,0:T(8,128)(2,1)S(1)}, bf16[4,128,256]{2,1,0:T(8,128)(2,1)S(1)}, u32[]{:S(2)}, u32[]{:S(2)}) collective-permute-start(bf16[4,128,256]{2,1,0:T(8,128)(2,1)S(1)} %broadcast_select_fusion), channel_id=1, source_target_pairs={{0,12},{1,13},{2,14},{3,15},{4,0},{5,1},{6,2},{7,3},{8,4},{9,5},{1... | collective-permute-start | bytes 786440 | tf_op jit(solution)/shard_map/ppermute | solution.py:41
  47.8 14.4 %collective-permute-start.5 = (bf16[4,128,256]{2,1,0:T(8,128)(2,1)S(1)}, bf16[4,128,256]{2,1,0:T(8,128)(2,1)S(1)}, u32[]{:S(2)}, u32[]{:S(2)}) collective-permute-start(bf16[4,128,256]{2,1,0:T(8,128)(2,1)S(1)} %collective-permute-done.3.refs_1_), channel_id=1, source_target_pairs={{0,16},{1,17},{2,18},{3,19},{4,20},{5,21},{6,22},{7,23},{8,24},{9,... | collective-permute-start | bytes 786440 | tf_op jit(solution)/shard_map/ppermute | solution.py:31
  58.0 12.7 %collective-permute-start.2 = (bf16[4,128,256]{2,1,0:T(8,128)(2,1)S(1)}, bf16[4,128,256]{2,1,0:T(8,128)(2,1)S(1)}, u32[]{:S(2)}, u32[]{:S(2)}) collective-permute-start(bf16[4,128,256]{2,1,0:T(8,128)(2,1)S(1)} %collective-permute-done.1.refs_0_), channel_id=1, source_target_pairs={{0,16},{1,17},{2,18},{3,19},{4,20},{5,21},{6,22},{7,23},{8,24},{9,... | collective-permute-start | bytes 786440 | tf_op jit(solution)/shard_map/ppermute | solution.py:31
